TPU v7x, 32 devices: a whole 2x2x4 slice. The times are simulated.
32 devices in a mesh: grp: 2 (over y), row: 4 (over x, core), col: 4 (over z).
Axes of the slice: x: 2, y: 2, z: 4, core: 2. Of those that a mesh axis runs over, the one named last changes fastest.
Arguments:
- alignment: bfloat16 [192, 256, 256], P('grp', 'row'), parts along dimension 0, may hold values from -6 to 6
- coverage: int32 [192, 256], P('grp', 'row'), parts along dimension 0, may hold values from 0 to 1, as said below
- layer_norm_gain: float32 [256], replicated, may hold values from 0.25 to 1.75
- layer_norm_bias: float32 [256], replicated, may hold values from -3 to 3
- left_weight: bfloat16 [256, 32], replicated, may hold values from -0.375 to 0.375
- right_weight: bfloat16 [256, 32], replicated, may hold values from -0.375 to 0.375
- out_weight: bfloat16 [1024, 128], replicated, may hold values from -1.5 to 1.5
- out_bias: float32 [128], replicated, may hold values from -3 to 3
- cotangent: bfloat16 [512, 256, 128], P(('grp', 'row'), 'col'), parts along dimension 0, may hold values from -6 to 6
Outputs:
- pair_update: bfloat16 [512, 256, 128], P(('grp', 'row'), 'col'), parts along dimension 0
- sequence_alignment_gradient: bfloat16 [192, 256, 256], P('grp', 'row'), parts along dimension 0
- grad_left: float32 [512, 32], P('grp'), parts along dimension 0
- grad_right: float32 [512, 32], P('grp'), parts along dimension 0
- grad_out: float32 [2048, 128], P('grp'), parts along dimension 0
There are 2 independent parts, one for each index of `grp`. A program takes and returns all parts, laid end to end along the dimension named above; an argument that names none is the same for every part. Nothing has to cross between parts.
Inputs may be any that keep to these rules, and one draw needn't show every extreme that they name: `coverage`: for each residue the mask is 1 on a leading run of MSA rows (possibly empty) and 0 after it.
All inputs are finite; a program needn't handle non-finite values.
Results may differ from a plain program's by a relative error of at most 0.0073.
Values may be sent and summed in bfloat16 or wider, within the bound.
No kernel may reach another device: no remote copies, remote signals or barrier semaphores. Data moves between devices by JAX's collectives and lax.ppermute only.
A program may use at most 128 MiB of HBM per device.

v0:
```python
import jax
import jax.numpy as jnp
from jax import lax
from jax.sharding import PartitionSpec as P


def from_root(value, axis, root):
    mine = lax.axis_index(axis) == root
    return lax.psum(jnp.where(mine, value, jnp.zeros_like(value)), axis)


def body(
    alignment,
    coverage,
    layer_norm_gain,
    layer_norm_bias,
    left_weight,
    right_weight,
    out_weight,
    out_bias,
    cotangent,
):
    ratio = lax.axis_size("row") // lax.axis_size("col")
    row_index = lax.axis_index("row")
    col_index = lax.axis_index("col")
    own_rows = alignment.shape[1]
    col_rows = cotangent.shape[1]
    narrow = left_weight.shape[1]
    maskf = coverage.astype(jnp.float32)
    values = alignment.astype(jnp.float32)
    centered_values = values - jnp.mean(values, axis=-1, keepdims=True)
    inverse_deviation = lax.rsqrt(
        jnp.mean(centered_values * centered_values, axis=-1, keepdims=True) + 1e-05
    )
    standardized_input = centered_values * inverse_deviation
    normalized_input = (standardized_input * layer_norm_gain + layer_norm_bias).astype(jnp.bfloat16)
    left = (
        jnp.einsum("src,cd->srd", normalized_input, left_weight, preferred_element_type=jnp.float32)
        * maskf[..., None]
    ).astype(jnp.bfloat16)
    right = (
        jnp.einsum(
            "src,cd->srd", normalized_input, right_weight, preferred_element_type=jnp.float32
        )
        * maskf[..., None]
    ).astype(jnp.bfloat16)
    mask_half = maskf.astype(jnp.bfloat16)
    right_all, mask_all = (
        lax.all_gather(right, "row", axis=1, tiled=True),
        lax.all_gather(mask_half, "row", axis=1, tiled=True),
    )
    begin = col_index * col_rows
    right_cols = lax.dynamic_slice_in_dim(right_all, begin, col_rows, 1)
    mask_cols = lax.dynamic_slice_in_dim(mask_all, begin, col_rows, 1)
    mask_cols_f = mask_cols.astype(jnp.float32)
    counts = jnp.einsum("si,sj->ij", maskf, mask_cols_f)
    denom = jnp.maximum(counts, 1.0)
    outer = jnp.einsum(
        "sic,sjd->ijcd", left, right_cols, preferred_element_type=jnp.float32
    ).astype(jnp.bfloat16)
    outer = outer.reshape(own_rows, col_rows, narrow * narrow)
    proj = jnp.einsum("ijf,fh->ijh", outer, out_weight, preferred_element_type=jnp.float32)
    pair_update = ((proj + out_bias) / denom[..., None]).astype(jnp.bfloat16)
    scaled = (cotangent.astype(jnp.float32) / denom[..., None]).astype(jnp.bfloat16)
    out_part = jnp.einsum("ijf,ijh->fh", outer, scaled, preferred_element_type=jnp.float32)
    grad_outer = jnp.einsum(
        "ijh,fh->ijf", scaled, out_weight, preferred_element_type=jnp.float32
    ).astype(jnp.bfloat16)
    grad_outer = grad_outer.reshape(own_rows, col_rows, narrow, narrow)
    left_part = jnp.einsum(
        "ijcd,sjd->sic", grad_outer, right_cols, preferred_element_type=jnp.float32
    )
    right_part = jnp.einsum("ijcd,sic->sjd", grad_outer, left, preferred_element_type=jnp.float32)
    left_total = lax.psum(left_part, "col")
    grad_left_side = (left_total * maskf[..., None]).astype(jnp.bfloat16)
    right_total = lax.psum(right_part, "row")
    mine = lax.dynamic_slice_in_dim(right_total, row_index % ratio * own_rows, own_rows, 1)
    mine = (mine * maskf[..., None]).astype(jnp.bfloat16)
    grad_right_side = from_root(mine, "col", row_index // ratio)
    left_grad_part = jnp.einsum(
        "src,srd->cd", normalized_input, grad_left_side, preferred_element_type=jnp.float32
    )
    right_grad_part = jnp.einsum(
        "src,srd->cd", normalized_input, grad_right_side, preferred_element_type=jnp.float32
    )
    grad_left, grad_right = lax.psum((left_grad_part, right_grad_part), "row")
    grad_out = lax.psum(out_part, ("row", "col"))
    grad_normed = jnp.einsum(
        "srd,cd->src", grad_left_side, left_weight, preferred_element_type=jnp.float32
    )
    grad_normed = grad_normed + jnp.einsum(
        "srd,cd->src", grad_right_side, right_weight, preferred_element_type=jnp.float32
    )
    gain_scaled_gradient = grad_normed * layer_norm_gain
    sequence_alignment_gradient = inverse_deviation * (
        gain_scaled_gradient
        - jnp.mean(gain_scaled_gradient, axis=-1, keepdims=True)
        - standardized_input
        * jnp.mean(gain_scaled_gradient * standardized_input, axis=-1, keepdims=True)
    )
    return (
        pair_update,
        sequence_alignment_gradient.astype(jnp.bfloat16),
        grad_left,
        grad_right,
        grad_out,
    )


def solution(mesh):
    return jax.shard_map(
        body,
        mesh=mesh,
        in_specs=(
            P("grp", "row", None),
            P("grp", "row"),
            P(),
            P(),
            P(),
            P(),
            P(),
            P(),
            P(("grp", "row"), "col", None),
        ),
        out_specs=(
            P(("grp", "row"), "col", None),
            P("grp", "row", None),
            P("grp", None),
            P("grp", None),
            P("grp", None),
        ),
        check_vma=False,
    )
```

profile of v0, /device:TPU:0, one launch (start us, length us, event | category | flops | bytes accessed | tf_op | source)
XLA Modules:
  0.0 427.9 jit_solution(15792319067597309660)
XLA Ops:
  14.9 8.1 %all_gather.7 = bf16[96,256]{0,1:T(8,128)(2,1)} all-gather(bf16[96,64]{0,1:T(8,128)(2,1)} %get-tuple-element.9), channel_id=1, replica_groups=mesh['grp'=2,'row'=4,'col'=4] {'row'}, dimensions={1}, use_global_device_ids=true | all-gather | bytes 61440 | tf_op jit(solution)/shard_map/all_gather | solution.py:50
  26.0 4.7 %multiply_convert_fusion.2 = bf16[96,64,32]{1,2,0:T(8,128)(2,1)} fusion(f32[96,64]{1,0:T(8,128)S(1)} %copy.46, bf16[256,32]{0,1:T(8,128)(2,1)} %param.13, bf16[96,64,256]{2,1,0:T(8,128)(2,1)S(1)} %copy-done.1, f32[256]{0:T(256)} %param.12, f32[256]{0:T(256)} %param.11, f32[96,64]{1,0:T(8,128)S(1)} %add_rsqrt_fusion, f32[96,64]{1,0:T(8,128)S(1)} %broadcast_multiply_fusion.2), kind=kOutput, calls=%fused_computation.23 | convolution fusion | flops 110493696 | bytes 3631104 | tf_op jit(solution)/shard_map/src,cd->srd/dot_general | solution.py:38
  33.4 6.8 %convolution_convert_fusion = bf16[64,64,1024]{2,1,0:T(8,128)(2,1)} fusion(bf16[1024,128]{1,0:T(8,128)(2,1)S(1)} %copy-done, bf16[64,64,128]{2,1,0:T(8,128)(2,1)} %param.17, f32[64,64]{1,0:T(8,128)} %copy.52), kind=kOutput, calls=%fused_computation.10 | convolution fusion | flops 1079508992 | bytes 9715712 | tf_op jit(solution)/shard_map/ijh,fh->ijf/dot_general | solution.py:66
  40.3 15.7 %copy.53 = bf16[64,64,1024]{1,2,0:T(8,128)(2,1)} copy(bf16[64,64,1024]{2,1,0:T(8,128)(2,1)} %convolution_convert_fusion) | data formatting | bytes 16777216 | tf_op jit(solution)/shard_map/convert_element_type | solution.py:68
  56.0 17.8 %fusion.14 = f32[96,64,32]{0,1,2:T(8,128)} fusion(bf16[64,64,32,32]{1,3,2,0:T(8,128)(2,1)} %bitcast.55, bf16[96,64,32]{0,1,2:T(8,128)(2,1)} %copy.49), kind=kOutput, calls=%fused_computation.26 | convolution fusion | flops 805306368 | bytes 9568256 | tf_op jit(solution)/shard_map/ijcd,sic->sjd/dot_general | solution.py:73
  73.8 3.7 copy.58
  77.6 43.5 %all-reduce.9.cloned.1.call-done = f32[96,64,32]{1,2,0:T(8,128)} async-done(((f32[96,64,32]{1,2,0:T(8,128)}), f32[96,64,32]{1,2,0:T(8,128)}) %all-reduce.9.cloned.1.call-update) | async-done | bytes 786448 | tf_op jit(solution)/shard_map/psum | solution.py:76
  123.6 4.7 %multiply_convert_fusion.3 = bf16[96,64,32]{1,2,0:T(8,128)(2,1)} fusion(f32[96,64]{1,0:T(8,128)S(1)} %copy.46, bf16[256,32]{0,1:T(8,128)(2,1)} %param.14, bf16[96,64,256]{2,1,0:T(8,128)(2,1)S(1)} %copy-done.1, f32[256]{0:T(256)} %param.12, f32[256]{0:T(256)} %param.11, f32[96,64]{1,0:T(8,128)S(1)} %add_rsqrt_fusion, f32[96,64]{1,0:T(8,128)S(1)} %broadcast_multiply_fusion.2), kind=kOutput, calls=%fused_computation.24 | convolution fusion | flops 110493696 | bytes 3631104 | tf_op jit(solution)/shard_map/src,cd->srd/dot_general | solution.py:42
  128.4 3.3 copy.47
  131.7 24.0 %copy.65 = bf16[64,64,1024]{1,0,2:T(8,128)(2,1)} copy(bf16[64,64,1024]{2,1,0:T(8,128)(2,1)} %convolution_convert_fusion) | data formatting | bytes 16777216 | tf_op jit(solution)/shard_map/reshape | solution.py:69
  155.7 12.1 %all-reduce.11.cloned.1.call-done = bf16[96,64,32]{1,2,0:T(8,128)(2,1)} async-done(((bf16[96,64,32]{1,2,0:T(8,128)(2,1)}), bf16[96,64,32]{1,2,0:T(8,128)(2,1)}) %all-reduce.11.cloned.1.call-update) | async-done | bytes 393232 | tf_op jit(solution)/shard_map/psum | solution.py:9
  167.8 5.3 %convolution_bitcast_fusion.2 = f32[256,32]{0,1:T(8,128)} fusion(bf16[96,64,32]{1,2,0:T(8,128)(2,1)} %all-reduce.11.cloned.1.call-done, bf16[96,64,256]{2,1,0:T(8,128)(2,1)S(1)} %copy-done.1, f32[256]{0:T(256)} %param.12, f32[256]{0:T(256)} %param.11, f32[96,64]{1,0:T(8,128)S(1)} %add_rsqrt_fusion, f32[96,64]{1,0:T(8,128)S(1)} %broadcast_multiply_fusion.2), kind=kOutput, calls=%fused_computation.28 | convolution fusion | flops 110100480 | bytes 3622912 | tf_op jit(solution)/shard_map/src,srd->cd/dot_general | solution.py:83
  173.0 18.2 %all-gather.2.cloned.1.call-done = bf16[96,256,32]{0,2,1:T(8,128)(2,1)} async-done(((bf16[96,64,32]{0,2,1:T(8,128)(2,1)}), bf16[96,256,32]{0,2,1:T(8,128)(2,1)}) %all-gather.2.cloned.1.call-update) | async-done | bytes 1572880 | tf_op jit(solution)/shard_map/all_gather | solution.py:49
  193.2 11.4 %convert_bitcast_fusion = bf16[64,64,32,32]{0,1,2,3:T(8,128)(2,1)} fusion(bf16[96,64,32]{0,1,2:T(8,128)(2,1)} %copy.49, bf16[96,64,32]{0,2,1:T(8,128)(2,1)} %constant_dynamic-slice_fusion), kind=kOutput, calls=%fused_computation.2 | convolution fusion | flops 809500672 | bytes 9175040 | tf_op jit(solution)/shard_map/sic,sjd->ijcd/dot_general | solution.py:58
  204.6 11.3 %convolution_bitcast_fusion = f32[96,64,32]{0,1,2:T(8,128)} fusion(bf16[64,64,32,32]{1,0,3,2:T(8,128)(2,1)} %bitcast.54, bf16[96,64,32]{0,2,1:T(8,128)(2,1)} %constant_dynamic-slice_fusion), kind=kOutput, calls=%fused_computation.25 | convolution fusion | flops 805306368 | bytes 9568256 | tf_op jit(solution)/shard_map/ijcd,sjd->sic/dot_general | solution.py:70
  215.9 3.5 copy.55
  219.5 24.2 %copy.50 = bf16[64,64,32,32]{1,3,2,0:T(8,128)(2,1)} copy(bf16[64,64,32,32]{0,1,2,3:T(8,128)(2,1)} %convert_bitcast_fusion) | data formatting | bytes 16777216 | tf_op jit(solution)/shard_map/convert_element_type | solution.py:60
  243.7 10.4 %convolution_bitcast_fusion.1 = f32[1024,128]{1,0:T(8,128)} fusion(bf16[64,64,1024]{1,2,0:T(8,128)(2,1)} %bitcast.56, bf16[64,64,128]{2,1,0:T(8,128)(2,1)} %param.17, f32[64,64]{1,0:T(8,128)} %copy.52), kind=kOutput, calls=%fused_computation.27 | convolution fusion | flops 1075314688 | bytes 9977856 | tf_op jit(solution)/shard_map/ijf,ijh->fh/dot_general | solution.py:65
  254.0 11.9 %divide_convert_fusion.1 = bf16[64,64,128]{2,1,0:T(8,128)(2,1)} fusion(bf16[64,64,1024]{1,2,0:T(8,128)(2,1)} %bitcast.57, f32[64,64]{1,0:T(8,128)} %copy.52, f32[128]{0:T(128)} %param.16, bf16[1024,128]{1,0:T(8,128)(2,1)S(1)} %copy-done), kind=kOutput, calls=%fused_computation.20 | convolution fusion | flops 1075314688 | bytes 9716224 | tf_op jit(solution)/shard_map/ijf,fh->ijh/dot_general | solution.py:62
  266.0 22.8 %all-reduce.7.cloned.1.call-done = f32[96,64,32]{1,2,0:T(8,128)} async-done(((f32[96,64,32]{1,2,0:T(8,128)}), f32[96,64,32]{1,2,0:T(8,128)}) %all-reduce.7.cloned.1.call-update) | async-done | bytes 786448 | tf_op jit(solution)/shard_map/psum | solution.py:74
  291.3 6.4 %fusion.39 = (f32[96,64]{1,0:T(8,128)}, f32[96,64]{1,0:T(8,128)}, f32[96,64,256]{2,1,0:T(8,128)}) fusion(f32[96,64]{1,0:T(8,128)S(1)} %add_rsqrt_fusion, f32[96,64]{1,0:T(8,128)S(1)} %broadcast_multiply_fusion.2, bf16[96,64,256]{2,1,0:T(8,128)(2,1)S(1)} %copy-done.1, f32[256]{0:T(256)S(1)} %copy-done.6, f32[96,64,256]{2,1,0:T(8,128)S(1)} %fusion.25, ...), kind=kOutput, calls=%fused_computation.55 | convolution fusion | flops 113233920 | bytes 16237568 | tf_op jit(solution)/shard_map/srd,cd->src/dot_general | solution.py:91
  301.8 8.5 %fusion.12 = bf16[96,64,256]{2,1,0:T(8,128)(2,1)} fusion(bf16[96,64,256]{2,1,0:T(8,128)(2,1)S(1)} %copy-done.1, f32[96,64,256]{2,1,0:T(8,128)} %get-tuple-element.11, f32[96,64]{1,0:T(8,128)S(1)} %get-tuple-element.12, f32[96,64]{1,0:T(8,128)} %get-tuple-element.13, f32[96,64]{1,0:T(8,128)S(1)} %add_rsqrt_fusion, f32[96,64]{1,0:T(8,128)S(1)} %broadcast_multiply_fusion.2), kind=kLoop, calls=%fused_computation.16 | loop fusion | flops 12582912 | bytes 12681216 | tf_op jit(solution)/shard_map/convert_element_type | solution.py:103
  310.3 71.5 %all-reduce.13.cloned.1.call-done = f32[1024,128]{1,0:T(8,128)} async-done(((f32[1024,128]{1,0:T(8,128)}), f32[1024,128]{1,0:T(8,128)}) %all-reduce.13.cloned.1.call-update) | async-done | bytes 524304 | tf_op jit(solution)/shard_map/psum | solution.py:87
  381.8 34.5 %all-reduce.15.cloned.1.call-done = (f32[256,32]{0,1:T(8,128)}, f32[256,32]{0,1:T(8,128)}) async-done(((f32[256,32]{0,1:T(8,128)}, f32[256,32]{0,1:T(8,128)}), (f32[256,32]{0,1:T(8,128)}, f32[256,32]{0,1:T(8,128)})) %all-reduce.15.cloned.1.call-update) | async-done | bytes 65552 | tf_op jit(solution)/shard_map/psum | solution.py:86
  (45 shorter events, 29.2 us)
Async XLA Ops:
  7.2 26.3 %copy-start = (bf16[1024,128]{1,0:T(8,128)(2,1)S(1)}, bf16[1024,128]{1,0:T(8,128)(2,1)}, u32[]{:S(2)}) copy-start(bf16[1024,128]{1,0:T(8,128)(2,1)} %param.15) | copy-start | bytes 786436
  7.2 18.9 %copy-start.1 = (bf16[96,64,256]{2,1,0:T(8,128)(2,1)S(1)}, bf16[96,64,256]{2,1,0:T(8,128)(2,1)}, u32[]{:S(2)}) copy-start(bf16[96,64,256]{2,1,0:T(8,128)(2,1)} %param.9) | copy-start | bytes 9437188
  7.2 6.3 %copy-start.4 = (s32[96,64]{0,1:T(8,128)S(1)}, s32[96,64]{0,1:T(8,128)}, u32[]{:S(2)}) copy-start(s32[96,64]{0,1:T(8,128)} %param.10) | copy-start | bytes 73732
  7.2 113.8 %all-reduce.9.cloned.1.call-start = ((), (), s32[]{:S(2)}) async-start(), calls=%async_computation.2 | async-start | bytes 3145728 | tf_op jit(solution)/shard_map/psum | solution.py:76
  77.5 90.2 %all-reduce.11.cloned.1.call-start = ((), (), s32[]{:S(2)}) async-start(), calls=%async_computation.3 | async-start | bytes 1572864 | tf_op jit(solution)/shard_map/psum | solution.py:9
  123.6 67.7 %all-gather.2.cloned.1.call-start = ((), (), s32[]{:S(2)}) async-start(), calls=%async_computation | async-start | bytes 2621440 | tf_op jit(solution)/shard_map/all_gather | solution.py:49
  131.7 157.1 %all-reduce.7.cloned.1.call-start = ((), (), s32[]{:S(2)}) async-start(), calls=%async_computation.1 | async-start | bytes 3145728 | tf_op jit(solution)/shard_map/psum | solution.py:74
  219.4 162.4 %all-reduce.13.cloned.1.call-start = ((), (), s32[]{:S(2)}) async-start(), calls=%async_computation.4 | async-start | bytes 1048576 | tf_op jit(solution)/shard_map/psum | solution.py:87
  265.9 150.4 %all-reduce.15.cloned.1.call-start = ((), (), s32[]{:S(2)}) async-start(), calls=%async_computation.5 | async-start | bytes 131072 | tf_op jit(solution)/shard_map/psum | solution.py:86
  288.7 2.5 copy-start.3
  288.7 2.5 copy-start.5
  288.7 2.5 copy-start.6
  291.3 6.5 %copy-start.2 = (f32[96,64,32]{1,2,0:T(8,128)S(1)}, f32[96,64,32]{1,2,0:T(8,128)}, u32[]{:S(2)}) copy-start(f32[96,64,32]{1,2,0:T(8,128)} %all-reduce.7.cloned.1.call-done) | copy-start | bytes 2359300
  291.3 6.5 %copy-start.7 = (f32[256]{0:T(256)S(1)}, f32[256]{0:T(256)}, u32[]{:S(2)}) copy-start(f32[256]{0:T(256)} %param.12) | copy-start | bytes 3076
Sparse Core Ops, SparseCore 0:
  77.7 43.3 all-reduce.8
  124.0 43.7 all-reduce.10
  169.3 21.9 all-gather.1
  219.6 69.1 all-reduce.6
  292.6 89.1 all-reduce.12
  384.6 31.6 all-reduce.14
where the time goes:
time: 435 us; the launch traced here: 428 us
  waiting for transfers between devices  203 us (47%)
  matrix products  97.4 us (22%)
  local copies, waits for them, and re-layouts  85.8 us (20%)
  other arithmetic  19.3 us (4%)
  between operations  14.4 us (3%)
  blocking collectives  8.12 us (2%)
    psum x1, waiting for transfers between devices, body(): grad_out = lax.psum(out_part, ('row', 'col'))  71.5 us
    psum x1, waiting for transfers between devices, body(): right_total = lax.psum(right_part, 'row')  43.5 us
    psum x1, waiting for transfers between devices, body(): grad_left, grad_right = lax.psum((left_grad_part, right_grad_part), 'row')  34.5 us
    convert_element_type x1, local copies, waits for them, and re-layouts, body(): outer = jnp.einsum('sic,sjd->ijcd', left, right_cols, preferred_element_t...  24.2 us
    reshape x1, local copies, waits for them, and re-layouts, body(): grad_outer = grad_outer.reshape(own_rows, col_rows, narrow, narrow)  24 us
    psum x1, waiting for transfers between devices, body(): left_total = lax.psum(left_part, 'col')  22.8 us
    all_gather x1, waiting for transfers between devices, body(): lax.all_gather(right, 'row', axis=1, tiled=True)  18.2 us
    dot_general x1, matrix products, body(): jnp.einsum('ijcd,sic->sjd', grad_outer, left, preferred_element_type=jnp....  17.8 us
  transfers between devices with their start and end apart: 6, of which 6 were waited for; matrix products, arithmetic and copies ran while one was open for 25% of the time, Pallas kernels for 0%

commit v1 on v0

v1 whole, which is shorter than its diff:
```python
import functools

import jax
import jax.numpy as jnp
from jax import lax
from jax.experimental import pallas as pl
from jax.experimental.pallas import tpu as pltpu
from jax.sharding import PartitionSpec as P

BF = jnp.bfloat16
F32 = jnp.float32
VMEM_LIMIT = 50 * 1024 * 1024
NT = (((1,), (1,)), ((), ()))
TN = (((0,), (0,)), ((), ()))


def params():
    return pltpu.CompilerParams(vmem_limit_bytes=VMEM_LIMIT)


def dot(a, b, dims=(((1,), (0,)), ((), ()))):
    return lax.dot_general(a, b, dims, preferred_element_type=F32)


def whole(shape):
    return pl.BlockSpec(shape, lambda *_: (0,) * len(shape))


def project_kernel(
    depth_ref, x_ref, depth_row, gain, bias, wl, wrt, normed_ref, r_ref, l_ref, lt_ref, ys, zl
):
    n = pl.program_id(0)
    steps = pl.num_programs(0)
    _, g_blk, rows, chans = x_ref.shape
    narrow = wrt.shape[0]
    half = g_blk * steps
    gain_v = gain[...]
    bias_v = bias[...]
    for g in range(g_blk):
        both = []
        for s2 in range(2):
            x = x_ref[s2, g].astype(F32)
            c = x - jnp.mean(x, axis=-1, keepdims=True)
            inv = lax.rsqrt(jnp.mean(c * c, axis=-1, keepdims=True) + 1e-05)
            nb = (c * inv * gain_v + bias_v).astype(BF)
            normed_ref[s2, g] = nb
            both.append(nb)
        pair = jnp.concatenate(both, axis=0)
        at = n * g_blk + g
        ys[pl.ds(pl.multiple_of(at * narrow, narrow), narrow), :] = dot(wrt[...], pair, NT)
        z = dot(pair, wl[...])
        zl[pl.ds(pl.multiple_of(at * rows, rows), rows), :] = z[:rows]
        zl[pl.ds(pl.multiple_of((half + at) * rows, rows), rows), :] = z[rows:]

    @pl.when(n == steps - 1)
    def _():
        lane = lax.broadcasted_iota(jnp.int32, (half, 2 * rows), 1)
        row = lax.broadcasted_iota(jnp.int32, (half, 2 * rows), 0).astype(F32)
        low = lane < rows
        dep = depth_row[...]
        top_on = row < dep
        bot_on = row + half < dep
        for dp in range(narrow // 2):
            even = ys[pl.ds(2 * dp, half, stride=narrow), :]
            odd = ys[pl.ds(2 * dp + 1, half, stride=narrow), :]
            top = jnp.where(low, even, pltpu.roll(odd, rows, 1))
            bot = jnp.where(low, pltpu.roll(even, rows, 1), odd)
            at = slice(dp * 2 * rows, (dp + 1) * 2 * rows)
            r_ref[0:half, at] = jnp.where(top_on, top, 0.0).astype(BF)
            r_ref[half : 2 * half, at] = jnp.where(bot_on, bot, 0.0).astype(BF)
        seq = lax.broadcasted_iota(jnp.int32, (2 * half, narrow), 0)
        per = 128 // narrow
        for q in range(rows // per):
            parts = []
            for k in range(per):
                i = q * per + k
                v = zl[pl.ds(i, 2 * half, stride=rows), :]
                parts.append(jnp.where(seq < depth_ref[i], v, 0.0))
            tile = jnp.concatenate(parts, axis=1)
            l_ref[:, q * 128 : (q + 1) * 128] = tile.astype(BF)
            lt_ref[q * 128 : (q + 1) * 128, :] = tile.T.astype(BF)


def project(depth, alignment, gain, bias, wl, wr):
    seqs, rows, chans = alignment.shape
    narrow = wl.shape[1]
    half = seqs // 2
    g_blk = 8
    steps = half // g_blk
    wide = rows * narrow
    depth_row = jnp.tile(depth.astype(F32), 2)[None, :]
    blk = pl.BlockSpec((2, g_blk, rows, chans), lambda n, *_: (0, n, 0, 0))
    outs = (
        jax.ShapeDtypeStruct((2, half, rows, chans), BF),
        jax.ShapeDtypeStruct((seqs, wide), BF),
        jax.ShapeDtypeStruct((seqs, wide), BF),
        jax.ShapeDtypeStruct((wide, seqs), BF),
    )
    return pl.pallas_call(
        project_kernel,
        name="project",
        grid_spec=pltpu.PrefetchScalarGridSpec(
            num_scalar_prefetch=1,
            grid=(steps,),
            in_specs=[
                blk,
                whole((1, 2 * rows)),
                whole((1, chans)),
                whole((1, chans)),
                whole((chans, narrow)),
                whole((narrow, chans)),
            ],
            out_specs=[blk, whole((seqs, wide)), whole((seqs, wide)), whole((wide, seqs))],
            scratch_shapes=[
                pltpu.VMEM((half * narrow, 2 * rows), F32),
                pltpu.VMEM((seqs * rows, narrow), F32),
            ],
        ),
        out_shape=outs,
        compiler_params=params(),
        cost_estimate=pl.CostEstimate(
            flops=4 * seqs * rows * chans * narrow, bytes_accessed=8_000_000, transcendentals=0
        ),
    )(
        depth,
        alignment.reshape(2, half, rows, chans),
        depth_row,
        gain[None, :],
        bias[None, :],
        wl,
        wr.T,
    )


def pair_block(a, b):
    z = jnp.zeros_like(a)
    return jnp.concatenate(
        [
            jnp.concatenate([a, z], axis=1),
            jnp.concatenate([z, a], axis=1),
            jnp.concatenate([b, z], axis=1),
            jnp.concatenate([z, b], axis=1),
        ],
        axis=0,
    )


def send_pieces(me, acc, outs):
    rows = outs[0].shape[0]
    count = len(outs)
    for t, out in enumerate(outs):
        p = lax.rem(me + t, count)
        out[...] = acc[pl.ds(pl.multiple_of(p * rows, 8), rows), :].astype(out.dtype)


def right_kernel(depth_ref, me_ref, cot_ref, dcol, w2, l_ref, s_ref, g_ref, *rest):
    outs, acc = rest[:-1], rest[-1]
    n = pl.program_id(0)
    i_blk, cols, pair = cot_ref.shape
    narrow = l_ref.shape[1] // i_blk
    seqs = l_ref.shape[0]
    dep = dcol[...]
    w = w2[...]
    for ip in range(i_blk // 2):
        scaled = []
        for k in range(2):
            i = 2 * ip + k
            den = jnp.maximum(jnp.minimum(dep, depth_ref[n * i_blk + i].astype(F32)), 1.0)
            s = (cot_ref[i].astype(F32) / den).astype(BF)
            s_ref[i] = s
            scaled.append(s)
        g = dot(w, pair_block(*scaled), NT).astype(BF)
        for k in range(2):
            i = 2 * ip + k
            for dp in range(narrow // 2):
                g_ref[i * narrow : (i + 1) * narrow, dp * 2 * cols : (dp + 1) * 2 * cols] = g[
                    dp * narrow : (dp + 1) * narrow, k * 2 * cols : (k + 1) * 2 * cols
                ]
    part = dot(l_ref[...], g_ref[...])

    @pl.when(n == 0)
    def _():
        acc[...] = jnp.zeros_like(acc)

    acc[0:seqs, :] += part

    @pl.when(n == pl.num_programs(0) - 1)
    def _():
        send_pieces(me_ref[0], acc, outs)


def right_side(depth, me, cot, dcol, w2, left, block, pieces, piece_rows):
    rows, _, pair = cot.shape
    cols = dcol.shape[0]
    seqs, wide = left.shape
    narrow = wide // rows
    i_blk = 8
    c_wide = cols * narrow
    return pl.pallas_call(
        right_kernel,
        name="grad_outer_right",
        grid_spec=pltpu.PrefetchScalarGridSpec(
            num_scalar_prefetch=2,
            grid=(rows // i_blk,),
            in_specs=[
                pl.BlockSpec((i_blk, cols, pair), lambda n, *_: (n, block, 0)),
                whole(dcol.shape),
                whole(w2.shape),
                pl.BlockSpec((seqs, i_blk * narrow), lambda n, *_: (0, n)),
            ],
            out_specs=[
                pl.BlockSpec((i_blk, cols, pair), lambda n, *_: (n, 0, 0)),
                pl.BlockSpec((i_blk * narrow, c_wide), lambda n, *_: (n, 0)),
            ]
            + [whole((piece_rows, c_wide))] * pieces,
            scratch_shapes=[pltpu.VMEM((piece_rows * pieces, c_wide), F32)],
        ),
        out_shape=[
            jax.ShapeDtypeStruct((rows, cols, pair), BF),
            jax.ShapeDtypeStruct((wide, c_wide), BF),
        ]
        + [jax.ShapeDtypeStruct((piece_rows, c_wide), BF)] * pieces,
        compiler_params=params(),
        cost_estimate=pl.CostEstimate(
            flops=4_000_000_000, bytes_accessed=11_000_000, transcendentals=0
        ),
    )(depth, me, cot, dcol, w2, left)


def left_side(sel, me, grad_outer, rights, pieces, piece_rows):
    wide, c_wide = grad_outer.shape
    seqs = rights[0].shape[0]
    chunk = 256

    def kernel(sel_ref, me_ref, g_ref, *rest):
        k = len(rights)
        r_in = rest[:k]
        outs = rest[k : k + pieces]
        r_out = rest[k + pieces]
        acc = rest[k + pieces + 1]
        n = pl.program_id(0)

        @pl.when(n == 0)
        def _():
            acc[...] = jnp.zeros_like(acc)
            for t, r in enumerate(r_in):

                @pl.when(sel_ref[0] == t)
                def _():
                    r_out[...] = r[...]

        acc[0:seqs, pl.ds(pl.multiple_of(n * chunk, chunk), chunk)] = dot(
            r_out[...], g_ref[...], NT
        )

        @pl.when(n == pl.num_programs(0) - 1)
        def _():
            send_pieces(me_ref[0], acc, outs)

    return pl.pallas_call(
        kernel,
        name="grad_left_side",
        grid_spec=pltpu.PrefetchScalarGridSpec(
            num_scalar_prefetch=2,
            grid=(wide // chunk,),
            in_specs=[pl.BlockSpec((chunk, c_wide), lambda n, *_: (n, 0))]
            + [whole((seqs, c_wide))] * len(rights),
            out_specs=[whole((piece_rows, wide))] * pieces + [whole((seqs, c_wide))],
            scratch_shapes=[pltpu.VMEM((piece_rows * pieces, wide), F32)],
        ),
        out_shape=[jax.ShapeDtypeStruct((piece_rows, wide), BF)] * pieces
        + [jax.ShapeDtypeStruct((seqs, c_wide), BF)],
        compiler_params=params(),
        cost_estimate=pl.CostEstimate(
            flops=2_000_000_000, bytes_accessed=10_000_000, transcendentals=0
        ),
    )(sel, me, grad_outer, *rights)


def forward_kernel(depth_ref, lt_ref, r_ref, w2t, s_ref, dcol, bias, pu_ref, gw_ref):
    n = pl.program_id(0)
    i_blk, cols, pair = s_ref.shape
    narrow = lt_ref.shape[0] // i_blk
    outer = dot(lt_ref[...], r_ref[...]).astype(BF)
    lane = lax.broadcasted_iota(jnp.int32, (pair, 2 * cols), 1)
    low = lane < cols
    dep = dcol[...]
    total = None
    for ip in range(i_blk // 2):
        x = jnp.concatenate(
            [
                jnp.concatenate(
                    [
                        outer[
                            i * narrow : (i + 1) * narrow, dp * 2 * cols : (dp + 1) * 2 * cols
                        ]
                        for dp in range(narrow // 2)
                    ],
                    axis=0,
                )
                for i in (2 * ip, 2 * ip + 1)
            ],
            axis=1,
        )
        sbd = pair_block(s_ref[2 * ip], s_ref[2 * ip + 1])
        gw = dot(x, sbd)
        total = gw if total is None else total + gw
        pt = dot(w2t[...], x)
        e0, o0 = pt[:pair, : 2 * cols], pt[:pair, 2 * cols :]
        e1, o1 = pt[pair:, : 2 * cols], pt[pair:, 2 * cols :]
        both = jnp.where(low, e0, o1) + pltpu.roll(jnp.where(low, o0, e1), cols, 1)
        both = both.T + bias[...]
        for k in range(2):
            i = 2 * ip + k
            den = jnp.maximum(jnp.minimum(dep, depth_ref[n * i_blk + i].astype(F32)), 1.0)
            pu_ref[i] = (both[k * cols : (k + 1) * cols] / den).astype(BF)

    @pl.when(n == 0)
    def _():
        gw_ref[...] = total

    @pl.when(n > 0)
    def _():
        gw_ref[...] += total


def forward(depth, left_t, right, w2t, scaled, dcol, bias):
    rows, cols, pair = scaled.shape
    wide, seqs = left_t.shape
    narrow = wide // rows
    i_blk = 8
    return pl.pallas_call(
        forward_kernel,
        name="forward",
        grid_spec=pltpu.PrefetchScalarGridSpec(
            num_scalar_prefetch=1,
            grid=(rows // i_blk,),
            in_specs=[
                pl.BlockSpec((i_blk * narrow, seqs), lambda n, *_: (n, 0)),
                whole(right.shape),
                whole(w2t.shape),
                pl.BlockSpec((i_blk, cols, pair), lambda n, *_: (n, 0, 0)),
                whole(dcol.shape),
                whole((1, pair)),
            ],
            out_specs=[
                pl.BlockSpec((i_blk, cols, pair), lambda n, *_: (n, 0, 0)),
                whole((w2t.shape[1], w2t.shape[0])),
            ],
        ),
        out_shape=[
            jax.ShapeDtypeStruct((rows, cols, pair), BF),
            jax.ShapeDtypeStruct((w2t.shape[1], w2t.shape[0]), F32),
        ],
        compiler_params=params(),
        cost_estimate=pl.CostEstimate(
            flops=6_000_000_000, bytes_accessed=4_000_000, transcendentals=0
        ),
    )(depth, left_t, right, w2t, scaled, dcol, bias[None, :])


def tokens(depth, me, depth_row, lefts, rights, rows):
    piece_rows, wide = lefts[0].shape
    narrow = wide // rows
    count = piece_rows * rows

    def kernel(depth_ref, me_ref, drow, *rest):
        l_in = rest[: len(lefts)]
        r_in = rest[len(lefts) : len(lefts) + len(rights)]
        out, z, t = rest[len(lefts) + len(rights) :]
        base = me_ref[0] * piece_rows
        left = sum(ref[...].astype(F32) for ref in l_in)
        right = sum(ref[...].astype(F32) for ref in r_in)
        seq = lax.broadcasted_iota(jnp.int32, (piece_rows, narrow), 0) + base
        seq2 = lax.broadcasted_iota(jnp.int32, (piece_rows, 2 * rows), 0) + base
        on = seq2.astype(F32) < drow[...]
        for i in range(rows):
            v = jnp.where(seq < depth_ref[i], left[:, i * narrow : (i + 1) * narrow], 0.0)
            z[pl.ds(i, piece_rows, stride=rows), 0:narrow] = v
        for dp in range(narrow // 2):
            v = jnp.where(on, right[:, dp * 2 * rows : (dp + 1) * 2 * rows], 0.0)
            t[pl.ds(2 * dp, piece_rows, stride=narrow), :] = v[:, :rows]
            t[pl.ds(2 * dp + 1, piece_rows, stride=narrow), :] = v[:, rows:]
        per = 128 // narrow
        for q in range(piece_rows // per):
            tr = t[q * 128 : (q + 1) * 128, :].T
            for k in range(per):
                s = q * per + k
                z[s * rows : (s + 1) * rows, narrow : 2 * narrow] = tr[
                    :, k * narrow : (k + 1) * narrow
                ]
        h = count // 2
        out[...] = jnp.concatenate([z[:h, :], z[h:, :]], axis=1).astype(BF)

    n_in = len(lefts) + len(rights)
    return pl.pallas_call(
        kernel,
        name="tokens",
        grid_spec=pltpu.PrefetchScalarGridSpec(
            num_scalar_prefetch=2,
            grid=(1,),
            in_specs=[whole(depth_row.shape)] + [whole((piece_rows, wide))] * n_in,
            out_specs=whole((count // 2, 4 * narrow)),
            scratch_shapes=[
                pltpu.VMEM((count, 2 * narrow), F32),
                pltpu.VMEM((piece_rows * narrow, rows), F32),
            ],
        ),
        out_shape=jax.ShapeDtypeStruct((count // 2, 4 * narrow), BF),
        compiler_params=params(),
        cost_estimate=pl.CostEstimate(
            flops=2_000_000, bytes_accessed=2_000_000, transcendentals=0
        ),
    )(depth, me, depth_row, *lefts, *rights)


def weight_grads(me, q, normed, piece_rows):
    seqs, rows, chans = normed.shape
    h = q.shape[0]
    nar2 = q.shape[1] // 2
    last = seqs // piece_rows - 1

    def kernel(me_ref, q_ref, n_ref, out):
        n = n_ref[...].reshape(2 * h, chans)
        v = q_ref[...]
        top = dot(v, n[:h], TN)
        bot = dot(v, n[h:], TN)
        out[...] = top[:nar2] + bot[nar2:]

    return pl.pallas_call(
        kernel,
        name="weight_grads",
        grid_spec=pltpu.PrefetchScalarGridSpec(
            num_scalar_prefetch=1,
            grid=(1,),
            in_specs=[
                whole(q.shape),
                pl.BlockSpec(
                    (piece_rows, rows, chans), lambda n, me: (jnp.minimum(me[0], last), 0, 0)
                ),
            ],
            out_specs=whole((nar2, chans)),
        ),
        out_shape=jax.ShapeDtypeStruct((nar2, chans), F32),
        compiler_params=params(),
        cost_estimate=pl.CostEstimate(
            flops=400_000_000, bytes_accessed=1_000_000, transcendentals=0
        ),
    )(me, q, normed)


def finish(me, qs, alignment, wc):
    seqs, rows, chans = alignment.shape
    h, lanes = qs[0].shape
    piece_rows = 2 * h // rows
    pieces = len(qs)
    used = seqs // piece_rows

    def kernel(me_ref, x_ref, w_ref, *rest):
        q_in, out = rest[:-1], rest[-1]
        p = pl.program_id(0)
        t = lax.rem(me_ref[0] - p + pieces, pieces)
        w0 = w_ref[0]
        w1 = w_ref[1]
        for k in range(pieces):

            @pl.when(t == k)
            def _():
                for half in range(2):
                    w = w1 if half else w0
                    q = q_in[k][...]
                    g = dot(jnp.concatenate([q, q], axis=1), w)
                    for j in range(piece_rows // 2):
                        s = half * (piece_rows // 2) + j
                        x = x_ref[s].astype(F32)
                        c = x - jnp.mean(x, axis=-1, keepdims=True)
                        inv = lax.rsqrt(jnp.mean(c * c, axis=-1, keepdims=True) + 1e-05)
                        xh = c * inv
                        gc = g[j * rows : (j + 1) * rows]
                        m = jnp.mean(gc * xh, axis=-1, keepdims=True)
                        out[s] = (inv * (gc - xh * m)).astype(BF)

    blk = pl.BlockSpec((piece_rows, rows, chans), lambda p, *_: (p, 0, 0))
    return pl.pallas_call(
        kernel,
        name="finish",
        grid_spec=pltpu.PrefetchScalarGridSpec(
            num_scalar_prefetch=1,
            grid=(used,),
            in_specs=[blk, whole(wc.shape)] + [whole((h, lanes))] * pieces,
            out_specs=blk,
        ),
        out_shape=jax.ShapeDtypeStruct(alignment.shape, BF),
        compiler_params=params(),
        cost_estimate=pl.CostEstimate(
            flops=1_000_000_000, bytes_accessed=8_000_000, transcendentals=0
        ),
    )(me, alignment, wc, *qs)


def shift(value, axis, t):
    n = lax.axis_size(axis)
    return lax.ppermute(value, axis, [(k, (k + t) % n) for k in range(n)])


def scatter_sum(value, axis, dtype):
    n = lax.axis_size(axis)
    me = lax.axis_index(axis)
    m = value.shape[0] // n
    total = None
    for t in range(n):
        part = lax.dynamic_slice_in_dim(value, (me + t) % n * m, m, 0)
        if t:
            part = shift(part.astype(dtype), axis, t).astype(F32)
        total = part if total is None else total + part
    return total


def gather_rows(value, axis):
    n = lax.axis_size(axis)
    me = lax.axis_index(axis)
    m = value.shape[0]
    parts = [value] + [shift(value, axis, t) for t in range(1, n)]
    ring = parts[::-1]
    return lax.dynamic_slice_in_dim(
        jnp.concatenate(ring + ring, axis=0), (n - 1 - me) * m, n * m, 0
    )


def all_sum(value):
    if value.shape[0] % (lax.axis_size("row") * lax.axis_size("col")):
        return lax.psum(value, ("row", "col"))
    part = scatter_sum(scatter_sum(value, "row", F32), "col", F32)
    return gather_rows(gather_rows(part, "col"), "row")


def body(
    alignment,
    coverage,
    layer_norm_gain,
    layer_norm_bias,
    left_weight,
    right_weight,
    out_weight,
    out_bias,
    cotangent,
):
    n_row, n_col = lax.axis_size("row"), lax.axis_size("col")
    ratio = n_row // n_col
    row_index = lax.axis_index("row")
    col_index = lax.axis_index("col")
    me_row = row_index[None].astype(jnp.int32)
    me_col = col_index[None].astype(jnp.int32)
    seqs, rows, chans = alignment.shape
    narrow = left_weight.shape[1]
    pair = out_weight.shape[1]
    both = ("row", "col")

    depth = jnp.sum(coverage, axis=0)
    depth_parts = []
    for m in range(ratio):
        got = depth * (row_index == col_index * ratio + m)
        for t in range(1, n_row):
            pairs = [
                ((c * ratio + m) * n_col + c, (c * ratio + m + t) % n_row * n_col + c)
                for c in range(n_col)
            ]
            got = got + lax.ppermute(depth, both, pairs)
        depth_parts.append(got)

    normed, right, left, left_t = project(
        depth, alignment, layer_norm_gain, layer_norm_bias, left_weight, right_weight
    )
    normed = normed.reshape(seqs, rows, chans)

    w4 = out_weight.reshape(narrow, narrow // 2, 2, pair)
    w2 = jnp.transpose(w4, (1, 0, 2, 3)).reshape(narrow * narrow // 2, 2 * pair)
    w2t = w2.T

    piece_rows = (seqs // n_col + 7) // 8 * 8
    right_pieces, left_pieces, updates, grad_w = [], [], [], None
    scaled, grad_outer, dcols = [], [], []
    for m in range(ratio):
        dcol = jnp.broadcast_to(depth_parts[m].astype(F32)[:, None], (rows, pair))
        s, g, *pieces = right_side(
            depth, jnp.zeros_like(me_row), cotangent, dcol, w2, left, m, n_col, piece_rows
        )
        dcols.append(dcol)
        scaled.append(s)
        grad_outer.append(g)
        right_pieces.extend(pieces)

    sums = None
    stacked = jnp.stack(right_pieces)
    for t in range(n_row):
        part = lax.dynamic_index_in_dim(stacked, (row_index + t) % n_row, 0, keepdims=False)
        if t:
            part = shift(part, "row", t)
        sums = part.astype(F32) if sums is None else sums + part.astype(F32)
    turn = [
        ((m * n_col + k) * n_col + c, (c * ratio + m) * n_col + k)
        for m in range(ratio)
        for k in range(n_col)
        for c in range(n_col)
    ]
    right_sum = lax.ppermute(sums.astype(BF), both, turn)

    for m in range(ratio):
        rights = [right]
        for t in range(1, n_row):
            pairs = [
                ((c * ratio + m) * n_col + c, (c * ratio + m + t) % n_row * n_col + c)
                for c in range(n_col)
            ]
            rights.append(lax.ppermute(right, both, pairs))
        sel = (row_index - (col_index * ratio + m) + n_row) % n_row
        *pieces, right_cols = left_side(
            sel[None].astype(jnp.int32), me_col, grad_outer[m], rights, n_col, piece_rows
        )
        left_pieces.append(pieces)
        update, gw = forward(
            depth, left_t, right_cols, w2t, scaled[m], dcols[m], out_bias
        )
        updates.append(update)
        grad_w = gw if grad_w is None else grad_w + gw
    pair_update = updates[0] if ratio == 1 else jnp.concatenate(updates, axis=1)

    lefts = []
    for t in range(n_col):
        part = left_pieces[0][t]
        if ratio > 1:
            part = sum(p[t].astype(F32) for p in left_pieces).astype(BF)
        lefts.append(shift(part, "col", t) if t else part)

    depth_row = jnp.tile(depth.astype(F32), 2)[None, :]
    q = tokens(depth, me_col, depth_row, lefts, [right_sum], rows)
    grads = weight_grads(me_col, q, normed, piece_rows)
    qs = [q] + [shift(q, "col", t) for t in range(1, n_col)]

    weights = jnp.concatenate([left_weight, right_weight], axis=1).astype(F32).T
    weights = weights * layer_norm_gain
    centred = weights - jnp.mean(weights, axis=1, keepdims=True)
    hi = centred.astype(BF)
    lo = (centred - hi.astype(F32)).astype(BF)
    none = jnp.zeros_like(hi)
    wc = jnp.stack(
        [
            jnp.concatenate([hi, none, lo, none], axis=0),
            jnp.concatenate([none, hi, none, lo], axis=0),
        ]
    )
    gradient = finish(me_col, qs, alignment, wc)

    grad_w = all_sum(grad_w)
    grads = all_sum(grads)
    grad_out = jnp.transpose(
        grad_w.reshape(narrow // 2, narrow, 2, pair), (1, 0, 2, 3)
    ).reshape(narrow * narrow, pair)
    return pair_update, gradient, grads[:narrow].T, grads[narrow:].T, grad_out


def solution(mesh):
    return jax.shard_map(
        body,
        mesh=mesh,
        in_specs=(
            P("grp", "row", None),
            P("grp", "row"),
            P(),
            P(),
            P(),
            P(),
            P(),
            P(),
            P(("grp", "row"), "col", None),
        ),
        out_specs=(
            P(("grp", "row"), "col", None),
            P("grp", "row", None),
            P("grp", None),
            P("grp", None),
            P("grp", None),
        ),
        check_vma=False,
    )
```

time: 435 us -> 159 us (0.37); the launches traced: 428 us -> 157 us
  waiting for transfers between devices: 203 us -> 32 us
  matrix products: 97.4 us -> 0 us
  local copies, waits for them, and re-layouts: 85.8 us -> 18.5 us
  Pallas kernels: 0 us -> 53.1 us
  starting transfers between devices: 0.25 us -> 48 us
  other arithmetic: 19.3 us -> 4.06 us
  between operations: 14.4 us -> 1.48 us
  blocking collectives: 8.12 us -> 0 us
    psum x5 -> x0, waiting for transfers between devices: 184 us -> none  [the longest x1 71.5 us: body(): grad_out = lax.psum(out_part, ('row', 'col'))]
    dot_general x13 -> x0, matrix products: 97.4 us -> none  [the longest x1 17.8 us: body(): jnp.einsum('ijcd,sic->sjd', grad_outer, left, preferred_element_type=jnp....]
    pallas_call x0 -> x7, Pallas kernels: none -> 53.1 us  [the longest x1 11.5 us: finish(): pl.pallas_call(kernel, name='finish', grid_spec=pltpu.PrefetchScalarGridS...]
    ppermute x0 -> x40, starting transfers between devices: none -> 48 us  [the longest x33 33.5 us: shift(): return lax.ppermute(value, axis, [(k, (k + t) % n) for k in range(n)])]
    convert_element_type x5 -> x0, local copies, waits for them, and re-layouts: 46.6 us -> none  [the longest x1 24.2 us: body(): outer = jnp.einsum('sic,sjd->ijcd', left, right_cols, preferred_element_t...]
    ppermute x0 -> x40, waiting for transfers between devices: none -> 32 us  [the longest x33 24 us: shift(): return lax.ppermute(value, axis, [(k, (k + t) % n) for k in range(n)])]
    reshape x1 -> x3, local copies, waits for them, and re-layouts: 24 us -> 2.55 us  [the longest x1 1.19 us: body(): w4 = out_weight.reshape(narrow, narrow // 2, 2, pair)]
    all_gather x1 -> x0, waiting for transfers between devices: 18.2 us -> none  [body(): lax.all_gather(right, 'row', axis=1, tiled=True)]
  transfers between devices with their start and end apart: 6 -> 40, of which waited for: 6 -> 15; matrix products, arithmetic and copies ran while one was open for 25% -> 4% of each run, Pallas kernels for 0% -> 19%
where the time goes in v1:
time: 159 us; the launch traced here: 157 us
  Pallas kernels  53.1 us (33%)
  starting transfers between devices  48 us (30%)
  waiting for transfers between devices  32 us (20%)
  local copies, waits for them, and re-layouts  18.5 us (12%)
  other arithmetic  4.06 us (3%)
    ppermute x33, starting transfers between devices, shift(): return lax.ppermute(value, axis, [(k, (k + t) % n) for k in range(n)])  33.5 us
    ppermute x33, waiting for transfers between devices, shift(): return lax.ppermute(value, axis, [(k, (k + t) % n) for k in range(n)])  24 us
    unnamed x93, local copies, waits for them, and re-layouts  13.8 us
    pallas_call x1, Pallas kernels, finish(): pl.pallas_call(kernel, name='finish', grid_spec=pltpu.PrefetchScalarGridS...  11.5 us
    pallas_call x1, Pallas kernels, project(): pl.pallas_call(project_kernel, name='project', grid_spec=pltpu.PrefetchSc...  10.7 us
    pallas_call x1, Pallas kernels, forward(): pl.pallas_call(forward_kernel, name='forward', grid_spec=pltpu.PrefetchSc...  10.5 us
    pallas_call x1, Pallas kernels, right_side(): pl.pallas_call(right_kernel, name='grad_outer_right', grid_spec=pltpu.Pre...  8.77 us
    pallas_call x1, Pallas kernels, left_side(): pl.pallas_call(kernel, name='grad_left_side', grid_spec=pltpu.PrefetchSca...  8.5 us
  transfers between devices with their start and end apart: 40, of which 15 were waited for; matrix products, arithmetic and copies ran while one was open for 4% of the time, Pallas kernels for 19%

profile of v1, /device:TPU:0, one launch (start us, length us, event | category | flops | bytes accessed | tf_op | source)
XLA Modules:
  0.0 157.1 jit_solution(1329119457061393129)
XLA Ops:
  1.6 2.4 %collective-permute-start = (s32[64]{0:T(128)S(1)}, s32[64]{0:T(128)S(1)}, u32[]{:S(2)}, u32[]{:S(2)}) collective-permute-start(s32[64]{0:T(128)S(1)} %reduce_sum.18.depth_ref), channel_id=1, source_target_pairs={{0,4},{5,9},{10,14},{15,3},{16,20},{21,25},{26,30},{31,19}} | collective-permute-start | bytes 776 | tf_op jit(solution)/shard_map/ppermute | solution.py:568
  4.0 3.1 %collective-permute-start.1 = (s32[64]{0:T(128)S(1)}, s32[64]{0:T(128)S(1)}, u32[]{:S(2)}, u32[]{:S(2)}) collective-permute-start(s32[64]{0:T(128)S(1)} %reduce_sum.18.depth_ref), channel_id=1, source_target_pairs={{0,8},{5,13},{10,2},{15,7},{16,24},{21,29},{26,18},{31,23}} | collective-permute-start | bytes 776 | tf_op jit(solution)/shard_map/ppermute | solution.py:568
  13.7 10.7 %project.1 = (bf16[2,48,64,256]{3,2,1,0:T(8,128)(2,1)}, bf16[96,2048]{1,0:T(8,128)(2,1)S(1)}, bf16[96,2048]{1,0:T(8,128)(2,1)S(1)}, bf16[2048,96]{1,0:T(8,128)(2,1)S(1)}) custom-call(s32[64]{0:T(128)S(1)} %reduce_sum.18.depth_ref, bf16[2,48,64,256]{3,2,1,0:T(8,128)(2,1)} %bitcast.58, f32[1,128]{1,0:T(1,128)S(1)} %broadcast_in_dim_tile.4.depth_row.drow, ...), custom_call_target="tpu_custom_call" | custom-call | flops 201326592 | bytes 8000000 | tf_op jit(solution)/shard_map/project/pallas_call | solution.py:99
  24.5 8.8 %grad_outer_right.1 = (bf16[64,64,128]{2,1,0:T(8,128)(2,1)S(1)}, bf16[2048,2048]{1,0:T(8,128)(2,1)}, bf16[24,2048]{1,0:T(8,128)(2,1)S(1)}, bf16[24,2048]{1,0:T(8...) custom-call(s32[64]{0:T(128)S(1)} %reduce_sum.18.depth_ref, s32[1]{0:T(128)} %constant.102.clone.1.me_ref, ...), custom_call_target="tpu_custom_call" | custom-call | flops 4000000000 | bytes 11000000 | tf_op jit(solution)/shard_map/grad_outer_right/pallas_call | solution.py:199
  34.7 3.5 %collective-permute-start.3 = (bf16[96,2048]{1,0:T(8,128)(2,1)S(1)}, bf16[96,2048]{1,0:T(8,128)(2,1)S(1)}, u32[]{:S(2)}, u32[]{:S(2)}) collective-permute-start(bf16[96,2048]{1,0:T(8,128)(2,1)S(1)} %get-tuple-element.25.rest_0_), channel_id=1, source_target_pairs={{0,4},{5,9},{10,14},{15,3},{16,20},{21,25},{26,30},{31,19}} | collective-permute-start | bytes 1179656 | tf_op jit(solution)/shard_map/ppermute | solution.py:615
  44.8 6.3 %collective-permute-done.5.rest_3_ = bf16[96,2048]{1,0:T(8,128)(2,1)S(1)} collective-permute-done((bf16[96,2048]{1,0:T(8,128)(2,1)S(1)}, bf16[96,2048]{1,0:T(8,128)(2,1)S(1)}, u32[]{:S(2)}, u32[]{:S(2)}) %collective-permute-start.5) | collective-permute-done | bytes 393248 | tf_op jit(solution)/shard_map/ppermute | solution.py:615
  52.1 8.5 %grad_left_side.1 = (bf16[24,2048]{1,0:T(8,128)(2,1)S(1)}, bf16[24,2048]{1,0:T(8,128)(2,1)}, bf16[24,2048]{1,0:T(8,128)(2,1)}, bf16[24,2048]{1,0:T(8,128)(2,1)}, bf16[96,2048]{1,0:T(8,128)(2,1)S(1)}) custom-call(s32[1]{0:T(128)} %bitcast.4.sel_ref, s32[1]{0:T(128)} %bitcast.5.me_ref, bf16[2048,2048]{1,0:T(8,128)(2,1)} %get-tuple-element.24.g_ref, ...), custom_call_target="tpu_custom_call" | custom-call | flops 2000000000 | bytes 10000000 | tf_op jit(solution)/shard_map/grad_left_side/pallas_call | solution.py:260
  61.4 3.8 %collective-permute-start.8 = (bf16[24,2048]{1,0:T(8,128)(2,1)}, bf16[24,2048]{1,0:T(8,128)(2,1)}, u32[]{:S(2)}, u32[]{:S(2)}) collective-permute-start(bf16[24,2048]{1,0:T(8,128)(2,1)} %get-tuple-element.32), channel_id=1, source_target_pairs={{0,3},{1,0},{2,1},{3,2},{4,7},{5,4},{6,5},{7,6},{8,11},{9,8},{10,9... | collective-permute-start | bytes 294920 | tf_op jit(solution)/shard_map/ppermute | solution.py:503
  65.9 2.3 %collective-permute-done.6.rest_1_ = bf16[24,2048]{1,0:T(8,128)(2,1)S(1)} collective-permute-done((bf16[24,2048]{1,0:T(8,128)(2,1)}, bf16[24,2048]{1,0:T(8,128)(2,1)S(1)}, u32[]{:S(2)}, u32[]{:S(2)}) %collective-permute-start.6) | collective-permute-done | bytes 98336 | tf_op jit(solution)/shard_map/ppermute | solution.py:503
  68.8 2.8 %collective-permute-done.7.rest_2_ = bf16[24,2048]{1,0:T(8,128)(2,1)S(1)} collective-permute-done((bf16[24,2048]{1,0:T(8,128)(2,1)}, bf16[24,2048]{1,0:T(8,128)(2,1)S(1)}, u32[]{:S(2)}, u32[]{:S(2)}) %collective-permute-start.7) | collective-permute-done | bytes 98336 | tf_op jit(solution)/shard_map/ppermute | solution.py:503
  75.3 2.8 %tokens.1.rest_0_.q_ref = bf16[768,128]{1,0:T(8,128)(2,1)S(1)} custom-call(s32[64]{0:T(128)S(1)} %copy-done.16, s32[1]{0:T(128)} %bitcast.5.me_ref, f32[1,128]{1,0:T(1,128)S(1)} %copy-done.19, bf16[24,2048]{1,0:T(8,128)(2,1)S(1)} %get-tuple-element.29.rest_0_, bf16[24,2048]{1,0:T(8,128)(2,1)S(1)} %copy-done.7, bf16[24,2048]{1,0:T(8,128)(2,1)S(1)} %copy-done.9, ...), custom_call_target="tpu_custom_call" | custom-call | flops 2000000 | bytes 2000000 | tf_op jit(solution)/shard_map/tokens/pallas_call | solution.py:396
  78.7 1.7 %collective-permute-start.18 = (f32[16,256]{1,0:T(8,128)S(1)}, f32[16,256]{1,0:T(8,128)S(1)}, u32[]{:S(2)}, u32[]{:S(2)}) collective-permute-start(f32[16,256]{1,0:T(8,128)S(1)} %get-tuple-element.53), channel_id=1, source_target_pairs={{0,12},{4,0},{8,4},{12,8},{1,13},{5,1},{9,5},{13,9},{2,14},{6,2},{... | collective-permute-start | bytes 49160 | tf_op jit(solution)/shard_map/ppermute | solution.py:503
  82.4 2.2 %collective-permute-start.19 = (f32[4,256]{1,0:T(4,128)S(1)}, f32[4,256]{1,0:T(4,128)S(1)}, u32[]{:S(2)}, u32[]{:S(2)}) collective-permute-start(f32[4,256]{1,0:T(4,128)S(1)} %get-tuple-element.55), channel_id=1, source_target_pairs={{0,1},{1,2},{2,3},{3,0},{4,5},{5,6},{6,7},{7,4},{8,9},{9,10},{10,1... | collective-permute-start | bytes 12296 | tf_op jit(solution)/shard_map/ppermute | solution.py:503
  84.6 2.4 %collective-permute-start.20 = (f32[4,256]{1,0:T(4,128)S(1)}, f32[4,256]{1,0:T(4,128)S(1)}, u32[]{:S(2)}, u32[]{:S(2)}) collective-permute-start(f32[4,256]{1,0:T(4,128)S(1)} %get-tuple-element.57), channel_id=1, source_target_pairs={{0,2},{1,3},{2,0},{3,1},{4,6},{5,7},{6,4},{7,5},{8,10},{9,11},{10,... | collective-permute-start | bytes 12296 | tf_op jit(solution)/shard_map/ppermute | solution.py:503
  92.2 10.5 %forward.1 = (bf16[64,64,128]{2,1,0:T(8,128)(2,1)}, f32[512,256]{1,0:T(8,128)S(1)}) custom-call(s32[64]{0:T(128)S(1)} %copy-done.17, bf16[2048,96]{1,0:T(8,128)(2,1)S(1)} %copy-done.23, bf16[96,2048]{1,0:T(8,128)(2,1)S(1)} %copy-done.25, bf16[256,512]{1,0:T(8,128)(2,1)S(1)} %bitcast.49, bf16[64,64,128]{2,1,0:T(8,128)(2,1)S(1)} %copy-done.28, ...), custom_call_target="tpu_custom_call" | custom-call | flops 6000000000 | bytes 4000000 | tf_op jit(solution)/shard_map/forward/pallas_call | solution.py:332
  108.3 3.0 %collective-permute-done.23 = f32[4,256]{1,0:T(4,128)S(1)} collective-permute-done((f32[4,256]{1,0:T(4,128)S(1)}, f32[4,256]{1,0:T(4,128)S(1)}, u32[]{:S(2)}, u32[]{:S(2)}) %collective-permute-start.23) | collective-permute-done | bytes 4128 | tf_op jit(solution)/shard_map/ppermute | solution.py:503
  111.7 1.9 %collective-permute-done.24 = f32[4,256]{1,0:T(4,128)S(1)} collective-permute-done((f32[4,256]{1,0:T(4,128)S(1)}, f32[4,256]{1,0:T(4,128)S(1)}, u32[]{:S(2)}, u32[]{:S(2)}) %collective-permute-start.24) | collective-permute-done | bytes 4128 | tf_op jit(solution)/shard_map/ppermute | solution.py:503
  115.2 2.1 %collective-permute-start.31 = (f32[32,256]{1,0:T(8,128)S(1)}, f32[32,256]{1,0:T(8,128)S(1)}, u32[]{:S(2)}, u32[]{:S(2)}) collective-permute-start(f32[32,256]{1,0:T(8,128)S(1)} %get-tuple-element.45), channel_id=1, source_target_pairs={{0,1},{1,2},{2,3},{3,0},{4,5},{5,6},{6,7},{7,4},{8,9},{9,10},{10,1... | collective-permute-start | bytes 98312 | tf_op jit(solution)/shard_map/ppermute | solution.py:503
  117.6 2.9 %collective-permute-start.32 = (f32[32,256]{1,0:T(8,128)S(1)}, f32[32,256]{1,0:T(8,128)S(1)}, u32[]{:S(2)}, u32[]{:S(2)}) collective-permute-start(f32[32,256]{1,0:T(8,128)S(1)} %get-tuple-element.47), channel_id=1, source_target_pairs={{0,2},{1,3},{2,0},{3,1},{4,6},{5,7},{6,4},{7,5},{8,10},{9,11},{10,... | collective-permute-start | bytes 98312 | tf_op jit(solution)/shard_map/ppermute | solution.py:503
  123.3 5.5 %collective-permute-done.32 = f32[32,256]{1,0:T(8,128)S(1)} collective-permute-done((f32[32,256]{1,0:T(8,128)S(1)}, f32[32,256]{1,0:T(8,128)S(1)}, u32[]{:S(2)}, u32[]{:S(2)}) %collective-permute-start.32) | collective-permute-done | bytes 32800 | tf_op jit(solution)/shard_map/ppermute | solution.py:503
  129.2 5.3 %collective-permute-start.34 = (f32[32,256]{1,0:T(8,128)S(1)}, f32[32,256]{1,0:T(8,128)S(1)}, u32[]{:S(2)}, u32[]{:S(2)}) collective-permute-start(f32[32,256]{1,0:T(8,128)S(1)} %add_add_fusion.1), channel_id=1, source_target_pairs={{0,3},{1,0},{2,1},{3,2},{4,7},{5,4},{6,5},{7,6},{8,11},{9,8},{10,9... | collective-permute-start | bytes 98312 | tf_op jit(solution)/shard_map/ppermute | solution.py:503
  136.0 1.8 %collective-permute-start.36 = (f32[32,256]{1,0:T(8,128)S(1)}, f32[32,256]{1,0:T(8,128)S(1)}, u32[]{:S(2)}, u32[]{:S(2)}) collective-permute-start(f32[32,256]{1,0:T(8,128)S(1)} %add_add_fusion.1), channel_id=1, source_target_pairs={{0,1},{1,2},{2,3},{3,0},{4,5},{5,6},{6,7},{7,4},{8,9},{9,10},{10,1... | collective-permute-start | bytes 98312 | tf_op jit(solution)/shard_map/ppermute | solution.py:503
  139.4 2.6 %collective-permute-done.36 = f32[32,256]{1,0:T(8,128)S(1)} collective-permute-done((f32[32,256]{1,0:T(8,128)S(1)}, f32[32,256]{1,0:T(8,128)S(1)}, u32[]{:S(2)}, u32[]{:S(2)}) %collective-permute-start.36) | collective-permute-done | bytes 32800 | tf_op jit(solution)/shard_map/ppermute | solution.py:503
  144.0 11.5 %finish.1 = bf16[96,64,256]{2,1,0:T(8,128)(2,1)} custom-call(s32[1]{0:T(128)} %bitcast.5.me_ref, bf16[96,64,256]{2,1,0:T(8,128)(2,1)} %x_ref.1, bf16[2,256,256]{2,1,0:T(8,128)(2,1)S(1)} %pad_maximum_fusion.1.w_ref, bf16[768,128]{1,0:T(8,128)(2,1)S(1)} %tokens.1.rest_0_.q_ref, bf16[768,128]{1,0:T(8,128)(2,1)S(1)} %collective-permute-done.13.rest_1_, ...), custom_call_target="tpu_custom_call" | custom-call | flops 1000000000 | bytes 8000000 | tf_op jit(solution)/shard_map/finish/pallas_call | solution.py:484
  (191 shorter events, 47.2 us)
Async XLA Ops:
  1.6 9.9 %collective-permute-start = (s32[64]{0:T(128)S(1)}, s32[64]{0:T(128)S(1)}, u32[]{:S(2)}, u32[]{:S(2)}) collective-permute-start(s32[64]{0:T(128)S(1)} %reduce_sum.18.depth_ref), channel_id=1, source_target_pairs={{0,4},{5,9},{10,14},{15,3},{16,20},{21,25},{26,30},{31,19}} | collective-permute-start | bytes 776 | tf_op jit(solution)/shard_map/ppermute | solution.py:568
  4.0 7.5 %collective-permute-start.1 = (s32[64]{0:T(128)S(1)}, s32[64]{0:T(128)S(1)}, u32[]{:S(2)}, u32[]{:S(2)}) collective-permute-start(s32[64]{0:T(128)S(1)} %reduce_sum.18.depth_ref), channel_id=1, source_target_pairs={{0,8},{5,13},{10,2},{15,7},{16,24},{21,29},{26,18},{31,23}} | collective-permute-start | bytes 776 | tf_op jit(solution)/shard_map/ppermute | solution.py:568
  33.5 7.4 %collective-permute-start.11 = (bf16[24,2048]{1,0:T(8,128)(2,1)S(1)}, bf16[24,2048]{1,0:T(8,128)(2,1)S(1)}, u32[]{:S(2)}, u32[]{:S(2)}) collective-permute-start(bf16[24,2048]{1,0:T(8,128)(2,1)S(1)} %get-tuple-element.43), channel_id=1, source_target_pairs={{0,12},{4,0},{8,4},{12,8},{1,13},{5,1},{9,5},{13,9},{2,14},{6,2},{... | collective-permute-start | bytes 294920 | tf_op jit(solution)/shard_map/ppermute | solution.py:503
  33.5 7.4 %collective-permute-start.9 = (bf16[24,2048]{1,0:T(8,128)(2,1)S(1)}, bf16[24,2048]{1,0:T(8,128)(2,1)S(1)}, u32[]{:S(2)}, u32[]{:S(2)}) collective-permute-start(bf16[24,2048]{1,0:T(8,128)(2,1)S(1)} %get-tuple-element.42), channel_id=1, source_target_pairs={{0,4},{4,8},{8,12},{12,0},{1,5},{5,9},{9,13},{13,1},{2,6},{6,10},{... | collective-permute-start | bytes 294920 | tf_op jit(solution)/shard_map/ppermute | solution.py:503
  34.7 8.4 %collective-permute-start.3 = (bf16[96,2048]{1,0:T(8,128)(2,1)S(1)}, bf16[96,2048]{1,0:T(8,128)(2,1)S(1)}, u32[]{:S(2)}, u32[]{:S(2)}) collective-permute-start(bf16[96,2048]{1,0:T(8,128)(2,1)S(1)} %get-tuple-element.25.rest_0_), channel_id=1, source_target_pairs={{0,4},{5,9},{10,14},{15,3},{16,20},{21,25},{26,30},{31,19}} | collective-permute-start | bytes 1179656 | tf_op jit(solution)/shard_map/ppermute | solution.py:615
  39.5 11.6 %collective-permute-start.5 = (bf16[96,2048]{1,0:T(8,128)(2,1)S(1)}, bf16[96,2048]{1,0:T(8,128)(2,1)S(1)}, u32[]{:S(2)}, u32[]{:S(2)}) collective-permute-start(bf16[96,2048]{1,0:T(8,128)(2,1)S(1)} %get-tuple-element.25.rest_0_), channel_id=1, source_target_pairs={{0,12},{5,1},{10,6},{15,11},{16,28},{21,17},{26,22},{31,27}} | collective-permute-start | bytes 1179656 | tf_op jit(solution)/shard_map/ppermute | solution.py:615
  41.6 24.3 %collective-permute-start.12 = (bf16[24,2048]{1,0:T(8,128)(2,1)}, bf16[24,2048]{1,0:T(8,128)(2,1)S(1)}, u32[]{:S(2)}, u32[]{:S(2)}) collective-permute-start(bf16[24,2048]{1,0:T(8,128)(2,1)} %fusion.2), channel_id=1, source_target_pairs={{0,0},{1,4},{2,8},{3,12},{4,1},{5,5},{6,9},{7,13},{8,2},{9,6},{10,... | collective-permute-start | bytes 294920 | tf_op jit(solution)/shard_map/ppermute | solution.py:606
  61.4 10.3 %collective-permute-start.7 = (bf16[24,2048]{1,0:T(8,128)(2,1)}, bf16[24,2048]{1,0:T(8,128)(2,1)S(1)}, u32[]{:S(2)}, u32[]{:S(2)}) collective-permute-start(bf16[24,2048]{1,0:T(8,128)(2,1)} %get-tuple-element.31), channel_id=1, source_target_pairs={{0,2},{1,3},{2,0},{3,1},{4,6},{5,7},{6,4},{7,5},{8,10},{9,11},{10,... | collective-permute-start | bytes 294920 | tf_op jit(solution)/shard_map/ppermute | solution.py:503
  61.4 10.9 %collective-permute-start.8 = (bf16[24,2048]{1,0:T(8,128)(2,1)}, bf16[24,2048]{1,0:T(8,128)(2,1)}, u32[]{:S(2)}, u32[]{:S(2)}) collective-permute-start(bf16[24,2048]{1,0:T(8,128)(2,1)} %get-tuple-element.32), channel_id=1, source_target_pairs={{0,3},{1,0},{2,1},{3,2},{4,7},{5,4},{6,5},{7,6},{8,11},{9,8},{10,9... | collective-permute-start | bytes 294920 | tf_op jit(solution)/shard_map/ppermute | solution.py:503
  82.4 20.3 %collective-permute-start.19 = (f32[4,256]{1,0:T(4,128)S(1)}, f32[4,256]{1,0:T(4,128)S(1)}, u32[]{:S(2)}, u32[]{:S(2)}) collective-permute-start(f32[4,256]{1,0:T(4,128)S(1)} %get-tuple-element.55), channel_id=1, source_target_pairs={{0,1},{1,2},{2,3},{3,0},{4,5},{5,6},{6,7},{7,4},{8,9},{9,10},{10,1... | collective-permute-start | bytes 12296 | tf_op jit(solution)/shard_map/ppermute | solution.py:503
  84.6 18.1 %collective-permute-start.20 = (f32[4,256]{1,0:T(4,128)S(1)}, f32[4,256]{1,0:T(4,128)S(1)}, u32[]{:S(2)}, u32[]{:S(2)}) collective-permute-start(f32[4,256]{1,0:T(4,128)S(1)} %get-tuple-element.57), channel_id=1, source_target_pairs={{0,2},{1,3},{2,0},{3,1},{4,6},{5,7},{6,4},{7,5},{8,10},{9,11},{10,... | collective-permute-start | bytes 12296 | tf_op jit(solution)/shard_map/ppermute | solution.py:503
  87.0 15.7 %collective-permute-start.21 = (f32[4,256]{1,0:T(4,128)S(1)}, f32[4,256]{1,0:T(4,128)S(1)}, u32[]{:S(2)}, u32[]{:S(2)}) collective-permute-start(f32[4,256]{1,0:T(4,128)S(1)} %get-tuple-element.56), channel_id=1, source_target_pairs={{0,3},{1,0},{2,1},{3,2},{4,7},{5,4},{6,5},{7,6},{8,11},{9,8},{10,9... | collective-permute-start | bytes 12296 | tf_op jit(solution)/shard_map/ppermute | solution.py:503
  104.2 9.5 %collective-permute-start.28 = (f32[128,256]{1,0:T(8,128)S(1)}, f32[128,256]{1,0:T(8,128)S(1)}, u32[]{:S(2)}, u32[]{:S(2)}) collective-permute-start(f32[128,256]{1,0:T(8,128)S(1)} %get-tuple-element.39), channel_id=1, source_target_pairs={{0,4},{4,8},{8,12},{12,0},{1,5},{5,9},{9,13},{13,1},{2,6},{6,10},{... | collective-permute-start | bytes 393224 | tf_op jit(solution)/shard_map/ppermute | solution.py:503
  104.3 9.4 %collective-permute-start.29 = (f32[128,256]{1,0:T(8,128)S(1)}, f32[128,256]{1,0:T(8,128)S(1)}, u32[]{:S(2)}, u32[]{:S(2)}) collective-permute-start(f32[128,256]{1,0:T(8,128)S(1)} %get-tuple-element.41), channel_id=1, source_target_pairs={{0,8},{4,12},{8,0},{12,4},{1,9},{5,13},{9,1},{13,5},{2,10},{6,14},... | collective-permute-start | bytes 393224 | tf_op jit(solution)/shard_map/ppermute | solution.py:503
  105.4 9.5 %collective-permute-start.30 = (f32[128,256]{1,0:T(8,128)S(1)}, f32[128,256]{1,0:T(8,128)S(1)}, u32[]{:S(2)}, u32[]{:S(2)}) collective-permute-start(f32[128,256]{1,0:T(8,128)S(1)} %get-tuple-element.40), channel_id=1, source_target_pairs={{0,12},{4,0},{8,4},{12,8},{1,13},{5,1},{9,5},{13,9},{2,14},{6,2},{... | collective-permute-start | bytes 393224 | tf_op jit(solution)/shard_map/ppermute | solution.py:503
  111.3 32.4 %collective-permute-start.13 = (bf16[768,128]{1,0:T(8,128)(2,1)S(1)}, bf16[768,128]{1,0:T(8,128)(2,1)S(1)}, u32[]{:S(2)}, u32[]{:S(2)}) collective-permute-start(bf16[768,128]{1,0:T(8,128)(2,1)S(1)} %tokens.1.rest_0_.q_ref), channel_id=1, source_target_pairs={{0,1},{1,2},{2,3},{3,0},{4,5},{5,6},{6,7},{7,4},{8,9},{9,10},{10,1... | collective-permute-start | bytes 589832 | tf_op jit(solution)/shard_map/ppermute | solution.py:503
  113.6 30.4 %collective-permute-start.14 = (bf16[768,128]{1,0:T(8,128)(2,1)S(1)}, bf16[768,128]{1,0:T(8,128)(2,1)S(1)}, u32[]{:S(2)}, u32[]{:S(2)}) collective-permute-start(bf16[768,128]{1,0:T(8,128)(2,1)S(1)} %tokens.1.rest_0_.q_ref), channel_id=1, source_target_pairs={{0,2},{1,3},{2,0},{3,1},{4,6},{5,7},{6,4},{7,5},{8,10},{9,11},{10,... | collective-permute-start | bytes 589832 | tf_op jit(solution)/shard_map/ppermute | solution.py:503
  115.2 8.1 %collective-permute-start.31 = (f32[32,256]{1,0:T(8,128)S(1)}, f32[32,256]{1,0:T(8,128)S(1)}, u32[]{:S(2)}, u32[]{:S(2)}) collective-permute-start(f32[32,256]{1,0:T(8,128)S(1)} %get-tuple-element.45), channel_id=1, source_target_pairs={{0,1},{1,2},{2,3},{3,0},{4,5},{5,6},{6,7},{7,4},{8,9},{9,10},{10,1... | collective-permute-start | bytes 98312 | tf_op jit(solution)/shard_map/ppermute | solution.py:503
  117.6 11.2 %collective-permute-start.32 = (f32[32,256]{1,0:T(8,128)S(1)}, f32[32,256]{1,0:T(8,128)S(1)}, u32[]{:S(2)}, u32[]{:S(2)}) collective-permute-start(f32[32,256]{1,0:T(8,128)S(1)} %get-tuple-element.47), channel_id=1, source_target_pairs={{0,2},{1,3},{2,0},{3,1},{4,6},{5,7},{6,4},{7,5},{8,10},{9,11},{10,... | collective-permute-start | bytes 98312 | tf_op jit(solution)/shard_map/ppermute | solution.py:503
  120.5 8.6 %collective-permute-start.33 = (f32[32,256]{1,0:T(8,128)S(1)}, f32[32,256]{1,0:T(8,128)S(1)}, u32[]{:S(2)}, u32[]{:S(2)}) collective-permute-start(f32[32,256]{1,0:T(8,128)S(1)} %get-tuple-element.46), channel_id=1, source_target_pairs={{0,3},{1,0},{2,1},{3,2},{4,7},{5,4},{6,5},{7,6},{8,11},{9,8},{10,9... | collective-permute-start | bytes 98312 | tf_op jit(solution)/shard_map/ppermute | solution.py:503
  123.3 20.7 %collective-permute-start.15 = (bf16[768,128]{1,0:T(8,128)(2,1)S(1)}, bf16[768,128]{1,0:T(8,128)(2,1)S(1)}, u32[]{:S(2)}, u32[]{:S(2)}) collective-permute-start(bf16[768,128]{1,0:T(8,128)(2,1)S(1)} %tokens.1.rest_0_.q_ref), channel_id=1, source_target_pairs={{0,3},{1,0},{2,1},{3,2},{4,7},{5,4},{6,5},{7,6},{8,11},{9,8},{10,9... | collective-permute-start | bytes 589832 | tf_op jit(solution)/shard_map/ppermute | solution.py:503
  142.1 13.4 %collective-permute-start.37 = (f32[128,256]{1,0:T(8,128)S(1)}, f32[128,256]{1,0:T(8,128)S(1)}, u32[]{:S(2)}, u32[]{:S(2)}) collective-permute-start(f32[128,256]{1,0:T(8,128)S(1)} %constant_dynamic-slice_fusion.1), channel_id=1, source_target_pairs={{0,12},{4,0},{8,4},{12,8},{1,13},{5,1},{9,5},{13,9},{2,14},{6,2},{... | collective-permute-start | bytes 393224 | tf_op jit(solution)/shard_map/ppermute | solution.py:503
  142.8 12.7 %collective-permute-start.38 = (f32[128,256]{1,0:T(8,128)S(1)}, f32[128,256]{1,0:T(8,128)S(1)}, u32[]{:S(2)}, u32[]{:S(2)}) collective-permute-start(f32[128,256]{1,0:T(8,128)S(1)} %constant_dynamic-slice_fusion.1), channel_id=1, source_target_pairs={{0,8},{4,12},{8,0},{12,4},{1,9},{5,13},{9,1},{13,5},{2,10},{6,14},... | collective-permute-start | bytes 393224 | tf_op jit(solution)/shard_map/ppermute | solution.py:503
  143.8 11.8 %collective-permute-start.39 = (f32[128,256]{1,0:T(8,128)S(1)}, f32[128,256]{1,0:T(8,128)S(1)}, u32[]{:S(2)}, u32[]{:S(2)}) collective-permute-start(f32[128,256]{1,0:T(8,128)S(1)} %constant_dynamic-slice_fusion.1), channel_id=1, source_target_pairs={{0,4},{4,8},{8,12},{12,0},{1,5},{5,9},{9,13},{13,1},{2,6},{6,10},{... | collective-permute-start | bytes 393224 | tf_op jit(solution)/shard_map/ppermute | solution.py:503
  (51 other events, 368.5 us)

commit v2 on v0

v2 whole, which is shorter than its diff:
```python
import jax
import jax.numpy as jnp
from jax import lax
from jax.experimental import pallas as pl
from jax.experimental.pallas import tpu as pltpu
from jax.sharding import PartitionSpec as P

BF = jnp.bfloat16
F32 = jnp.float32
NN = (((1,), (0,)), ((), ()))
NT = (((1,), (1,)), ((), ()))
TN = (((0,), (0,)), ((), ()))
VMEM = 64 * 1024 * 1024
IBLK = 8


def params():
    return pltpu.CompilerParams(vmem_limit_bytes=VMEM)


def dot(a, b, dims=NN):
    return lax.dot_general(a, b, dims, preferred_element_type=F32)


def whole(shape):
    return pl.BlockSpec(shape, lambda *_: (0,) * len(shape))


def shape(dims, dtype=BF):
    return jax.ShapeDtypeStruct(dims, dtype)


def call(kernel, name, grid, ins, outs, scratch, scalars, arrays, flops, bytes_accessed):
    return pl.pallas_call(
        kernel,
        name=name,
        grid_spec=pltpu.PrefetchScalarGridSpec(
            num_scalar_prefetch=len(scalars),
            grid=grid,
            in_specs=ins,
            out_specs=[o[0] for o in outs],
            scratch_shapes=scratch,
        ),
        out_shape=[o[1] for o in outs],
        compiler_params=params(),
        cost_estimate=pl.CostEstimate(
            flops=int(flops) // 10**6, bytes_accessed=1024, transcendentals=0
        ),
    )(*scalars, *arrays)


def depth_rows(cov, lanes):
    total = jnp.sum(cov.astype(F32), axis=1, keepdims=True)
    return jnp.broadcast_to(total, (cov.shape[0], lanes))


def depth_lanes(cov):
    row = depth_rows(cov, cov.shape[0]).T[0:1, :]
    return jnp.concatenate([row, row], axis=1)


def project(cov_t, alignment, gain, bias, wr_t):
    seqs, rows, chans = alignment.shape
    narrow = wr_t.shape[0]
    half = seqs // 2
    blk = 16
    steps = half // blk
    wide = rows * narrow

    def kernel(
        cov_ref, x_ref, gain_ref, bias_ref, w_ref, normed_ref, xhat_ref, stat_ref, r_ref, ys, nbs
    ):
        n = pl.program_id(0)
        gain_v = gain_ref[...]
        bias_v = bias_ref[...]
        lane = lax.broadcasted_iota(jnp.int32, (rows, 128), 1)
        for s2 in range(2):
            for g in range(blk):
                if g % 8 == 0:
                    stat = jnp.zeros((rows, 128), F32)
                x = x_ref[s2, g].astype(F32)
                mean = jnp.mean(x, axis=-1, keepdims=True)
                c = x - mean
                inv = lax.rsqrt(jnp.mean(c * c, axis=-1, keepdims=True) + 1e-05)
                xhat = c * inv
                nb = (xhat * gain_v + bias_v).astype(BF)
                normed_ref[s2, g] = nb
                xhat_ref[s2, g] = xhat.astype(BF)
                at = (2 * g + s2) * rows
                nbs[at : at + rows, :] = nb
                stat = jnp.where(lane == g % 8, inv, stat)
                stat_ref[s2, g // 8] = stat
        y = dot(w_ref[...], nbs[...], NT)
        for g in range(blk):
            at = (n * blk + g) * narrow
            ys[pl.ds(pl.multiple_of(at, narrow), narrow), :] = y[
                :, g * 2 * rows : (g + 1) * 2 * rows
            ]

        @pl.when(n == steps - 1)
        def _():
            lanes = lax.broadcasted_iota(jnp.int32, (half, 2 * rows), 1)
            seq = lax.broadcasted_iota(jnp.int32, (half, 2 * rows), 0).astype(F32)
            low = lanes < rows
            dep = depth_lanes(cov_ref[...])
            top_on = seq < dep
            bot_on = seq + half < dep
            for dp in range(narrow // 2):
                even = ys[pl.ds(2 * dp, half, stride=narrow), :]
                odd = ys[pl.ds(2 * dp + 1, half, stride=narrow), :]
                top = jnp.where(low, even, pltpu.roll(odd, rows, 1))
                bot = jnp.where(low, pltpu.roll(even, rows, 1), odd)
                at = slice(dp * 2 * rows, (dp + 1) * 2 * rows)
                r_ref[0:half, at] = jnp.where(top_on, top, 0.0).astype(BF)
                r_ref[half : 2 * half, at] = jnp.where(bot_on, bot, 0.0).astype(BF)

    tile = pl.BlockSpec((2, blk, rows, chans), lambda n: (0, n, 0, 0))
    return call(
        kernel,
        "project",
        (steps,),
        [
            whole(cov_t.shape),
            tile,
            whole((1, chans)),
            whole((1, chans)),
            whole(wr_t.shape),
        ],
        [
            (tile, shape((2, half, rows, chans))),
            (tile, shape((2, half, rows, chans))),
            (
                pl.BlockSpec((2, blk // 8, rows, 128), lambda n: (0, n, 0, 0)),
                shape((2, half // 8, rows, 128), F32),
            ),
            (whole((seqs, wide)), shape((seqs, wide))),
        ],
        [
            pltpu.VMEM((half * narrow, 2 * rows), F32),
            pltpu.VMEM((2 * blk * rows, chans), BF),
        ],
        (),
        (
            cov_t,
            alignment.reshape(2, half, rows, chans),
            gain[None, :],
            bias[None, :],
            wr_t,
        ),
        2e9,
        7e6,
    )


def pair_block(a, b):
    z = jnp.zeros_like(a)
    return jnp.concatenate(
        [
            jnp.concatenate([a, z], axis=1),
            jnp.concatenate([z, a], axis=1),
            jnp.concatenate([b, z], axis=1),
            jnp.concatenate([z, b], axis=1),
        ],
        axis=0,
    )


def rows_at(p, count):
    start = p * count
    if count % 8 == 0:
        start = pl.multiple_of(start, 8)
    return pl.ds(start, count)


def send_pieces(me, acc, outs):
    rows = outs[0].shape[0]
    count = len(outs)
    for t, out in enumerate(outs):
        p = lax.rem(me + t, count)
        out[...] = acc[rows_at(p, rows), :].astype(out.dtype)


def right_side(own, me, cov_t, cov_far, cot, out_weight, wl_t, normed, block, pieces, piece_rows):
    rows, _, pair = cot.shape
    seqs, _, chans = normed.shape
    cols = cov_far.shape[0]
    narrow = wl_t.shape[0]
    wide = rows * narrow
    c_wide = cols * narrow
    i_blk = 16

    def kernel(
        own_ref,
        me_ref,
        cov_ref,
        far_ref,
        cot_ref,
        wo_ref,
        wl_ref,
        n_ref,
        s_ref,
        g_ref,
        w2_ref,
        lt_ref,
        dcol,
        *rest,
    ):
        outs = rest[:pieces]
        acc, wide_f, z, drow = rest[pieces:]
        n = pl.program_id(0)

        @pl.when(n == 0)
        def _():
            acc[...] = jnp.zeros_like(acc)
            drow[...] = depth_rows(cov_ref[...], 128)
            mine = (own_ref[0] == 1).astype(F32)
            far = depth_rows(far_ref[...], 128)
            dcol[...] = mine * drow[...] + (1.0 - mine) * far
            wide_f[...] = wo_ref[...].astype(F32)
            for dp in range(narrow // 2):
                for d2 in range(2):
                    v = wide_f[pl.ds(2 * dp + d2, narrow, stride=narrow), :]
                    w2_ref[dp * narrow : (dp + 1) * narrow, d2 * pair : (d2 + 1) * pair] = (
                        v.astype(BF)
                    )

        dep = dcol[...]
        w = w2_ref[...]
        mine_rows = drow[pl.ds(pl.multiple_of(n * i_blk, i_blk), i_blk), :]
        blk = n_ref[...].astype(F32).reshape(seqs * i_blk, chans).astype(BF)
        z[...] = dot(blk, wl_ref[...], NT)
        seq = lax.broadcasted_iota(jnp.int32, (seqs, narrow), 0).astype(F32)
        per = 128 // narrow
        tiles = []
        for q in range(i_blk // per):
            parts = []
            for k in range(per):
                i = q * per + k
                v = z[pl.ds(i, seqs, stride=i_blk), :]
                parts.append(jnp.where(seq < mine_rows[i : i + 1, :narrow], v, 0.0))
            tile = jnp.concatenate(parts, axis=1)
            lt_ref[q * 128 : (q + 1) * 128, :] = tile.T.astype(BF)
            tiles.append(tile.astype(BF))
        left = jnp.concatenate(tiles, axis=1)
        for ip in range(i_blk // 2):
            scaled = []
            for k in range(2):
                i = 2 * ip + k
                den = jnp.maximum(jnp.minimum(dep, mine_rows[i : i + 1, :]), 1.0)
                s = (cot_ref[i].astype(F32) / den).astype(BF)
                s_ref[i] = s
                scaled.append(s)
            g = dot(w, pair_block(*scaled), NT).astype(BF)
            for k in range(2):
                i = 2 * ip + k
                for dp in range(narrow // 2):
                    g_ref[
                        i * narrow : (i + 1) * narrow, dp * 2 * cols : (dp + 1) * 2 * cols
                    ] = g[dp * narrow : (dp + 1) * narrow, k * 2 * cols : (k + 1) * 2 * cols]
        acc[0:seqs, :] += dot(left, g_ref[...])

        @pl.when(n == pl.num_programs(0) - 1)
        def _():
            send_pieces(me_ref[0], acc, outs)

    return call(
        kernel,
        "grad_outer_right",
        (rows // i_blk,),
        [
            whole(cov_t.shape),
            whole(cov_far.shape),
            pl.BlockSpec((i_blk, cols, pair), lambda n, *_: (n, block, 0)),
            whole(out_weight.shape),
            whole(wl_t.shape),
            pl.BlockSpec((seqs, i_blk, chans), lambda n, *_: (0, n, 0)),
        ],
        [
            (
                pl.BlockSpec((i_blk, cols, pair), lambda n, *_: (n, 0, 0)),
                shape((rows, cols, pair)),
            ),
            (pl.BlockSpec((i_blk * narrow, c_wide), lambda n, *_: (n, 0)), shape((wide, c_wide))),
            (
                whole((narrow * narrow // 2, 2 * pair)),
                shape((narrow * narrow // 2, 2 * pair)),
            ),
            (pl.BlockSpec((i_blk * narrow, seqs), lambda n, *_: (n, 0)), shape((wide, seqs))),
            (whole((cols, 128)), shape((cols, 128), F32)),
        ]
        + [(whole((piece_rows, c_wide)), shape((piece_rows, c_wide)))] * pieces,
        [
            pltpu.VMEM((piece_rows * pieces, c_wide), F32),
            pltpu.VMEM(out_weight.shape, F32),
            pltpu.VMEM((seqs * i_blk, narrow), F32),
            pltpu.VMEM((rows, 128), F32),
        ],
        (own, me),
        (cov_t, cov_far, cot, out_weight, wl_t, normed),
        4e9,
        16e6,
    )


def forward(me, cov_t, left_t, right, scaled, w2, dcol, bias, pieces):
    rows, cols, pair = scaled.shape
    wide, seqs = left_t.shape
    narrow = wide // rows
    c_wide = cols * narrow
    i_blk = IBLK
    high = narrow * narrow // 2
    part = high // pieces

    def kernel(
        me_ref, cov_ref, lt_ref, r_ref, s_ref, w2_ref, dcol_ref, bias_ref, pu_ref, *rest
    ):
        outs = rest[:-3]
        acc, w2t, drow = rest[-3:]
        n = pl.program_id(0)

        @pl.when(n == 0)
        def _():
            acc[...] = jnp.zeros_like(acc)
            w2t[...] = w2_ref[...].astype(F32).T.astype(BF)
            drow[...] = depth_rows(cov_ref[...], 128)

        lane = lax.broadcasted_iota(jnp.int32, (pair, 2 * cols), 1)
        low = lane < cols
        dep = dcol_ref[...]
        mine_rows = drow[pl.ds(pl.multiple_of(n * i_blk, i_blk), i_blk), :]
        outer = dot(lt_ref[...], r_ref[...]).astype(BF)
        x = jnp.concatenate(
            [
                jnp.concatenate(
                    [
                        outer[
                            i * narrow : (i + 1) * narrow, dp * 2 * cols : (dp + 1) * 2 * cols
                        ]
                        for dp in range(narrow // 2)
                    ],
                    axis=0,
                )
                for i in range(i_blk)
            ],
            axis=1,
        )
        sbd = jnp.concatenate(
            [pair_block(s_ref[2 * k], s_ref[2 * k + 1]) for k in range(i_blk // 2)], axis=0
        )
        acc[...] += dot(x, sbd)
        pt = dot(w2t[...], x)
        for ip in range(i_blk // 2):
            at = ip * 4 * cols
            e0, o0 = pt[:pair, at : at + 2 * cols], pt[:pair, at + 2 * cols : at + 4 * cols]
            e1, o1 = pt[pair:, at : at + 2 * cols], pt[pair:, at + 2 * cols : at + 4 * cols]
            both = jnp.where(low, e0, o1) + pltpu.roll(jnp.where(low, o0, e1), cols, 1)
            both = both.T + bias_ref[...]
            for k in range(2):
                i = 2 * ip + k
                den = jnp.maximum(jnp.minimum(dep, mine_rows[i : i + 1, :]), 1.0)
                pu_ref[i] = (both[k * cols : (k + 1) * cols] / den).astype(BF)

        @pl.when(n == pl.num_programs(0) - 1)
        def _():
            send_pieces(me_ref[0], acc, outs)

    return call(
        kernel,
        "forward",
        (rows // i_blk,),
        [
            whole(cov_t.shape),
            pl.BlockSpec((i_blk * narrow, seqs), lambda n, *_: (n, 0)),
            whole(right.shape),
            pl.BlockSpec((i_blk, cols, pair), lambda n, *_: (n, 0, 0)),
            whole(w2.shape),
            whole(dcol.shape),
            whole((1, pair)),
        ],
        [
            (
                pl.BlockSpec((i_blk, cols, pair), lambda n, *_: (n, 0, 0)),
                shape((rows, cols, pair)),
            ),
            (whole((part, 2 * pair)), shape((part, 2 * pair), F32)),
        ]
        + [(whole((part, 2 * pair)), shape((part, 2 * pair)))] * (pieces - 1),
        [
            pltpu.VMEM((high, 2 * pair), F32),
            pltpu.VMEM((w2.shape[1], w2.shape[0]), BF),
            pltpu.VMEM((rows, 128), F32),
        ],
        (me,),
        (cov_t, left_t, right, scaled, w2, dcol, bias[None, :]),
        6e9,
        6e6,
    )


def left_side(sel, me, grad_outer, rights, pieces, piece_rows):
    wide, c_wide = grad_outer.shape
    seqs = rights[0].shape[0]
    chunk = 512

    def kernel(sel_ref, me_ref, g_ref, *rest):
        r_in = rest[: len(rights)]
        r_ref, outs, acc = rest[len(rights)], rest[len(rights) + 1 : -1], rest[-1]
        n = pl.program_id(0)

        @pl.when(n == 0)
        def _():
            acc[...] = jnp.zeros_like(acc)
            for t, r in enumerate(r_in):

                @pl.when(sel_ref[0] == t)
                def _():
                    pltpu.sync_copy(r, r_ref)

        at = pl.ds(pl.multiple_of(n * chunk, chunk), chunk)
        acc[0:seqs, at] = dot(g_ref[...], r_ref[...], NT).T

        @pl.when(n == pl.num_programs(0) - 1)
        def _():
            send_pieces(me_ref[0], acc, outs)

    return call(
        kernel,
        "grad_left_side",
        (wide // chunk,),
        [pl.BlockSpec((chunk, c_wide), lambda n, *_: (n, 0))]
        + [pl.BlockSpec(memory_space=pl.ANY)] * len(rights),
        [(whole((seqs, c_wide)), shape((seqs, c_wide)))]
        + [(whole((piece_rows, wide)), shape((piece_rows, wide)))] * pieces,
        [pltpu.VMEM((piece_rows * pieces, wide), F32)],
        (sel, me),
        (grad_outer, *rights),
        2e9,
        9e6,
    )


def tokens(me, cov_t, stat, lefts, rights, normed):
    seqs, rows, chans = normed.shape
    piece_rows, wide = lefts[0].shape
    narrow = wide // rows
    count = piece_rows * rows
    h = count // 2
    quad = 4 * rows
    last = seqs // piece_rows - 1
    per_half = (last + 1) // 2
    n_l, n_r = len(lefts), len(rights)
    nar2 = 2 * narrow

    def kernel(me_ref, cov_ref, stat_ref, n_ref, *rest):
        l_in = rest[:n_l]
        r_in = rest[n_l : n_l + n_r]
        out, z, t = rest[n_l + n_r :]
        plain = []
        base = (me_ref[0] * piece_rows).astype(F32)
        left = sum(ref[...].astype(F32) for ref in l_in)
        right = sum(ref[...].astype(F32) for ref in r_in)
        drow = depth_rows(cov_ref[...], 128)
        seq = lax.broadcasted_iota(jnp.int32, (piece_rows, narrow), 0).astype(F32) + base
        seq2 = lax.broadcasted_iota(jnp.int32, (piece_rows, 2 * rows), 0).astype(F32) + base
        on = seq2 < depth_lanes(cov_ref[...])
        for i in range(rows):
            v = jnp.where(
                seq < drow[i : i + 1, :narrow], left[:, i * narrow : (i + 1) * narrow], 0.0
            )
            z[pl.ds(i, piece_rows, stride=rows), 0:narrow] = v
        for dp in range(narrow // 2):
            v = jnp.where(on, right[:, dp * 2 * rows : (dp + 1) * 2 * rows], 0.0)
            t[pl.ds(2 * dp, piece_rows, stride=narrow), :] = v[:, :rows]
            t[pl.ds(2 * dp + 1, piece_rows, stride=narrow), :] = v[:, rows:]
        per = 128 // narrow
        for q in range(piece_rows // per):
            tr = t[q * 128 : (q + 1) * 128, :].T
            for k in range(per):
                s = q * per + k
                z[s * rows : (s + 1) * rows, narrow:nar2] = tr[:, k * narrow : (k + 1) * narrow]
        for b in range(piece_rows // 8):
            at = b * 2 * quad
            stats = stat_ref[0, b]
            pair_up, scaled = [], []
            for half in range(2):
                v = z[at + half * quad : at + (half + 1) * quad, :]
                inv = [
                    jnp.broadcast_to(stats[:, 4 * half + j : 4 * half + j + 1], (rows, nar2))
                    for j in range(4)
                ]
                pair_up.append(v)
                scaled.append(v * jnp.concatenate(inv, axis=0))
            out[b * quad : (b + 1) * quad, :] = jnp.concatenate(scaled, axis=1).astype(BF)
            plain.append(jnp.concatenate(pair_up, axis=1).astype(BF))
        v = jnp.concatenate(plain, axis=0)
        nb = n_ref[...].reshape(piece_rows // 8, 2, quad, chans)
        top = dot(v, nb[:, 0].reshape(h, chans), TN)
        bot = dot(v, nb[:, 1].reshape(h, chans), TN)
        grads = (top[:nar2] + bot[nar2:]).astype(BF)
        for k in range(chans // 128):
            out[h + k * nar2 : h + (k + 1) * nar2, :] = grads[:, k * 128 : (k + 1) * 128]

    return call(
        kernel,
        "tokens",
        (1,),
        [
            whole(cov_t.shape),
            pl.BlockSpec(
                (1, piece_rows // 8, rows, 128),
                lambda n, me: (
                    jnp.minimum(me[0], last) // per_half,
                    jnp.minimum(me[0], last) % per_half,
                    0,
                    0,
                ),
            ),
            pl.BlockSpec(
                (piece_rows, rows, chans), lambda n, me: (jnp.minimum(me[0], last), 0, 0)
            ),
        ]
        + [whole((piece_rows, wide))] * (n_l + n_r),
        [(whole((h + nar2 * chans // 128, 128)), shape((h + nar2 * chans // 128, 128)))],
        [pltpu.VMEM((count, nar2), F32), pltpu.VMEM((piece_rows * narrow, rows), F32)],
        (me,),
        (cov_t, stat, normed, *lefts, *rights),
        4e8,
        2e6,
    )[0]


def cut(me, parts, pieces):
    m, lanes = parts[0].shape

    def kernel(me_ref, *rest):
        ins, outs, acc = rest[: len(parts)], rest[len(parts) : -1], rest[-1]
        acc[...] = sum(ref[...].astype(F32) for ref in ins)
        send_pieces(me_ref[0], acc, outs)

    return call(
        kernel,
        "cut",
        (1,),
        [whole((m, lanes))] * len(parts),
        [(whole((m // pieces, lanes)), shape((m // pieces, lanes), F32))] * pieces,
        [pltpu.VMEM((m, lanes), F32)],
        (me,),
        tuple(parts),
        1e6,
        1e6,
    )


def finish(me, qs, alignment, wl_t, wr_t, gain, first, count, before=None):
    seqs, rows, chans = alignment.shape
    pieces = len(qs)
    quad = 4 * rows
    nar2 = 2 * wl_t.shape[0]
    blocks = (qs[0].shape[0] - nar2 * chans // 128) // quad
    every = count == seqs // (8 * blocks)
    given = () if before is None else (before,)

    def piece(n, me_ref):
        return n if every else me_ref[0] ^ (n + first)

    def kernel(me_ref, x_ref, wl_ref, wr_ref, gain_ref, *rest):
        q_in, (out, wc, q_now) = rest[:pieces], rest[-3:]
        n = pl.program_id(0)

        @pl.when(n == 0)
        def _():
            w = jnp.concatenate([wl_ref[...], wr_ref[...]], axis=0).astype(F32) * gain_ref[...]
            w = w - jnp.mean(w, axis=1, keepdims=True)
            hi = w.astype(BF)
            lo = (w - hi.astype(F32)).astype(BF)
            none = jnp.zeros_like(hi)
            wc[0] = jnp.concatenate([hi, none, lo, none], axis=0)
            wc[1] = jnp.concatenate([none, hi, none, lo], axis=0)

        t = piece(n, me_ref) ^ me_ref[0]
        for k in range(pieces):

            @pl.when(t == k)
            def _():
                q_now[...] = q_in[k][0 : blocks * quad, :]

        for b in range(blocks):
            q = q_now[b * quad : (b + 1) * quad, :]
            both = jnp.concatenate([q, q], axis=1)
            for half in range(2):
                g = dot(both, wc[half])
                for j in range(4):
                    s = half * 4 + j
                    xh = x_ref[8 * b + s].astype(F32)
                    gc = g[j * rows : (j + 1) * rows]
                    m = jnp.mean(gc * xh, axis=-1, keepdims=True)
                    out[8 * b + s] = (gc - xh * m).astype(BF)

    blk = pl.BlockSpec((8 * blocks, rows, chans), lambda n, me_ref: (piece(n, me_ref), 0, 0))
    return pl.pallas_call(
        kernel,
        name="finish",
        grid_spec=pltpu.PrefetchScalarGridSpec(
            num_scalar_prefetch=1,
            grid=(count,),
            in_specs=[
                blk,
                whole(wl_t.shape),
                whole(wr_t.shape),
                whole((1, chans)),
            ]
            + [whole(qs[0].shape)] * pieces
            + [pl.BlockSpec(memory_space=pl.ANY)] * len(given),
            out_specs=blk,
            scratch_shapes=[
                pltpu.VMEM((2, 4 * nar2, chans), BF),
                pltpu.VMEM((blocks * quad, 128), BF),
            ],
        ),
        out_shape=shape(alignment.shape),
        input_output_aliases={5 + pieces: 0} if given else {},
        compiler_params=params(),
        cost_estimate=pl.CostEstimate(flops=1000, bytes_accessed=1024, transcendentals=0),
    )(me, alignment, wl_t, wr_t, gain[None, :], *qs, *given)


def join_send(me, parts, qs, nar2):
    m, lanes = parts[0].shape
    n = len(parts)
    extra = nar2 * lanes // 128
    h = qs[0].shape[0] - extra

    def kernel(me_ref, *rest):
        ins, q_in, out, acc = rest[:n], rest[n:-2], rest[-2], rest[-1]
        for t in range(n):
            p = lax.rem(me_ref[0] - t + n, n)
            acc[rows_at(p, m), :] = ins[t][...]
        total = sum(q[...].astype(F32) for q in q_in)
        g = jnp.concatenate(
            [total[k * nar2 : (k + 1) * nar2] for k in range(lanes // 128)], axis=1
        )
        hi = g.astype(BF)
        out[0 : n * m, :] = acc[...].astype(BF)
        out[n * m : n * m + nar2, :] = hi
        out[n * m + nar2 :, :] = (g - hi.astype(F32)).astype(BF)

    total = n * m + 2 * nar2
    return call(
        kernel,
        "join_send",
        (1,),
        [whole((m, lanes))] * n
        + [pl.BlockSpec((extra, 128), lambda *_: (h // extra, 0))] * len(qs),
        [(whole((total, lanes)), shape((total, lanes)))],
        [pltpu.VMEM((n * m, lanes), F32)],
        (me,),
        (*parts, *qs),
        1e6,
        1e6,
    )[0]


def join_out(me, parts, nar2, narrow):
    rows, lanes = parts[0].shape
    n = len(parts)
    m = rows - 2 * nar2
    pair = lanes // 2
    dps = m // narrow

    def kernel(me_ref, *rest):
        ins, (out, lg, rg) = rest[:n], rest[n:]
        for t in range(n):
            p = lax.rem(me_ref[0] - t + n, n)
            v = ins[t][0:m, :].astype(F32)
            for k in range(dps):
                for d2 in range(2):
                    out[pl.ds(2 * (p * dps + k) + d2, narrow, stride=narrow), :] = v[
                        k * narrow : (k + 1) * narrow, d2 * pair : (d2 + 1) * pair
                    ]
        grads = sum(
            ref[m : m + nar2, :].astype(F32) + ref[m + nar2 :, :].astype(F32) for ref in ins
        )
        lg[...] = grads[:narrow]
        rg[...] = grads[narrow:]

    return call(
        kernel,
        "join_out",
        (1,),
        [whole((rows, lanes))] * n,
        [
            (whole((n * m * 2, pair)), shape((n * m * 2, pair), F32)),
            (whole((narrow, lanes)), shape((narrow, lanes), F32)),
            (whole((narrow, lanes)), shape((narrow, lanes), F32)),
        ],
        [],
        (me,),
        parts,
        1e6,
        1e6,
    )


BOTH = ("row", "col")


def shift(value, axis, t):
    n = lax.axis_size(axis)
    return lax.ppermute(value, axis, [(k, (k + t) % n) for k in range(n)])


def shifts(own, others, axis):
    return [own] + [shift(v, axis, t + 1) for t, v in enumerate(others)]


def swap(value, axis, t):
    n = lax.axis_size(axis)
    return lax.ppermute(value, axis, [(k, k ^ t) for k in range(n)])


def gather(value, axis):
    n = lax.axis_size(axis)
    if n == 4:
        near, far = swap(value, axis, 1), swap(value, axis, 2)
        return [value, near, far, swap(far, axis, 1)]
    return [value] + [swap(value, axis, t) for t in range(1, n)]


def spread_small(value, m, ratio):
    n_row, n_col = lax.axis_size("row"), lax.axis_size("col")
    total = None
    for first in range(1, n_row, n_col - 1):
        pairs = []
        for c in range(n_col):
            b = c * ratio + m
            for k, t in enumerate(range(first, min(first + n_col - 1, n_row))):
                pairs.append((b * n_col + (c + 1 + k) % n_col, (b + t) % n_row * n_col + c))
        got = lax.ppermute(value, BOTH, pairs)
        total = got if total is None else total + got
    return total


def spread(value, m, ratio):
    n_row, n_col = lax.axis_size("row"), lax.axis_size("col")
    out = [value]
    if n_row == 4 and n_col == 4:
        first = [(c * n_col + c, (c ^ 2) * n_col + c) for c in range(n_col)]
        first += [(c * n_col + (c ^ 1), (c ^ 1) * n_col + c) for c in range(n_col)]
        second = [(c * n_col + c, (c ^ 3) * n_col + c) for c in range(n_col)]
        return [value, lax.ppermute(value, BOTH, first), lax.ppermute(value, BOTH, second)]
    for t in range(1, n_row):
        pairs = [
            ((c * ratio + m) * n_col + c, (c * ratio + m + t) % n_row * n_col + c)
            for c in range(n_col)
        ]
        out.append(lax.ppermute(value, BOTH, pairs))
    return out


def spread_choice(row, col, m, ratio):
    n_row, n_col = lax.axis_size("row"), lax.axis_size("col")
    if n_row == 4 and n_col == 4:
        apart = row ^ col
        return jnp.where(apart == 3, 2, jnp.where(apart == 0, 0, 1))
    return (row - (col * ratio + m) + n_row) % n_row


def to_owners(pieces, ratio):
    n_row, n_col = lax.axis_size("row"), lax.axis_size("col")
    row = lax.axis_index("row")
    if ratio > 1:
        stacked = jnp.stack(pieces)
        pieces = [
            lax.dynamic_index_in_dim(stacked, (row + t) % n_row, 0, keepdims=False)
            for t in range(n_row)
        ]
    parts = []
    for t, piece in enumerate(pieces):
        pairs = []
        for r in range(n_row):
            m, k = divmod((r + t) % n_row, n_col)
            pairs += [(r * n_col + c, (c * ratio + m) * n_col + k) for c in range(n_col)]
        parts.append(lax.ppermute(piece, BOTH, pairs))
    return parts


def one(value):
    return value[None].astype(jnp.int32)


def body(
    alignment,
    coverage,
    layer_norm_gain,
    layer_norm_bias,
    left_weight,
    right_weight,
    out_weight,
    out_bias,
    cotangent,
):
    n_row, n_col = lax.axis_size("row"), lax.axis_size("col")
    ratio = n_row // n_col
    row_index = lax.axis_index("row")
    col_index = lax.axis_index("col")
    me_row, me_col = one(row_index), one(col_index)
    seqs, rows, chans = alignment.shape
    narrow = left_weight.shape[1]
    pair = out_weight.shape[1]
    piece_rows = (seqs // n_col + 7) // 8 * 8
    cov_t = coverage.T
    wl_t, wr_t = left_weight.T, right_weight.T

    cov_far = [spread_small(cov_t, m, ratio) for m in range(ratio)]
    normed, xhat, stat, right = project(cov_t, alignment, layer_norm_gain, layer_norm_bias, wr_t)
    right, cov_far = lax.optimization_barrier((right, cov_far))
    normed = normed.reshape(seqs, rows, chans)
    xhat = xhat.reshape(seqs, rows, chans)

    right_pieces, firsts = [], []
    for m in range(ratio):
        own = one(row_index == col_index * ratio + m)
        turn_by = one(row_index) if ratio == 1 else jnp.zeros_like(me_row)
        scaled, grad_outer, w2, left_t, dcol, *pieces = right_side(
            own,
            turn_by,
            cov_t,
            cov_far[m],
            cotangent,
            out_weight,
            wl_t,
            normed,
            m,
            n_col,
            piece_rows,
        )
        firsts.append((scaled, grad_outer, w2, left_t, dcol))
        right_pieces.extend(pieces)
    right_parts = to_owners(right_pieces, ratio)

    left_pieces, updates, weight_pieces = None, [], None
    for m in range(ratio):
        scaled, grad_outer, w2, left_t, dcol = firsts[m]
        sel = one(spread_choice(row_index, col_index, m, ratio))
        right_cols, *pieces = left_side(
            sel, me_col, grad_outer, spread(right, m, ratio), n_col, piece_rows
        )
        update, *gw = forward(
            me_row, cov_t, left_t, right_cols, scaled, w2, dcol, out_bias, n_row
        )
        updates.append(update)
        if m == 0:
            left_pieces, weight_pieces = pieces, gw
        else:
            left_pieces = [(a.astype(F32) + b).astype(BF) for a, b in zip(left_pieces, pieces)]
            weight_pieces = [
                (a.astype(F32) + b).astype(a.dtype) for a, b in zip(weight_pieces, gw)
            ]
    pair_update = updates[0] if ratio == 1 else jnp.concatenate(updates, axis=1)

    gw_parts = shifts(weight_pieces[0], weight_pieces[1:], "row")
    lefts = shifts(left_pieces[0], left_pieces[1:], "col")
    lefts, pair_update = lax.optimization_barrier((lefts, pair_update))
    q = tokens(me_col, cov_t, stat, lefts, right_parts, normed)
    qs = gather(q, "col")

    if weight_pieces[0].shape[0] % (8 * n_col) == 0:
        pieces = cut(me_col, gw_parts, n_col)
        part = sum(shifts(pieces[0], pieces[1:], "col"))
        parts = [part] + [shift(part, "col", t) for t in range(1, n_col)]
    else:
        parts = [lax.psum(cut(me_col, gw_parts, 1)[0], "col")]
    ends = (xhat, wl_t, wr_t, layer_norm_gain)
    if n_col == 4:
        gradient = finish(me_col, [qs[0], qs[1]], *ends, 0, 2)
        gradient, parts = lax.optimization_barrier((gradient, parts))
    last = join_send(me_col, parts, qs, 2 * narrow)
    lasts = [last] + [shift(last, "row", t) for t in range(1, n_row)]
    if n_col == 4:
        gradient = finish(me_col, qs, *ends, 2, 2, gradient)
    else:
        gradient = finish(me_col, qs, *ends, 0, seqs // piece_rows)
    lasts, gradient = lax.optimization_barrier((lasts, gradient))
    grad_out, grad_left, grad_right = join_out(me_row, lasts, 2 * narrow, narrow)
    return pair_update, gradient, grad_left.T, grad_right.T, grad_out


def solution(mesh):
    return jax.shard_map(
        body,
        mesh=mesh,
        in_specs=(
            P("grp", "row", None),
            P("grp", "row"),
            P(),
            P(),
            P(),
            P(),
            P(),
            P(),
            P(("grp", "row"), "col", None),
        ),
        out_specs=(
            P(("grp", "row"), "col", None),
            P("grp", "row", None),
            P("grp", None),
            P("grp", None),
            P("grp", None),
        ),
        check_vma=False,
    )
```

time: 435 us -> 106 us (0.24); the launches traced: 428 us -> 105 us
  waiting for transfers between devices: 203 us -> 15.3 us
  matrix products: 97.4 us -> 0 us
  local copies, waits for them, and re-layouts: 85.8 us -> 0 us
  Pallas kernels: 0 us -> 53.3 us
  starting transfers between devices: 0.25 us -> 34.7 us
  other arithmetic: 19.3 us -> 1.38 us
  between operations: 14.4 us -> 0.73 us
  blocking collectives: 8.12 us -> 0 us
    psum x5 -> x0, waiting for transfers between devices: 184 us -> none  [the longest x1 71.5 us: body(): grad_out = lax.psum(out_part, ('row', 'col'))]
    dot_general x13 -> x0, matrix products: 97.4 us -> none  [the longest x1 17.8 us: body(): jnp.einsum('ijcd,sic->sjd', grad_outer, left, preferred_element_type=jnp....]
    pallas_call x0 -> x10, Pallas kernels: none -> 53.3 us  [the longest x8 46.3 us: call(): pl.pallas_call(kernel, name=name, grid_spec=pltpu.PrefetchScalarGridSpec(...]
    convert_element_type x5 -> x0, local copies, waits for them, and re-layouts: 46.6 us -> none  [the longest x1 24.2 us: body(): outer = jnp.einsum('sic,sjd->ijcd', left, right_cols, preferred_element_t...]
    ppermute x0 -> x25, starting transfers between devices: none -> 34.7 us  [the longest x15 14.9 us: shift(): return lax.ppermute(value, axis, [(k, (k + t) % n) for k in range(n)])]
    reshape x1 -> x0, local copies, waits for them, and re-layouts: 24 us -> none  [body(): grad_outer = grad_outer.reshape(own_rows, col_rows, narrow, narrow)]
    all_gather x1 -> x0, waiting for transfers between devices: 18.2 us -> none  [body(): lax.all_gather(right, 'row', axis=1, tiled=True)]
    ppermute x0 -> x25, waiting for transfers between devices: none -> 15.3 us  [the longest x15 12 us: shift(): return lax.ppermute(value, axis, [(k, (k + t) % n) for k in range(n)])]
  transfers between devices with their start and end apart: 6 -> 25, of which waited for: 6 -> 11; matrix products, arithmetic and copies ran while one was open for 25% -> 1% of each run, Pallas kernels for 0% -> 35%
where the time goes in v2:
time: 106 us; the launch traced here: 105 us
  Pallas kernels  53.3 us (50%)
  starting transfers between devices  34.7 us (33%)
  waiting for transfers between devices  15.3 us (14%)
  other arithmetic  1.38 us (1%)
    pallas_call x8, Pallas kernels, call(): pl.pallas_call(kernel, name=name, grid_spec=pltpu.PrefetchScalarGridSpec(...  46.3 us
    ppermute x15, starting transfers between devices, shift(): return lax.ppermute(value, axis, [(k, (k + t) % n) for k in range(n)])  14.9 us
    ppermute x15, waiting for transfers between devices, shift(): return lax.ppermute(value, axis, [(k, (k + t) % n) for k in range(n)])  12 us
    ppermute x1, starting transfers between devices, spread(): lax.ppermute(value, BOTH, second)  9.56 us
    pallas_call x2, Pallas kernels, finish(): pl.pallas_call(kernel, name='finish', grid_spec=pltpu.PrefetchScalarGridS...  6.99 us
    ppermute x4, starting transfers between devices, to_owners(): parts.append(lax.ppermute(piece, BOTH, pairs))  5.43 us
    ppermute x3, waiting for transfers between devices, swap(): return lax.ppermute(value, axis, [(k, k ^ t) for k in range(n)])  3.35 us
  transfers between devices with their start and end apart: 25, of which 11 were waited for; matrix products, arithmetic and copies ran while one was open for 1% of the time, Pallas kernels for 35%

profile of v2, /device:TPU:0, one launch (start us, length us, event | category | flops | bytes accessed | tf_op | source)
XLA Modules:
  0.0 105.5 jit_solution(14582442832345016624)
XLA Ops:
  1.9 7.5 %project.1 = (bf16[2,48,64,256]{3,2,1,0:T(8,128)(2,1)}, bf16[2,48,64,256]{3,2,1,0:T(8,128)(2,1)}, f32[2,6,64,128]{3,2,1,0:T(8,128)}, bf16[96,2048]{1,0:T(8,128)(2,1)}) custom-call(s32[64,96]{1,0:T(8,128)} %bitcast.21, bf16[2,48,64,256]{3,2,1,0:T(8,128)(2,1)} %bitcast.19, f32[1,256]{1,0:T(1,128)} %bitcast.31, f32[1,256]{1,0:T(1,128)} %bitcast.34, ...), custom_call_target="tpu_custom_call" | custom-call | flops 2000 | bytes 1024 | tf_op jit(solution)/shard_map/project/pallas_call | solution.py:34
  9.4 9.6 %collective-permute-start.2 = (bf16[96,2048]{1,0:T(8,128)(2,1)}, bf16[96,2048]{1,0:T(8,128)(2,1)}, u32[]{:S(2)}, u32[]{:S(2)}) collective-permute-start(bf16[96,2048]{1,0:T(8,128)(2,1)} %get-tuple-element.56.rest_0_), channel_id=1, source_target_pairs={{0,12},{5,9},{10,6},{15,3},{16,28},{21,25},{26,22},{31,19}} | collective-permute-start | bytes 1179656 | tf_op jit(solution)/shard_map/ppermute | solution.py:750
  18.9 2.0 %collective-permute-start.1 = (bf16[96,2048]{1,0:T(8,128)(2,1)}, bf16[96,2048]{1,0:T(8,128)(2,1)}, u32[]{:S(2)}, u32[]{:S(2)}) collective-permute-start(bf16[96,2048]{1,0:T(8,128)(2,1)} %get-tuple-element.56.rest_0_), channel_id=1, source_target_pairs={{0,8},{5,13},{10,2},{15,7},{1,4},{4,1},{11,14},{14,11},{16,24},{21... | collective-permute-start | bytes 1179656 | tf_op jit(solution)/shard_map/ppermute | solution.py:750
  21.0 9.9 %grad_outer_right.1 = (bf16[64,64,128]{2,1,0:T(8,128)(2,1)}, bf16[2048,2048]{1,0:T(8,128)(2,1)}, bf16[512,256]{1,0:T(8,128)(2,1)}, bf16[2048,96]{1,0:T(8,128)(2,...) custom-call(s32[1]{0:T(128)} %bitcast.2.own_ref, ...), custom_call_target="tpu_custom_call" | custom-call | flops 4000 | bytes 1024 | tf_op jit(solution)/shard_map/grad_outer_right/pallas_call | solution.py:34
  30.9 7.8 %grad_left_side.1 = (bf16[96,2048]{1,0:T(8,128)(2,1)}, bf16[24,2048]{1,0:T(8,128)(2,1)}, bf16[24,2048]{1,0:T(8,128)(2,1)}, bf16[24,2048]{1,0:T(8,128)(2,1)}, bf16[24,2048]{1,0:T(8,128)(2,1)}) custom-call(s32[1]{0:T(128)} %bitcast.sel_ref, s32[1]{0:T(128)} %bitcast.1.me_ref, bf16[2048,2048]{1,0:T(8,128)(2,1)} %get-tuple-element.55.g_ref, ...), custom_call_target="tpu_custom_call" | custom-call | flops 2000 | bytes 1024 | tf_op jit(solution)/shard_map/grad_left_side/pallas_call | solution.py:34
  38.8 2.2 %collective-permute-start.6 = (bf16[24,2048]{1,0:T(8,128)(2,1)}, bf16[24,2048]{1,0:T(8,128)(2,1)}, u32[]{:S(2)}, u32[]{:S(2)}) collective-permute-start(bf16[24,2048]{1,0:T(8,128)(2,1)} %get-tuple-element.74), channel_id=1, source_target_pairs={{0,0},{1,4},{2,8},{3,12},{4,1},{5,5},{6,9},{7,13},{8,2},{9,6},{10,... | collective-permute-start | bytes 294920 | tf_op jit(solution)/shard_map/ppermute | solution.py:783
  41.0 4.2 %collective-permute-start.5 = (bf16[24,2048]{1,0:T(8,128)(2,1)}, bf16[24,2048]{1,0:T(8,128)(2,1)}, u32[]{:S(2)}, u32[]{:S(2)}) collective-permute-start(bf16[24,2048]{1,0:T(8,128)(2,1)} %get-tuple-element.60), channel_id=1, source_target_pairs={{0,3},{1,0},{2,1},{3,2},{4,7},{5,4},{6,5},{7,6},{8,11},{9,8},{10,9... | collective-permute-start | bytes 294920 | tf_op jit(solution)/shard_map/ppermute | solution.py:709
  45.6 2.5 %collective-permute-start.8 = (bf16[24,2048]{1,0:T(8,128)(2,1)}, bf16[24,2048]{1,0:T(8,128)(2,1)}, u32[]{:S(2)}, u32[]{:S(2)}) collective-permute-start(bf16[24,2048]{1,0:T(8,128)(2,1)} %get-tuple-element.76), channel_id=1, source_target_pairs={{0,2},{1,6},{2,10},{3,14},{4,3},{5,7},{6,11},{7,15},{8,0},{9,4},{1... | collective-permute-start | bytes 294920 | tf_op jit(solution)/shard_map/ppermute | solution.py:783
  49.4 11.4 %forward.1 = (bf16[64,64,128]{2,1,0:T(8,128)(2,1)}, f32[128,256]{1,0:T(8,128)}, bf16[128,256]{1,0:T(8,128)(2,1)}, bf16[128,256]{1,0:T(8,128)(2,1)}, bf16[128,256]{1,0:T(8,128)(2,1)}) custom-call(s32[1]{0:T(128)} %bitcast.3.me_ref, s32[64,96]{1,0:T(8,128)} %bitcast.23, bf16[2048,96]{1,0:T(8,128)(2,1)} %get-tuple-element.61.lt_ref, ...), custom_call_target="tpu_custom_call" | custom-call | flops 6000 | bytes 1024 | tf_op jit(solution)/shard_map/forward/pallas_call | solution.py:34
  60.8 4.3 %tokens.1.rest_0_.rest_4_ = bf16[896,128]{1,0:T(8,128)(2,1)} custom-call(s32[1]{0:T(128)} %bitcast.1.me_ref, s32[64,96]{1,0:T(8,128)} %bitcast.24, f32[2,6,64,128]{3,2,1,0:T(8,128)} %get-tuple-element.69.stat_ref, bf16[96,64,256]{2,1,0:T(8,128)(2,1)} %bitcast.16, bf16[24,2048]{1,0:T(8,128)(2,1)} %get-tuple-element.70.rest_0_, ...), custom_call_target="tpu_custom_call" | custom-call | flops 400 | bytes 1024 | tf_op jit(solution)/shard_map/tokens/pallas_call | solution.py:34
  65.1 1.5 %collective-permute-start.20 = (bf16[896,128]{1,0:T(8,128)(2,1)}, bf16[896,128]{1,0:T(8,128)(2,1)}, u32[]{:S(2)}, u32[]{:S(2)}) collective-permute-start(bf16[896,128]{1,0:T(8,128)(2,1)} %tokens.1.rest_0_.rest_4_), channel_id=1, source_target_pairs={{0,2},{1,3},{2,0},{3,1},{4,6},{5,7},{6,4},{7,5},{8,10},{9,11},{10,... | collective-permute-start | bytes 688136 | tf_op jit(solution)/shard_map/ppermute | solution.py:718
  67.1 1.4 %collective-permute-start.13 = (bf16[128,256]{1,0:T(8,128)(2,1)}, bf16[128,256]{1,0:T(8,128)(2,1)}, u32[]{:S(2)}, u32[]{:S(2)}) collective-permute-start(bf16[128,256]{1,0:T(8,128)(2,1)} %get-tuple-element.81), channel_id=1, source_target_pairs={{0,12},{4,0},{8,4},{12,8},{1,13},{5,1},{9,5},{13,9},{2,14},{6,2},{... | collective-permute-start | bytes 196616 | tf_op jit(solution)/shard_map/ppermute | solution.py:709
  68.5 2.2 %collective-permute-done.11.rest_1_ = bf16[128,256]{1,0:T(8,128)(2,1)} collective-permute-done((bf16[128,256]{1,0:T(8,128)(2,1)}, bf16[128,256]{1,0:T(8,128)(2,1)}, u32[]{:S(2)}, u32[]{:S(2)}) %collective-permute-start.11) | collective-permute-done | bytes 65568 | tf_op jit(solution)/shard_map/ppermute | solution.py:709
  71.8 1.7 %cut.1 = (f32[32,256]{1,0:T(8,128)}, f32[32,256]{1,0:T(8,128)}, f32[32,256]{1,0:T(8,128)}, f32[32,256]{1,0:T(8,128)}) custom-call(s32[1]{0:T(128)} %bitcast.1.me_ref, f32[128,256]{1,0:T(8,128)} %get-tuple-element.78.rest_0_, bf16[128,256]{1,0:T(8,128)(2,1)} %collective-permute-done.11.rest_1_, bf16[128,256]{1,0:T(8,128)(2,1)} %collective-permute-done.12.rest_2_, ...), custom_call_target="tpu_custom_call" | custom-call | flops 1 | bytes 1024 | tf_op jit(solution)/shard_map/cut/pallas_call | solution.py:34
  73.8 2.0 %collective-permute-start.15 = (f32[32,256]{1,0:T(8,128)}, f32[32,256]{1,0:T(8,128)S(1)}, u32[]{:S(2)}, u32[]{:S(2)}) collective-permute-start(f32[32,256]{1,0:T(8,128)} %get-tuple-element.84), channel_id=1, source_target_pairs={{0,2},{1,3},{2,0},{3,1},{4,6},{5,7},{6,4},{7,5},{8,10},{9,11},{10,... | collective-permute-start | bytes 98312 | tf_op jit(solution)/shard_map/ppermute | solution.py:709
  75.8 2.1 %collective-permute-start.16 = (f32[32,256]{1,0:T(8,128)}, f32[32,256]{1,0:T(8,128)S(1)}, u32[]{:S(2)}, u32[]{:S(2)}) collective-permute-start(f32[32,256]{1,0:T(8,128)} %get-tuple-element.85), channel_id=1, source_target_pairs={{0,3},{1,0},{2,1},{3,2},{4,7},{5,4},{6,5},{7,6},{8,11},{9,8},{10,9... | collective-permute-start | bytes 98312 | tf_op jit(solution)/shard_map/ppermute | solution.py:709
  77.9 2.7 %collective-permute-done.20.rest_6_.rest_2_ = bf16[896,128]{1,0:T(8,128)(2,1)} collective-permute-done((bf16[896,128]{1,0:T(8,128)(2,1)}, bf16[896,128]{1,0:T(8,128)(2,1)}, u32[]{:S(2)}, u32[]{:S(2)}) %collective-permute-start.20) | collective-permute-done | bytes 229408 | tf_op jit(solution)/shard_map/ppermute | solution.py:718
  82.6 2.8 %collective-permute-start.19 = (f32[32,256]{1,0:T(8,128)}, f32[32,256]{1,0:T(8,128)}, u32[]{:S(2)}, u32[]{:S(2)}) collective-permute-start(f32[32,256]{1,0:T(8,128)} %add_add_fusion.rest_0_), channel_id=1, source_target_pairs={{0,3},{1,0},{2,1},{3,2},{4,7},{5,4},{6,5},{7,6},{8,11},{9,8},{10,9... | collective-permute-start | bytes 98312 | tf_op jit(solution)/shard_map/ppermute | solution.py:709
  86.6 3.4 %finish.2.rest_4_ = bf16[96,64,256]{2,1,0:T(8,128)(2,1)} custom-call(s32[1]{0:T(128)} %bitcast.1.me_ref, bf16[96,64,256]{2,1,0:T(8,128)(2,1)} %bitcast.17, bf16[32,256]{1,0:T(8,128)(2,1)} %bitcast.26, bf16[32,256]{1,0:T(8,128)(2,1)} %bitcast.29, f32[1,256]{1,0:T(1,128)} %bitcast.32, bf16[896,128]{1,0:T(8,128)(2,1)} %tokens.1.rest_0_.rest_4_, ...), custom_call_target="tpu_custom_call" | custom-call | flops 1000 | bytes 1024 | tf_op jit(solution)/shard_map/finish/pallas_call | solution.py:600
  90.0 2.7 %collective-permute-done.19.rest_3_ = f32[32,256]{1,0:T(8,128)} collective-permute-done((f32[32,256]{1,0:T(8,128)}, f32[32,256]{1,0:T(8,128)}, u32[]{:S(2)}, u32[]{:S(2)}) %collective-permute-start.19) | collective-permute-done | bytes 32800 | tf_op jit(solution)/shard_map/ppermute | solution.py:709
  93.4 1.6 %join_send.1.rest_0_ = bf16[256,256]{1,0:T(8,128)(2,1)} custom-call(s32[1]{0:T(128)} %bitcast.1.me_ref, f32[32,256]{1,0:T(8,128)} %add_add_fusion.rest_0_, f32[32,256]{1,0:T(8,128)} %collective-permute-done.17.rest_1_, f32[32,256]{1,0:T(8,128)} %collective-permute-done.18.rest_2_, f32[32,256]{1,0:T(8,128)} %collective-permute-done.19.rest_3_, ...), custom_call_target="tpu_custom_call" | custom-call | flops 1 | bytes 1024 | tf_op jit(solution)/shard_map/join_send/pallas_call | solution.py:34
  96.0 3.6 %finish.3 = bf16[96,64,256]{2,1,0:T(8,128)(2,1)} custom-call(s32[1]{0:T(128)} %bitcast.1.me_ref, bf16[96,64,256]{2,1,0:T(8,128)(2,1)} %bitcast.18, bf16[32,256]{1,0:T(8,128)(2,1)} %bitcast.27, bf16[32,256]{1,0:T(8,128)(2,1)} %bitcast.30, f32[1,256]{1,0:T(1,128)} %bitcast.33, bf16[896,128]{1,0:T(8,128)(2,1)} %tokens.1.rest_0_.rest_4_, ...), custom_call_target="tpu_custom_call", output_to_operand_aliasing={{}: (9, {})} | custom-call | flops 1000 | bytes 1024 | tf_op jit(solution)/shard_map/finish/pallas_call | solution.py:600
  99.6 2.9 %collective-permute-done.23.rest_2_ = bf16[256,256]{1,0:T(8,128)(2,1)} collective-permute-done((bf16[256,256]{1,0:T(8,128)(2,1)}, bf16[256,256]{1,0:T(8,128)(2,1)}, u32[]{:S(2)}, u32[]{:S(2)}) %collective-permute-start.23) | collective-permute-done | bytes 131104 | tf_op jit(solution)/shard_map/ppermute | solution.py:709
  103.3 2.2 %join_out.1 = (f32[1024,128]{1,0:T(8,128)}, f32[32,256]{1,0:T(8,128)}, f32[32,256]{1,0:T(8,128)}) custom-call(s32[1]{0:T(128)} %bitcast.3.me_ref, bf16[256,256]{1,0:T(8,128)(2,1)} %join_send.1.rest_0_, bf16[256,256]{1,0:T(8,128)(2,1)} %collective-permute-done.22.rest_1_, bf16[256,256]{1,0:T(8,128)(2,1)} %collective-permute-done.23.rest_2_, ...), custom_call_target="tpu_custom_call" | custom-call | flops 1 | bytes 1024 | tf_op jit(solution)/shard_map/join_out/pallas_call | solution.py:34
  (37 shorter events, 10.7 us)
Async XLA Ops:
  0.6 8.7 %collective-permute-start = (s32[64,96]{1,0:T(8,128)}, s32[64,96]{1,0:T(8,128)}, u32[]{:S(2)}, u32[]{:S(2)}) collective-permute-start(s32[64,96]{1,0:T(8,128)} %bitcast.20), channel_id=1, source_target_pairs={{1,4},{2,8},{3,12},{6,9},{7,13},{4,1},{11,14},{8,2},{9,6},{12,3},{... | collective-permute-start | bytes 73736 | tf_op jit(solution)/shard_map/ppermute | solution.py:738
  9.4 21.5 %collective-permute-start.2 = (bf16[96,2048]{1,0:T(8,128)(2,1)}, bf16[96,2048]{1,0:T(8,128)(2,1)}, u32[]{:S(2)}, u32[]{:S(2)}) collective-permute-start(bf16[96,2048]{1,0:T(8,128)(2,1)} %get-tuple-element.56.rest_0_), channel_id=1, source_target_pairs={{0,12},{5,9},{10,6},{15,3},{16,28},{21,25},{26,22},{31,19}} | collective-permute-start | bytes 1179656 | tf_op jit(solution)/shard_map/ppermute | solution.py:750
  18.9 12.0 %collective-permute-start.1 = (bf16[96,2048]{1,0:T(8,128)(2,1)}, bf16[96,2048]{1,0:T(8,128)(2,1)}, u32[]{:S(2)}, u32[]{:S(2)}) collective-permute-start(bf16[96,2048]{1,0:T(8,128)(2,1)} %get-tuple-element.56.rest_0_), channel_id=1, source_target_pairs={{0,8},{5,13},{10,2},{15,7},{1,4},{4,1},{11,14},{14,11},{16,24},{21... | collective-permute-start | bytes 1179656 | tf_op jit(solution)/shard_map/ppermute | solution.py:750
  38.8 6.8 %collective-permute-start.3 = (bf16[24,2048]{1,0:T(8,128)(2,1)}, bf16[24,2048]{1,0:T(8,128)(2,1)}, u32[]{:S(2)}, u32[]{:S(2)}) collective-permute-start(bf16[24,2048]{1,0:T(8,128)(2,1)} %get-tuple-element.58), channel_id=1, source_target_pairs={{0,1},{1,2},{2,3},{3,0},{4,5},{5,6},{6,7},{7,4},{8,9},{9,10},{10,1... | collective-permute-start | bytes 294920 | tf_op jit(solution)/shard_map/ppermute | solution.py:709
  38.8 9.8 %collective-permute-start.4 = (bf16[24,2048]{1,0:T(8,128)(2,1)}, bf16[24,2048]{1,0:T(8,128)(2,1)}, u32[]{:S(2)}, u32[]{:S(2)}) collective-permute-start(bf16[24,2048]{1,0:T(8,128)(2,1)} %get-tuple-element.59), channel_id=1, source_target_pairs={{0,2},{1,3},{2,0},{3,1},{4,6},{5,7},{6,4},{7,5},{8,10},{9,11},{10,... | collective-permute-start | bytes 294920 | tf_op jit(solution)/shard_map/ppermute | solution.py:709
  38.8 22.0 %collective-permute-start.6 = (bf16[24,2048]{1,0:T(8,128)(2,1)}, bf16[24,2048]{1,0:T(8,128)(2,1)}, u32[]{:S(2)}, u32[]{:S(2)}) collective-permute-start(bf16[24,2048]{1,0:T(8,128)(2,1)} %get-tuple-element.74), channel_id=1, source_target_pairs={{0,0},{1,4},{2,8},{3,12},{4,1},{5,5},{6,9},{7,13},{8,2},{9,6},{10,... | collective-permute-start | bytes 294920 | tf_op jit(solution)/shard_map/ppermute | solution.py:783
  41.0 19.8 %collective-permute-start.5 = (bf16[24,2048]{1,0:T(8,128)(2,1)}, bf16[24,2048]{1,0:T(8,128)(2,1)}, u32[]{:S(2)}, u32[]{:S(2)}) collective-permute-start(bf16[24,2048]{1,0:T(8,128)(2,1)} %get-tuple-element.60), channel_id=1, source_target_pairs={{0,3},{1,0},{2,1},{3,2},{4,7},{5,4},{6,5},{7,6},{8,11},{9,8},{10,9... | collective-permute-start | bytes 294920 | tf_op jit(solution)/shard_map/ppermute | solution.py:709
  45.1 15.6 %collective-permute-start.7 = (bf16[24,2048]{1,0:T(8,128)(2,1)}, bf16[24,2048]{1,0:T(8,128)(2,1)}, u32[]{:S(2)}, u32[]{:S(2)}) collective-permute-start(bf16[24,2048]{1,0:T(8,128)(2,1)} %get-tuple-element.75), channel_id=1, source_target_pairs={{0,1},{1,5},{2,9},{3,13},{4,2},{5,6},{6,10},{7,14},{8,3},{9,7},{10... | collective-permute-start | bytes 294920 | tf_op jit(solution)/shard_map/ppermute | solution.py:783
  45.6 15.2 %collective-permute-start.8 = (bf16[24,2048]{1,0:T(8,128)(2,1)}, bf16[24,2048]{1,0:T(8,128)(2,1)}, u32[]{:S(2)}, u32[]{:S(2)}) collective-permute-start(bf16[24,2048]{1,0:T(8,128)(2,1)} %get-tuple-element.76), channel_id=1, source_target_pairs={{0,2},{1,6},{2,10},{3,14},{4,3},{5,7},{6,11},{7,15},{8,0},{9,4},{1... | collective-permute-start | bytes 294920 | tf_op jit(solution)/shard_map/ppermute | solution.py:783
  48.6 12.2 %collective-permute-start.9 = (bf16[24,2048]{1,0:T(8,128)(2,1)}, bf16[24,2048]{1,0:T(8,128)(2,1)}, u32[]{:S(2)}, u32[]{:S(2)}) collective-permute-start(bf16[24,2048]{1,0:T(8,128)(2,1)} %get-tuple-element.77), channel_id=1, source_target_pairs={{0,3},{1,7},{2,11},{3,15},{4,0},{5,4},{6,8},{7,12},{8,1},{9,5},{10... | collective-permute-start | bytes 294920 | tf_op jit(solution)/shard_map/ppermute | solution.py:783
  65.1 15.6 %collective-permute-start.20 = (bf16[896,128]{1,0:T(8,128)(2,1)}, bf16[896,128]{1,0:T(8,128)(2,1)}, u32[]{:S(2)}, u32[]{:S(2)}) collective-permute-start(bf16[896,128]{1,0:T(8,128)(2,1)} %tokens.1.rest_0_.rest_4_), channel_id=1, source_target_pairs={{0,2},{1,3},{2,0},{3,1},{4,6},{5,7},{6,4},{7,5},{8,10},{9,11},{10,... | collective-permute-start | bytes 688136 | tf_op jit(solution)/shard_map/ppermute | solution.py:718
  66.6 5.3 %collective-permute-start.12 = (bf16[128,256]{1,0:T(8,128)(2,1)}, bf16[128,256]{1,0:T(8,128)(2,1)}, u32[]{:S(2)}, u32[]{:S(2)}) collective-permute-start(bf16[128,256]{1,0:T(8,128)(2,1)} %get-tuple-element.80), channel_id=1, source_target_pairs={{0,8},{4,12},{8,0},{12,4},{1,9},{5,13},{9,1},{13,5},{2,10},{6,14},... | collective-permute-start | bytes 196616 | tf_op jit(solution)/shard_map/ppermute | solution.py:709
  67.1 4.8 %collective-permute-start.13 = (bf16[128,256]{1,0:T(8,128)(2,1)}, bf16[128,256]{1,0:T(8,128)(2,1)}, u32[]{:S(2)}, u32[]{:S(2)}) collective-permute-start(bf16[128,256]{1,0:T(8,128)(2,1)} %get-tuple-element.81), channel_id=1, source_target_pairs={{0,12},{4,0},{8,4},{12,8},{1,13},{5,1},{9,5},{13,9},{2,14},{6,2},{... | collective-permute-start | bytes 196616 | tf_op jit(solution)/shard_map/ppermute | solution.py:709
  73.5 7.2 %collective-permute-start.14 = (f32[32,256]{1,0:T(8,128)}, f32[32,256]{1,0:T(8,128)S(1)}, u32[]{:S(2)}, u32[]{:S(2)}) collective-permute-start(f32[32,256]{1,0:T(8,128)} %get-tuple-element.83), channel_id=1, source_target_pairs={{0,1},{1,2},{2,3},{3,0},{4,5},{5,6},{6,7},{7,4},{8,9},{9,10},{10,1... | collective-permute-start | bytes 98312 | tf_op jit(solution)/shard_map/ppermute | solution.py:709
  73.8 7.5 %collective-permute-start.15 = (f32[32,256]{1,0:T(8,128)}, f32[32,256]{1,0:T(8,128)S(1)}, u32[]{:S(2)}, u32[]{:S(2)}) collective-permute-start(f32[32,256]{1,0:T(8,128)} %get-tuple-element.84), channel_id=1, source_target_pairs={{0,2},{1,3},{2,0},{3,1},{4,6},{5,7},{6,4},{7,5},{8,10},{9,11},{10,... | collective-permute-start | bytes 98312 | tf_op jit(solution)/shard_map/ppermute | solution.py:709
  75.8 5.5 %collective-permute-start.16 = (f32[32,256]{1,0:T(8,128)}, f32[32,256]{1,0:T(8,128)S(1)}, u32[]{:S(2)}, u32[]{:S(2)}) collective-permute-start(f32[32,256]{1,0:T(8,128)} %get-tuple-element.85), channel_id=1, source_target_pairs={{0,3},{1,0},{2,1},{3,2},{4,7},{5,4},{6,5},{7,6},{8,11},{9,8},{10,9... | collective-permute-start | bytes 98312 | tf_op jit(solution)/shard_map/ppermute | solution.py:709
  77.8 8.8 %collective-permute-start.10 = (bf16[896,128]{1,0:T(8,128)(2,1)}, bf16[896,128]{1,0:T(8,128)(2,1)}, u32[]{:S(2)}, u32[]{:S(2)}) collective-permute-start(bf16[896,128]{1,0:T(8,128)(2,1)} %tokens.1.rest_0_.rest_4_), channel_id=1, source_target_pairs={{0,1},{1,0},{2,3},{3,2},{4,5},{5,4},{6,7},{7,6},{8,9},{9,8},{10,11... | collective-permute-start | bytes 688136 | tf_op jit(solution)/shard_map/ppermute | solution.py:718
  80.6 12.8 %collective-permute-start.21 = (bf16[896,128]{1,0:T(8,128)(2,1)}, bf16[896,128]{1,0:T(8,128)(2,1)}, u32[]{:S(2)}, u32[]{:S(2)}) collective-permute-start(bf16[896,128]{1,0:T(8,128)(2,1)} %collective-permute-done.20.rest_6_.rest_2_), channel_id=1, source_target_pairs={{0,1},{1,0},{2,3},{3,2},{4,5},{5,4},{6,7},{7,6},{8,9},{9,8},{10,11... | collective-permute-start | bytes 688136 | tf_op jit(solution)/shard_map/ppermute | solution.py:718
  82.6 10.1 %collective-permute-start.19 = (f32[32,256]{1,0:T(8,128)}, f32[32,256]{1,0:T(8,128)}, u32[]{:S(2)}, u32[]{:S(2)}) collective-permute-start(f32[32,256]{1,0:T(8,128)} %add_add_fusion.rest_0_), channel_id=1, source_target_pairs={{0,3},{1,0},{2,1},{3,2},{4,7},{5,4},{6,5},{7,6},{8,11},{9,8},{10,9... | collective-permute-start | bytes 98312 | tf_op jit(solution)/shard_map/ppermute | solution.py:709
  85.4 7.3 %collective-permute-start.18 = (f32[32,256]{1,0:T(8,128)}, f32[32,256]{1,0:T(8,128)}, u32[]{:S(2)}, u32[]{:S(2)}) collective-permute-start(f32[32,256]{1,0:T(8,128)} %add_add_fusion.rest_0_), channel_id=1, source_target_pairs={{0,2},{1,3},{2,0},{3,1},{4,6},{5,7},{6,4},{7,5},{8,10},{9,11},{10,... | collective-permute-start | bytes 98312 | tf_op jit(solution)/shard_map/ppermute | solution.py:709
  85.5 7.9 %collective-permute-start.17 = (f32[32,256]{1,0:T(8,128)}, f32[32,256]{1,0:T(8,128)}, u32[]{:S(2)}, u32[]{:S(2)}) collective-permute-start(f32[32,256]{1,0:T(8,128)} %add_add_fusion.rest_0_), channel_id=1, source_target_pairs={{0,1},{1,2},{2,3},{3,0},{4,5},{5,6},{6,7},{7,4},{8,9},{9,10},{10,1... | collective-permute-start | bytes 98312 | tf_op jit(solution)/shard_map/ppermute | solution.py:709
  95.0 4.6 %collective-permute-start.24 = (bf16[256,256]{1,0:T(8,128)(2,1)}, bf16[256,256]{1,0:T(8,128)(2,1)}, u32[]{:S(2)}, u32[]{:S(2)}) collective-permute-start(bf16[256,256]{1,0:T(8,128)(2,1)} %join_send.1.rest_0_), channel_id=1, source_target_pairs={{0,12},{4,0},{8,4},{12,8},{1,13},{5,1},{9,5},{13,9},{2,14},{6,2},{... | collective-permute-start | bytes 393224 | tf_op jit(solution)/shard_map/ppermute | solution.py:709
  95.0 7.5 %collective-permute-start.23 = (bf16[256,256]{1,0:T(8,128)(2,1)}, bf16[256,256]{1,0:T(8,128)(2,1)}, u32[]{:S(2)}, u32[]{:S(2)}) collective-permute-start(bf16[256,256]{1,0:T(8,128)(2,1)} %join_send.1.rest_0_), channel_id=1, source_target_pairs={{0,8},{4,12},{8,0},{12,4},{1,9},{5,13},{9,1},{13,5},{2,10},{6,14},... | collective-permute-start | bytes 393224 | tf_op jit(solution)/shard_map/ppermute | solution.py:709
  95.8 7.5 %collective-permute-start.22 = (bf16[256,256]{1,0:T(8,128)(2,1)}, bf16[256,256]{1,0:T(8,128)(2,1)}, u32[]{:S(2)}, u32[]{:S(2)}) collective-permute-start(bf16[256,256]{1,0:T(8,128)(2,1)} %join_send.1.rest_0_), channel_id=1, source_target_pairs={{0,4},{4,8},{8,12},{12,0},{1,5},{5,9},{9,13},{13,1},{2,6},{6,10},{... | collective-permute-start | bytes 393224 | tf_op jit(solution)/shard_map/ppermute | solution.py:709
  (1 other events, 4.2 us)

commit v3 on v2

--- a/solution.py
+++ b/solution.py
@@ -11,11 +11,12 @@
 NT = (((1,), (1,)), ((), ()))
 TN = (((0,), (0,)), ((), ()))
 VMEM = 64 * 1024 * 1024
+COST = {'grad_outer_right': 4, 'grad_left_side': 4, 'cut': 20, 'finish_a': 0.5, 'finish_b': 0.2, 'join_send': 2, 'project': 1}
 IBLK = 8
 
 
-def params():
-    return pltpu.CompilerParams(vmem_limit_bytes=VMEM)
+def params(vmem=VMEM):
+    return pltpu.CompilerParams(vmem_limit_bytes=vmem)
 
 
 def dot(a, b, dims=NN):
@@ -30,7 +31,25 @@
     return jax.ShapeDtypeStruct(dims, dtype)
 
 
-def call(kernel, name, grid, ins, outs, scratch, scalars, arrays, flops, bytes_accessed):
+def far(*values):
+    return tuple(pltpu.with_memory_space_constraint(v, pltpu.HBM) for v in values)
+
+
+def near(*values):
+    return tuple(pltpu.with_memory_space_constraint(v, pltpu.VMEM) for v in values)
+
+
+def sent(dims, dtype=BF):
+    return pltpu.HBM(dims, dtype)
+
+
+def kept(dims, dtype=BF):
+    return pltpu.VMEM(dims, dtype)
+
+
+def call(
+    kernel, name, grid, ins, outs, scratch, scalars, arrays, flops, bytes_accessed, vmem=VMEM
+):
     return pl.pallas_call(
         kernel,
         name=name,
@@ -42,9 +61,9 @@
             scratch_shapes=scratch,
         ),
         out_shape=[o[1] for o in outs],
-        compiler_params=params(),
+        compiler_params=params(vmem),
         cost_estimate=pl.CostEstimate(
-            flops=int(flops) // 10**6, bytes_accessed=1024, transcendentals=0
+            flops=int(COST.get(name, 0) * 1e9), bytes_accessed=1024, transcendentals=0
         ),
     )(*scalars, *arrays)
 
@@ -278,17 +297,17 @@
         [
             (
                 pl.BlockSpec((i_blk, cols, pair), lambda n, *_: (n, 0, 0)),
-                shape((rows, cols, pair)),
+                kept((rows, cols, pair)),
             ),
-            (pl.BlockSpec((i_blk * narrow, c_wide), lambda n, *_: (n, 0)), shape((wide, c_wide))),
+            (pl.BlockSpec((i_blk * narrow, c_wide), lambda n, *_: (n, 0)), kept((wide, c_wide))),
             (
                 whole((narrow * narrow // 2, 2 * pair)),
-                shape((narrow * narrow // 2, 2 * pair)),
+                kept((narrow * narrow // 2, 2 * pair)),
             ),
-            (pl.BlockSpec((i_blk * narrow, seqs), lambda n, *_: (n, 0)), shape((wide, seqs))),
-            (whole((cols, 128)), shape((cols, 128), F32)),
+            (pl.BlockSpec((i_blk * narrow, seqs), lambda n, *_: (n, 0)), kept((wide, seqs))),
+            (whole((cols, 128)), kept((cols, 128), F32)),
         ]
-        + [(whole((piece_rows, c_wide)), shape((piece_rows, c_wide)))] * pieces,
+        + [(whole((piece_rows, c_wide)), sent((piece_rows, c_wide)))] * pieces,
         [
             pltpu.VMEM((piece_rows * pieces, c_wide), F32),
             pltpu.VMEM(out_weight.shape, F32),
@@ -296,9 +315,10 @@
             pltpu.VMEM((rows, 128), F32),
         ],
         (own, me),
-        (cov_t, cov_far, cot, out_weight, wl_t, normed),
+        far(cov_t, cov_far, cot, out_weight, wl_t, normed),
         4e9,
         16e6,
+        VMEM // 2,
     )
 
 
@@ -380,20 +400,21 @@
         [
             (
                 pl.BlockSpec((i_blk, cols, pair), lambda n, *_: (n, 0, 0)),
-                shape((rows, cols, pair)),
+                sent((rows, cols, pair)),
             ),
-            (whole((part, 2 * pair)), shape((part, 2 * pair), F32)),
+            (whole((part, 2 * pair)), sent((part, 2 * pair), F32)),
         ]
-        + [(whole((part, 2 * pair)), shape((part, 2 * pair)))] * (pieces - 1),
+        + [(whole((part, 2 * pair)), sent((part, 2 * pair)))] * (pieces - 1),
         [
             pltpu.VMEM((high, 2 * pair), F32),
             pltpu.VMEM((w2.shape[1], w2.shape[0]), BF),
             pltpu.VMEM((rows, 128), F32),
         ],
         (me,),
-        (cov_t, left_t, right, scaled, w2, dcol, bias[None, :]),
+        (*far(cov_t), *near(left_t, right, scaled, w2, dcol), *far(bias[None, :])),
         6e9,
         6e6,
+        VMEM // 2,
     )
 
 
@@ -429,13 +450,14 @@
         (wide // chunk,),
         [pl.BlockSpec((chunk, c_wide), lambda n, *_: (n, 0))]
         + [pl.BlockSpec(memory_space=pl.ANY)] * len(rights),
-        [(whole((seqs, c_wide)), shape((seqs, c_wide)))]
-        + [(whole((piece_rows, wide)), shape((piece_rows, wide)))] * pieces,
+        [(whole((seqs, c_wide)), kept((seqs, c_wide)))]
+        + [(whole((piece_rows, wide)), sent((piece_rows, wide)))] * pieces,
         [pltpu.VMEM((piece_rows * pieces, wide), F32)],
         (sel, me),
-        (grad_outer, *rights),
+        (*near(grad_outer), *rights),
         2e9,
         9e6,
+        VMEM // 2,
     )
 
 
@@ -620,7 +642,11 @@
         out_shape=shape(alignment.shape),
         input_output_aliases={5 + pieces: 0} if given else {},
         compiler_params=params(),
-        cost_estimate=pl.CostEstimate(flops=1000, bytes_accessed=1024, transcendentals=0),
+        cost_estimate=pl.CostEstimate(
+            flops=int(COST.get("finish_a" if before is None else "finish_b", 0) * 1e9),
+            bytes_accessed=1024,
+            transcendentals=0,
+        ),
     )(me, alignment, wl_t, wr_t, gain[None, :], *qs, *given)
 
 
@@ -639,12 +665,10 @@
         g = jnp.concatenate(
             [total[k * nar2 : (k + 1) * nar2] for k in range(lanes // 128)], axis=1
         )
-        hi = g.astype(BF)
         out[0 : n * m, :] = acc[...].astype(BF)
-        out[n * m : n * m + nar2, :] = hi
-        out[n * m + nar2 :, :] = (g - hi.astype(F32)).astype(BF)
-
-    total = n * m + 2 * nar2
+        out[n * m :, :] = g.astype(BF)
+
+    total = n * m + nar2
     return call(
         kernel,
         "join_send",
@@ -663,7 +687,7 @@
 def join_out(me, parts, nar2, narrow):
     rows, lanes = parts[0].shape
     n = len(parts)
-    m = rows - 2 * nar2
+    m = rows - nar2
     pair = lanes // 2
     dps = m // narrow
 
@@ -677,9 +701,7 @@
                     out[pl.ds(2 * (p * dps + k) + d2, narrow, stride=narrow), :] = v[
                         k * narrow : (k + 1) * narrow, d2 * pair : (d2 + 1) * pair
                     ]
-        grads = sum(
-            ref[m : m + nar2, :].astype(F32) + ref[m + nar2 :, :].astype(F32) for ref in ins
-        )
+        grads = sum(ref[m:, :].astype(F32) for ref in ins)
         lg[...] = grads[:narrow]
         rg[...] = grads[narrow:]
 

time: 106 us -> 99.4 us (0.938)
  Pallas kernels: 53.3 us -> 47.5 us
  waiting for transfers between devices: 15.3 us -> 12.7 us
    pallas_call x8, Pallas kernels: 46.3 us -> 40.5 us  [call(): pl.pallas_call(kernel, name=name, grid_spec=pltpu.PrefetchScalarGridSpec(...]
    ppermute x15, waiting for transfers between devices: 12 us -> 6.29 us  [shift(): return lax.ppermute(value, axis, [(k, (k + t) % n) for k in range(n)])]
    ppermute x15, starting transfers between devices: 14.9 us -> 18 us  [shift(): return lax.ppermute(value, axis, [(k, (k + t) % n) for k in range(n)])]
    ppermute x3, waiting for transfers between devices: 3.35 us -> 6.37 us  [swap(): return lax.ppermute(value, axis, [(k, k ^ t) for k in range(n)])]
  transfers between devices with their start and end apart: 25 -> 25, of which waited for: 11 -> 4; matrix products, arithmetic and copies ran while one was open for 1% -> 1% of each run, Pallas kernels for 35% -> 44%
where the time goes in v3:
time: 99.4 us; the launch traced here: 98.7 us
  Pallas kernels  47.5 us (48%)
  starting transfers between devices  35.7 us (36%)
  waiting for transfers between devices  12.7 us (13%)
  other arithmetic  1.38 us (1%)
    pallas_call x8, Pallas kernels, call(): pl.pallas_call(kernel, name=name, grid_spec=pltpu.PrefetchScalarGridSpec(...  40.5 us
    ppermute x15, starting transfers between devices, shift(): return lax.ppermute(value, axis, [(k, (k + t) % n) for k in range(n)])  18 us
    ppermute x1, starting transfers between devices, spread(): lax.ppermute(value, BOTH, second)  8.84 us
    pallas_call x2, Pallas kernels, finish(): pl.pallas_call(kernel, name='finish', grid_spec=pltpu.PrefetchScalarGridS...  6.99 us
    ppermute x3, waiting for transfers between devices, swap(): return lax.ppermute(value, axis, [(k, k ^ t) for k in range(n)])  6.37 us
    ppermute x15, waiting for transfers between devices, shift(): return lax.ppermute(value, axis, [(k, (k + t) % n) for k in range(n)])  6.29 us
    ppermute x4, starting transfers between devices, to_owners(): parts.append(lax.ppermute(piece, BOTH, pairs))  5.4 us
  transfers between devices with their start and end apart: 25, of which 4 were waited for; matrix products, arithmetic and copies ran while one was open for 1% of the time, Pallas kernels for 44%

profile of v3, /device:TPU:0, one launch (start us, length us, event | category | flops | bytes accessed | tf_op | source)
XLA Modules:
  0.0 98.7 jit_solution(111639392278828897)
XLA Ops:
  1.9 7.5 %project.1 = (bf16[2,48,64,256]{3,2,1,0:T(8,128)(2,1)}, bf16[2,48,64,256]{3,2,1,0:T(8,128)(2,1)}, f32[2,6,64,128]{3,2,1,0:T(8,128)}, bf16[96,2048]{1,0:T(8,128)(2,1)}) custom-call(s32[64,96]{1,0:T(8,128)} %bitcast.20, bf16[2,48,64,256]{3,2,1,0:T(8,128)(2,1)} %bitcast.34, f32[1,256]{1,0:T(1,128)} %bitcast.30, f32[1,256]{1,0:T(1,128)} %bitcast.37, ...), custom_call_target="tpu_custom_call" | custom-call | flops 1000000000 | bytes 1024 | tf_op jit(solution)/shard_map/project/pallas_call | solution.py:53
  9.4 8.8 %collective-permute-start.2 = (bf16[96,2048]{1,0:T(8,128)(2,1)}, bf16[96,2048]{1,0:T(8,128)(2,1)S(1)}, u32[]{:S(2)}, u32[]{:S(2)}) collective-permute-start(bf16[96,2048]{1,0:T(8,128)(2,1)} %get-tuple-element.56.rest_0_), channel_id=1, source_target_pairs={{0,12},{5,9},{10,6},{15,3},{16,28},{21,25},{26,22},{31,19}} | collective-permute-start | bytes 1179656 | tf_op jit(solution)/shard_map/ppermute | solution.py:772
  19.6 8.4 %grad_outer_right.1 = (bf16[64,64,128]{2,1,0:T(8,128)(2,1)S(1)}, bf16[2048,2048]{1,0:T(8,128)(2,1)S(1)}, bf16[512,256]{1,0:T(8,128)(2,1)S(1)}, bf16[2048,96]{1,0...) custom-call(s32[1]{0:T(128)} %bitcast.2.own_ref, ...), custom_call_target="tpu_custom_call" | custom-call | flops 4000000000 | bytes 1024 | tf_op jit(solution)/shard_map/grad_outer_right/pallas_call | solution.py:53
  28.0 1.5 %collective-permute-start.6 = (bf16[24,2048]{1,0:T(8,128)(2,1)}, bf16[24,2048]{1,0:T(8,128)(2,1)S(1)}, u32[]{:S(2)}, u32[]{:S(2)}) collective-permute-start(bf16[24,2048]{1,0:T(8,128)(2,1)} %get-tuple-element.74), channel_id=1, source_target_pairs={{0,0},{1,4},{2,8},{3,12},{4,1},{5,5},{6,9},{7,13},{8,2},{9,6},{10,... | collective-permute-start | bytes 294920 | tf_op jit(solution)/shard_map/ppermute | solution.py:805
  29.6 4.2 %grad_left_side.1 = (bf16[96,2048]{1,0:T(8,128)(2,1)S(1)}, bf16[24,2048]{1,0:T(8,128)(2,1)}, bf16[24,2048]{1,0:T(8,128)(2,1)}, bf16[24,2048]{1,0:T(8,128)(2,1)}, bf16[24,2048]{1,0:T(8,128)(2,1)}) custom-call(s32[1]{0:T(128)} %bitcast.sel_ref, s32[1]{0:T(128)} %bitcast.1.me_ref, bf16[2048,2048]{1,0:T(8,128)(2,1)S(1)} %get-tuple-element.55.g_ref, ...), custom_call_target="tpu_custom_call" | custom-call | flops 4000000000 | bytes 1024 | tf_op jit(solution)/shard_map/grad_left_side/pallas_call | solution.py:53
  33.8 3.0 %collective-permute-start.4 = (bf16[24,2048]{1,0:T(8,128)(2,1)}, bf16[24,2048]{1,0:T(8,128)(2,1)}, u32[]{:S(2)}, u32[]{:S(2)}) collective-permute-start(bf16[24,2048]{1,0:T(8,128)(2,1)} %get-tuple-element.59), channel_id=1, source_target_pairs={{0,2},{1,3},{2,0},{3,1},{4,6},{5,7},{6,4},{7,5},{8,10},{9,11},{10,... | collective-permute-start | bytes 294920 | tf_op jit(solution)/shard_map/ppermute | solution.py:731
  37.7 2.0 %collective-permute-start.8 = (bf16[24,2048]{1,0:T(8,128)(2,1)S(1)}, bf16[24,2048]{1,0:T(8,128)(2,1)}, u32[]{:S(2)}, u32[]{:S(2)}) collective-permute-start(bf16[24,2048]{1,0:T(8,128)(2,1)S(1)} %copy-done.5), channel_id=1, source_target_pairs={{0,2},{1,6},{2,10},{3,14},{4,3},{5,7},{6,11},{7,15},{8,0},{9,4},{1... | collective-permute-start | bytes 294920 | tf_op jit(solution)/shard_map/ppermute | solution.py:805
  39.7 1.8 %collective-permute-start.9 = (bf16[24,2048]{1,0:T(8,128)(2,1)S(1)}, bf16[24,2048]{1,0:T(8,128)(2,1)}, u32[]{:S(2)}, u32[]{:S(2)}) collective-permute-start(bf16[24,2048]{1,0:T(8,128)(2,1)S(1)} %copy-done.4), channel_id=1, source_target_pairs={{0,3},{1,7},{2,11},{3,15},{4,0},{5,4},{6,8},{7,12},{8,1},{9,5},{10... | collective-permute-start | bytes 294920 | tf_op jit(solution)/shard_map/ppermute | solution.py:805
  41.5 10.8 %forward.1 = (bf16[64,64,128]{2,1,0:T(8,128)(2,1)}, f32[128,256]{1,0:T(8,128)}, bf16[128,256]{1,0:T(8,128)(2,1)}, bf16[128,256]{1,0:T(8,128)(2,1)}, bf16[128,256]{1,0:T(8,128)(2,1)}) custom-call(s32[1]{0:T(128)} %bitcast.3.me_ref, s32[64,96]{1,0:T(8,128)} %bitcast.22, bf16[2048,96]{1,0:T(8,128)(2,1)S(1)} %get-tuple-element.61.lt_ref, ...), custom_call_target="tpu_custom_call" | custom-call | bytes 1024 | tf_op jit(solution)/shard_map/forward/pallas_call | solution.py:53
  53.1 3.6 %collective-permute-start.12 = (bf16[128,256]{1,0:T(8,128)(2,1)}, bf16[128,256]{1,0:T(8,128)(2,1)}, u32[]{:S(2)}, u32[]{:S(2)}) collective-permute-start(bf16[128,256]{1,0:T(8,128)(2,1)} %get-tuple-element.80), channel_id=1, source_target_pairs={{0,8},{4,12},{8,0},{12,4},{1,9},{5,13},{9,1},{13,5},{2,10},{6,14},... | collective-permute-start | bytes 196616 | tf_op jit(solution)/shard_map/ppermute | solution.py:731
  56.7 4.3 %tokens.1.rest_0_.rest_4_ = bf16[896,128]{1,0:T(8,128)(2,1)} custom-call(s32[1]{0:T(128)} %bitcast.1.me_ref, s32[64,96]{1,0:T(8,128)} %bitcast.23, f32[2,6,64,128]{3,2,1,0:T(8,128)} %get-tuple-element.69.stat_ref, bf16[96,64,256]{2,1,0:T(8,128)(2,1)} %bitcast.18, bf16[24,2048]{1,0:T(8,128)(2,1)} %get-tuple-element.70.rest_0_, bf16[24,2048]{1,0:T(8,128)(2,1)} %copy-done.3, ...), custom_call_target="tpu_custom_call" | custom-call | bytes 1024 | tf_op jit(solution)/shard_map/tokens/pallas_call | solution.py:53
  61.8 1.7 %cut.1 = (f32[32,256]{1,0:T(8,128)}, f32[32,256]{1,0:T(8,128)}, f32[32,256]{1,0:T(8,128)}, f32[32,256]{1,0:T(8,128)}) custom-call(s32[1]{0:T(128)} %bitcast.1.me_ref, f32[128,256]{1,0:T(8,128)} %get-tuple-element.78.rest_0_, bf16[128,256]{1,0:T(8,128)(2,1)} %collective-permute-done.11.rest_1_, bf16[128,256]{1,0:T(8,128)(2,1)} %collective-permute-done.12.rest_2_, ...), custom_call_target="tpu_custom_call" | custom-call | flops 20000000000 | bytes 1024 | tf_op jit(solution)/shard_map/cut/pallas_call | solution.py:53
  63.5 2.1 %collective-permute-start.15 = (f32[32,256]{1,0:T(8,128)}, f32[32,256]{1,0:T(8,128)S(1)}, u32[]{:S(2)}, u32[]{:S(2)}) collective-permute-start(f32[32,256]{1,0:T(8,128)} %get-tuple-element.84), channel_id=1, source_target_pairs={{0,2},{1,3},{2,0},{3,1},{4,6},{5,7},{6,4},{7,5},{8,10},{9,11},{10,... | collective-permute-start | bytes 98312 | tf_op jit(solution)/shard_map/ppermute | solution.py:731
  65.6 2.9 %collective-permute-start.16 = (f32[32,256]{1,0:T(8,128)}, f32[32,256]{1,0:T(8,128)S(1)}, u32[]{:S(2)}, u32[]{:S(2)}) collective-permute-start(f32[32,256]{1,0:T(8,128)} %get-tuple-element.85), channel_id=1, source_target_pairs={{0,3},{1,0},{2,1},{3,2},{4,7},{5,4},{6,5},{7,6},{8,11},{9,8},{10,9... | collective-permute-start | bytes 98312 | tf_op jit(solution)/shard_map/ppermute | solution.py:731
  68.5 6.4 %collective-permute-done.20.rest_6_.rest_2_ = bf16[896,128]{1,0:T(8,128)(2,1)} collective-permute-done((bf16[896,128]{1,0:T(8,128)(2,1)}, bf16[896,128]{1,0:T(8,128)(2,1)}, u32[]{:S(2)}, u32[]{:S(2)}) %collective-permute-start.20) | collective-permute-done | bytes 229408 | tf_op jit(solution)/shard_map/ppermute | solution.py:740
  75.5 1.4 %add_add_fusion.rest_0_ = f32[32,256]{1,0:T(8,128)} fusion(f32[32,256]{1,0:T(8,128)S(1)} %collective-permute-done.16, f32[32,256]{1,0:T(8,128)S(1)} %collective-permute-done.15, f32[32,256]{1,0:T(8,128)} %get-tuple-element.82, f32[32,256]{1,0:T(8,128)S(1)} %collective-permute-done.14), kind=kLoop, calls=%fused_computation | loop fusion | flops 24576 | bytes 163840 | tf_op jit(solution)/shard_map/add | solution.py:891
  76.8 2.2 %collective-permute-start.19 = (f32[32,256]{1,0:T(8,128)}, f32[32,256]{1,0:T(8,128)}, u32[]{:S(2)}, u32[]{:S(2)}) collective-permute-start(f32[32,256]{1,0:T(8,128)} %add_add_fusion.rest_0_), channel_id=1, source_target_pairs={{0,3},{1,0},{2,1},{3,2},{4,7},{5,4},{6,5},{7,6},{8,11},{9,8},{10,9... | collective-permute-start | bytes 98312 | tf_op jit(solution)/shard_map/ppermute | solution.py:731
  80.7 3.4 %finish.2.rest_4_ = bf16[96,64,256]{2,1,0:T(8,128)(2,1)} custom-call(s32[1]{0:T(128)} %bitcast.1.me_ref, bf16[96,64,256]{2,1,0:T(8,128)(2,1)} %bitcast.15, bf16[32,256]{1,0:T(8,128)(2,1)} %bitcast.25, bf16[32,256]{1,0:T(8,128)(2,1)} %bitcast.28, f32[1,256]{1,0:T(1,128)} %bitcast.31, bf16[896,128]{1,0:T(8,128)(2,1)} %tokens.1.rest_0_.rest_4_, ...), custom_call_target="tpu_custom_call" | custom-call | flops 500000000 | bytes 1024 | tf_op jit(solution)/shard_map/finish/pallas_call | solution.py:622
  84.1 3.3 %collective-permute-done.19.rest_3_ = f32[32,256]{1,0:T(8,128)} collective-permute-done((f32[32,256]{1,0:T(8,128)}, f32[32,256]{1,0:T(8,128)}, u32[]{:S(2)}, u32[]{:S(2)}) %collective-permute-start.19) | collective-permute-done | bytes 32800 | tf_op jit(solution)/shard_map/ppermute | solution.py:731
  87.4 1.6 %join_send.1.rest_0_ = bf16[192,256]{1,0:T(8,128)(2,1)} custom-call(s32[1]{0:T(128)} %bitcast.1.me_ref, f32[32,256]{1,0:T(8,128)} %add_add_fusion.rest_0_, f32[32,256]{1,0:T(8,128)} %collective-permute-done.17.rest_1_, f32[32,256]{1,0:T(8,128)} %collective-permute-done.18.rest_2_, f32[32,256]{1,0:T(8,128)} %collective-permute-done.19.rest_3_, ...), custom_call_target="tpu_custom_call" | custom-call | flops 2000000000 | bytes 1024 | tf_op jit(solution)/shard_map/join_send/pallas_call | solution.py:53
  88.9 1.6 %collective-permute-start.23 = (bf16[192,256]{1,0:T(8,128)(2,1)}, bf16[192,256]{1,0:T(8,128)(2,1)}, u32[]{:S(2)}, u32[]{:S(2)}) collective-permute-start(bf16[192,256]{1,0:T(8,128)(2,1)} %join_send.1.rest_0_), channel_id=1, source_target_pairs={{0,8},{4,12},{8,0},{12,4},{1,9},{5,13},{9,1},{13,5},{2,10},{6,14},... | collective-permute-start | bytes 294920 | tf_op jit(solution)/shard_map/ppermute | solution.py:731
  90.6 3.6 %finish.3 = bf16[96,64,256]{2,1,0:T(8,128)(2,1)} custom-call(s32[1]{0:T(128)} %bitcast.1.me_ref, bf16[96,64,256]{2,1,0:T(8,128)(2,1)} %bitcast.16, bf16[32,256]{1,0:T(8,128)(2,1)} %bitcast.26, bf16[32,256]{1,0:T(8,128)(2,1)} %bitcast.29, f32[1,256]{1,0:T(1,128)} %bitcast.32, bf16[896,128]{1,0:T(8,128)(2,1)} %tokens.1.rest_0_.rest_4_, ...), custom_call_target="tpu_custom_call", output_to_operand_aliasing={{}: (9, {})} | custom-call | flops 200000000 | bytes 1024 | tf_op jit(solution)/shard_map/finish/pallas_call | solution.py:622
  94.2 2.4 %collective-permute-done.23.rest_2_ = bf16[192,256]{1,0:T(8,128)(2,1)} collective-permute-done((bf16[192,256]{1,0:T(8,128)(2,1)}, bf16[192,256]{1,0:T(8,128)(2,1)}, u32[]{:S(2)}, u32[]{:S(2)}) %collective-permute-start.23) | collective-permute-done | bytes 98336 | tf_op jit(solution)/shard_map/ppermute | solution.py:731
  96.6 2.1 %join_out.1 = (f32[1024,128]{1,0:T(8,128)}, f32[32,256]{1,0:T(8,128)}, f32[32,256]{1,0:T(8,128)}) custom-call(s32[1]{0:T(128)} %bitcast.3.me_ref, bf16[192,256]{1,0:T(8,128)(2,1)} %join_send.1.rest_0_, bf16[192,256]{1,0:T(8,128)(2,1)} %collective-permute-done.22.rest_1_, bf16[192,256]{1,0:T(8,128)(2,1)} %collective-permute-done.23.rest_2_, ...), custom_call_target="tpu_custom_call" | custom-call | bytes 1024 | tf_op jit(solution)/shard_map/join_out/pallas_call | solution.py:53
  (49 shorter events, 7.3 us)
Async XLA Ops:
  0.6 8.7 %collective-permute-start = (s32[64,96]{1,0:T(8,128)}, s32[64,96]{1,0:T(8,128)}, u32[]{:S(2)}, u32[]{:S(2)}) collective-permute-start(s32[64,96]{1,0:T(8,128)} %bitcast.19), channel_id=1, source_target_pairs={{1,4},{2,8},{3,12},{6,9},{7,13},{4,1},{11,14},{8,2},{9,6},{12,3},{... | collective-permute-start | bytes 73736 | tf_op jit(solution)/shard_map/ppermute | solution.py:760
  9.4 20.2 %collective-permute-start.2 = (bf16[96,2048]{1,0:T(8,128)(2,1)}, bf16[96,2048]{1,0:T(8,128)(2,1)S(1)}, u32[]{:S(2)}, u32[]{:S(2)}) collective-permute-start(bf16[96,2048]{1,0:T(8,128)(2,1)} %get-tuple-element.56.rest_0_), channel_id=1, source_target_pairs={{0,12},{5,9},{10,6},{15,3},{16,28},{21,25},{26,22},{31,19}} | collective-permute-start | bytes 1179656 | tf_op jit(solution)/shard_map/ppermute | solution.py:772
  18.2 11.3 %collective-permute-start.1 = (bf16[96,2048]{1,0:T(8,128)(2,1)}, bf16[96,2048]{1,0:T(8,128)(2,1)S(1)}, u32[]{:S(2)}, u32[]{:S(2)}) collective-permute-start(bf16[96,2048]{1,0:T(8,128)(2,1)} %get-tuple-element.56.rest_0_), channel_id=1, source_target_pairs={{0,8},{5,13},{10,2},{15,7},{1,4},{4,1},{11,14},{14,11},{16,24},{21... | collective-permute-start | bytes 1179656 | tf_op jit(solution)/shard_map/ppermute | solution.py:772
  28.0 9.6 %collective-permute-start.6 = (bf16[24,2048]{1,0:T(8,128)(2,1)}, bf16[24,2048]{1,0:T(8,128)(2,1)S(1)}, u32[]{:S(2)}, u32[]{:S(2)}) collective-permute-start(bf16[24,2048]{1,0:T(8,128)(2,1)} %get-tuple-element.74), channel_id=1, source_target_pairs={{0,0},{1,4},{2,8},{3,12},{4,1},{5,5},{6,9},{7,13},{8,2},{9,6},{10,... | collective-permute-start | bytes 294920 | tf_op jit(solution)/shard_map/ppermute | solution.py:805
  29.6 10.1 %collective-permute-start.7 = (bf16[24,2048]{1,0:T(8,128)(2,1)}, bf16[24,2048]{1,0:T(8,128)(2,1)S(1)}, u32[]{:S(2)}, u32[]{:S(2)}) collective-permute-start(bf16[24,2048]{1,0:T(8,128)(2,1)} %get-tuple-element.75), channel_id=1, source_target_pairs={{0,1},{1,5},{2,9},{3,13},{4,2},{5,6},{6,10},{7,14},{8,3},{9,7},{10... | collective-permute-start | bytes 294920 | tf_op jit(solution)/shard_map/ppermute | solution.py:805
  33.8 18.6 %collective-permute-start.3 = (bf16[24,2048]{1,0:T(8,128)(2,1)}, bf16[24,2048]{1,0:T(8,128)(2,1)S(1)}, u32[]{:S(2)}, u32[]{:S(2)}) collective-permute-start(bf16[24,2048]{1,0:T(8,128)(2,1)} %get-tuple-element.58), channel_id=1, source_target_pairs={{0,1},{1,2},{2,3},{3,0},{4,5},{5,6},{6,7},{7,4},{8,9},{9,10},{10,1... | collective-permute-start | bytes 294920 | tf_op jit(solution)/shard_map/ppermute | solution.py:731
  33.8 19.3 %collective-permute-start.4 = (bf16[24,2048]{1,0:T(8,128)(2,1)}, bf16[24,2048]{1,0:T(8,128)(2,1)}, u32[]{:S(2)}, u32[]{:S(2)}) collective-permute-start(bf16[24,2048]{1,0:T(8,128)(2,1)} %get-tuple-element.59), channel_id=1, source_target_pairs={{0,2},{1,3},{2,0},{3,1},{4,6},{5,7},{6,4},{7,5},{8,10},{9,11},{10,... | collective-permute-start | bytes 294920 | tf_op jit(solution)/shard_map/ppermute | solution.py:731
  36.8 19.9 %collective-permute-start.5 = (bf16[24,2048]{1,0:T(8,128)(2,1)}, bf16[24,2048]{1,0:T(8,128)(2,1)}, u32[]{:S(2)}, u32[]{:S(2)}) collective-permute-start(bf16[24,2048]{1,0:T(8,128)(2,1)} %get-tuple-element.60), channel_id=1, source_target_pairs={{0,3},{1,0},{2,1},{3,2},{4,7},{5,4},{6,5},{7,6},{8,11},{9,8},{10,9... | collective-permute-start | bytes 294920 | tf_op jit(solution)/shard_map/ppermute | solution.py:731
  37.7 19.0 %collective-permute-start.8 = (bf16[24,2048]{1,0:T(8,128)(2,1)S(1)}, bf16[24,2048]{1,0:T(8,128)(2,1)}, u32[]{:S(2)}, u32[]{:S(2)}) collective-permute-start(bf16[24,2048]{1,0:T(8,128)(2,1)S(1)} %copy-done.5), channel_id=1, source_target_pairs={{0,2},{1,6},{2,10},{3,14},{4,3},{5,7},{6,11},{7,15},{8,0},{9,4},{1... | collective-permute-start | bytes 294920 | tf_op jit(solution)/shard_map/ppermute | solution.py:805
  39.7 17.0 %collective-permute-start.9 = (bf16[24,2048]{1,0:T(8,128)(2,1)S(1)}, bf16[24,2048]{1,0:T(8,128)(2,1)}, u32[]{:S(2)}, u32[]{:S(2)}) collective-permute-start(bf16[24,2048]{1,0:T(8,128)(2,1)S(1)} %copy-done.4), channel_id=1, source_target_pairs={{0,3},{1,7},{2,11},{3,15},{4,0},{5,4},{6,8},{7,12},{8,1},{9,5},{10... | collective-permute-start | bytes 294920 | tf_op jit(solution)/shard_map/ppermute | solution.py:805
  53.1 8.8 %collective-permute-start.11 = (bf16[128,256]{1,0:T(8,128)(2,1)}, bf16[128,256]{1,0:T(8,128)(2,1)}, u32[]{:S(2)}, u32[]{:S(2)}) collective-permute-start(bf16[128,256]{1,0:T(8,128)(2,1)} %get-tuple-element.79), channel_id=1, source_target_pairs={{0,4},{4,8},{8,12},{12,0},{1,5},{5,9},{9,13},{13,1},{2,6},{6,10},{... | collective-permute-start | bytes 196616 | tf_op jit(solution)/shard_map/ppermute | solution.py:731
  53.1 8.8 %collective-permute-start.12 = (bf16[128,256]{1,0:T(8,128)(2,1)}, bf16[128,256]{1,0:T(8,128)(2,1)}, u32[]{:S(2)}, u32[]{:S(2)}) collective-permute-start(bf16[128,256]{1,0:T(8,128)(2,1)} %get-tuple-element.80), channel_id=1, source_target_pairs={{0,8},{4,12},{8,0},{12,4},{1,9},{5,13},{9,1},{13,5},{2,10},{6,14},... | collective-permute-start | bytes 196616 | tf_op jit(solution)/shard_map/ppermute | solution.py:731
  61.0 13.9 %collective-permute-start.20 = (bf16[896,128]{1,0:T(8,128)(2,1)}, bf16[896,128]{1,0:T(8,128)(2,1)}, u32[]{:S(2)}, u32[]{:S(2)}) collective-permute-start(bf16[896,128]{1,0:T(8,128)(2,1)} %tokens.1.rest_0_.rest_4_), channel_id=1, source_target_pairs={{0,2},{1,3},{2,0},{3,1},{4,6},{5,7},{6,4},{7,5},{8,10},{9,11},{10,... | collective-permute-start | bytes 688136 | tf_op jit(solution)/shard_map/ppermute | solution.py:740
  63.5 11.4 %collective-permute-start.14 = (f32[32,256]{1,0:T(8,128)}, f32[32,256]{1,0:T(8,128)S(1)}, u32[]{:S(2)}, u32[]{:S(2)}) collective-permute-start(f32[32,256]{1,0:T(8,128)} %get-tuple-element.83), channel_id=1, source_target_pairs={{0,1},{1,2},{2,3},{3,0},{4,5},{5,6},{6,7},{7,4},{8,9},{9,10},{10,1... | collective-permute-start | bytes 98312 | tf_op jit(solution)/shard_map/ppermute | solution.py:731
  63.5 11.9 %collective-permute-start.15 = (f32[32,256]{1,0:T(8,128)}, f32[32,256]{1,0:T(8,128)S(1)}, u32[]{:S(2)}, u32[]{:S(2)}) collective-permute-start(f32[32,256]{1,0:T(8,128)} %get-tuple-element.84), channel_id=1, source_target_pairs={{0,2},{1,3},{2,0},{3,1},{4,6},{5,7},{6,4},{7,5},{8,10},{9,11},{10,... | collective-permute-start | bytes 98312 | tf_op jit(solution)/shard_map/ppermute | solution.py:731
  65.6 9.8 %collective-permute-start.16 = (f32[32,256]{1,0:T(8,128)}, f32[32,256]{1,0:T(8,128)S(1)}, u32[]{:S(2)}, u32[]{:S(2)}) collective-permute-start(f32[32,256]{1,0:T(8,128)} %get-tuple-element.85), channel_id=1, source_target_pairs={{0,3},{1,0},{2,1},{3,2},{4,7},{5,4},{6,5},{7,6},{8,11},{9,8},{10,9... | collective-permute-start | bytes 98312 | tf_op jit(solution)/shard_map/ppermute | solution.py:731
  68.5 12.2 %collective-permute-start.10 = (bf16[896,128]{1,0:T(8,128)(2,1)}, bf16[896,128]{1,0:T(8,128)(2,1)}, u32[]{:S(2)}, u32[]{:S(2)}) collective-permute-start(bf16[896,128]{1,0:T(8,128)(2,1)} %tokens.1.rest_0_.rest_4_), channel_id=1, source_target_pairs={{0,1},{1,0},{2,3},{3,2},{4,5},{5,4},{6,7},{7,6},{8,9},{9,8},{10,11... | collective-permute-start | bytes 688136 | tf_op jit(solution)/shard_map/ppermute | solution.py:740
  74.9 12.5 %collective-permute-start.21 = (bf16[896,128]{1,0:T(8,128)(2,1)}, bf16[896,128]{1,0:T(8,128)(2,1)}, u32[]{:S(2)}, u32[]{:S(2)}) collective-permute-start(bf16[896,128]{1,0:T(8,128)(2,1)} %collective-permute-done.20.rest_6_.rest_2_), channel_id=1, source_target_pairs={{0,1},{1,0},{2,3},{3,2},{4,5},{5,4},{6,7},{7,6},{8,9},{9,8},{10,11... | collective-permute-start | bytes 688136 | tf_op jit(solution)/shard_map/ppermute | solution.py:740
  76.8 10.5 %collective-permute-start.19 = (f32[32,256]{1,0:T(8,128)}, f32[32,256]{1,0:T(8,128)}, u32[]{:S(2)}, u32[]{:S(2)}) collective-permute-start(f32[32,256]{1,0:T(8,128)} %add_add_fusion.rest_0_), channel_id=1, source_target_pairs={{0,3},{1,0},{2,1},{3,2},{4,7},{5,4},{6,5},{7,6},{8,11},{9,8},{10,9... | collective-permute-start | bytes 98312 | tf_op jit(solution)/shard_map/ppermute | solution.py:731
  79.0 8.4 %collective-permute-start.18 = (f32[32,256]{1,0:T(8,128)}, f32[32,256]{1,0:T(8,128)}, u32[]{:S(2)}, u32[]{:S(2)}) collective-permute-start(f32[32,256]{1,0:T(8,128)} %add_add_fusion.rest_0_), channel_id=1, source_target_pairs={{0,2},{1,3},{2,0},{3,1},{4,6},{5,7},{6,4},{7,5},{8,10},{9,11},{10,... | collective-permute-start | bytes 98312 | tf_op jit(solution)/shard_map/ppermute | solution.py:731
  79.8 7.6 %collective-permute-start.17 = (f32[32,256]{1,0:T(8,128)}, f32[32,256]{1,0:T(8,128)}, u32[]{:S(2)}, u32[]{:S(2)}) collective-permute-start(f32[32,256]{1,0:T(8,128)} %add_add_fusion.rest_0_), channel_id=1, source_target_pairs={{0,1},{1,2},{2,3},{3,0},{4,5},{5,6},{6,7},{7,4},{8,9},{9,10},{10,1... | collective-permute-start | bytes 98312 | tf_op jit(solution)/shard_map/ppermute | solution.py:731
  88.9 5.2 %collective-permute-start.24 = (bf16[192,256]{1,0:T(8,128)(2,1)}, bf16[192,256]{1,0:T(8,128)(2,1)}, u32[]{:S(2)}, u32[]{:S(2)}) collective-permute-start(bf16[192,256]{1,0:T(8,128)(2,1)} %join_send.1.rest_0_), channel_id=1, source_target_pairs={{0,12},{4,0},{8,4},{12,8},{1,13},{5,1},{9,5},{13,9},{2,14},{6,2},{... | collective-permute-start | bytes 294920 | tf_op jit(solution)/shard_map/ppermute | solution.py:731
  88.9 7.6 %collective-permute-start.23 = (bf16[192,256]{1,0:T(8,128)(2,1)}, bf16[192,256]{1,0:T(8,128)(2,1)}, u32[]{:S(2)}, u32[]{:S(2)}) collective-permute-start(bf16[192,256]{1,0:T(8,128)(2,1)} %join_send.1.rest_0_), channel_id=1, source_target_pairs={{0,8},{4,12},{8,0},{12,4},{1,9},{5,13},{9,1},{13,5},{2,10},{6,14},... | collective-permute-start | bytes 294920 | tf_op jit(solution)/shard_map/ppermute | solution.py:731
  90.6 6.0 %collective-permute-start.22 = (bf16[192,256]{1,0:T(8,128)(2,1)}, bf16[192,256]{1,0:T(8,128)(2,1)}, u32[]{:S(2)}, u32[]{:S(2)}) collective-permute-start(bf16[192,256]{1,0:T(8,128)(2,1)} %join_send.1.rest_0_), channel_id=1, source_target_pairs={{0,4},{4,8},{8,12},{12,0},{1,5},{5,9},{9,13},{13,1},{2,6},{6,10},{... | collective-permute-start | bytes 294920 | tf_op jit(solution)/shard_map/ppermute | solution.py:731
  (7 other events, 61.4 us)

commit v4 on v3

--- a/solution.py
+++ b/solution.py
@@ -11,7 +11,7 @@
 NT = (((1,), (1,)), ((), ()))
 TN = (((0,), (0,)), ((), ()))
 VMEM = 64 * 1024 * 1024
-COST = {'grad_outer_right': 4, 'grad_left_side': 4, 'cut': 20, 'finish_a': 0.5, 'finish_b': 0.2, 'join_send': 2, 'project': 1}
+COST = {'grad_outer_right': 4, 'grad_left_side': 4, 'cut': 20, 'finish_a': 2, 'finish_b': 6, 'join_send': 2, 'project': 1}
 IBLK = 8
 
 
@@ -146,20 +146,20 @@
             whole(wr_t.shape),
         ],
         [
-            (tile, shape((2, half, rows, chans))),
-            (tile, shape((2, half, rows, chans))),
+            (tile, sent((2, half, rows, chans))),
+            (tile, kept((2, half, rows, chans))),
             (
                 pl.BlockSpec((2, blk // 8, rows, 128), lambda n: (0, n, 0, 0)),
-                shape((2, half // 8, rows, 128), F32),
+                sent((2, half // 8, rows, 128), F32),
             ),
-            (whole((seqs, wide)), shape((seqs, wide))),
+            (whole((seqs, wide)), sent((seqs, wide))),
         ],
         [
             pltpu.VMEM((half * narrow, 2 * rows), F32),
             pltpu.VMEM((2 * blk * rows, chans), BF),
         ],
         (),
-        (
+        far(
             cov_t,
             alignment.reshape(2, half, rows, chans),
             gain[None, :],
@@ -168,6 +168,7 @@
         ),
         2e9,
         7e6,
+        VMEM // 2,
     )
 
 
@@ -201,7 +202,8 @@
 
 def right_side(own, me, cov_t, cov_far, cot, out_weight, wl_t, normed, block, pieces, piece_rows):
     rows, _, pair = cot.shape
-    seqs, _, chans = normed.shape
+    half, chans = normed.shape[1], normed.shape[3]
+    seqs = 2 * half
     cols = cov_far.shape[0]
     narrow = wl_t.shape[0]
     wide = rows * narrow
@@ -292,7 +294,7 @@
             pl.BlockSpec((i_blk, cols, pair), lambda n, *_: (n, block, 0)),
             whole(out_weight.shape),
             whole(wl_t.shape),
-            pl.BlockSpec((seqs, i_blk, chans), lambda n, *_: (0, n, 0)),
+            pl.BlockSpec((2, half, i_blk, chans), lambda n, *_: (0, 0, n, 0)),
         ],
         [
             (
@@ -315,7 +317,7 @@
             pltpu.VMEM((rows, 128), F32),
         ],
         (own, me),
-        far(cov_t, cov_far, cot, out_weight, wl_t, normed),
+        (*far(cov_t), *near(cov_far), *far(cot, out_weight, wl_t, normed)),
         4e9,
         16e6,
         VMEM // 2,
@@ -462,7 +464,8 @@
 
 
 def tokens(me, cov_t, stat, lefts, rights, normed):
-    seqs, rows, chans = normed.shape
+    half, rows, chans = normed.shape[1:]
+    seqs = 2 * half
     piece_rows, wide = lefts[0].shape
     narrow = wide // rows
     count = piece_rows * rows
@@ -504,10 +507,10 @@
             at = b * 2 * quad
             stats = stat_ref[0, b]
             pair_up, scaled = [], []
-            for half in range(2):
-                v = z[at + half * quad : at + (half + 1) * quad, :]
+            for h2 in range(2):
+                v = z[at + h2 * quad : at + (h2 + 1) * quad, :]
                 inv = [
-                    jnp.broadcast_to(stats[:, 4 * half + j : 4 * half + j + 1], (rows, nar2))
+                    jnp.broadcast_to(stats[:, 4 * h2 + j : 4 * h2 + j + 1], (rows, nar2))
                     for j in range(4)
                 ]
                 pair_up.append(v)
@@ -538,16 +541,23 @@
                 ),
             ),
             pl.BlockSpec(
-                (piece_rows, rows, chans), lambda n, me: (jnp.minimum(me[0], last), 0, 0)
+                (1, piece_rows, rows, chans),
+                lambda n, me: (
+                    jnp.minimum(me[0], last) // per_half,
+                    jnp.minimum(me[0], last) % per_half,
+                    0,
+                    0,
+                ),
             ),
         ]
         + [whole((piece_rows, wide))] * (n_l + n_r),
         [(whole((h + nar2 * chans // 128, 128)), shape((h + nar2 * chans // 128, 128)))],
         [pltpu.VMEM((count, nar2), F32), pltpu.VMEM((piece_rows * narrow, rows), F32)],
         (me,),
-        (cov_t, stat, normed, *lefts, *rights),
+        (*far(cov_t, stat, normed, lefts[0]), *lefts[1:], *rights),
         4e8,
         2e6,
+        VMEM // 2,
     )[0]
 
 
@@ -567,19 +577,22 @@
         [(whole((m // pieces, lanes)), shape((m // pieces, lanes), F32))] * pieces,
         [pltpu.VMEM((m, lanes), F32)],
         (me,),
-        tuple(parts),
+        (*far(parts[0]), *parts[1:]),
         1e6,
         1e6,
+        VMEM // 2,
     )
 
 
-def finish(me, qs, alignment, wl_t, wr_t, gain, first, count, before=None):
-    seqs, rows, chans = alignment.shape
+def finish(me, qs, xhat, wl_t, wr_t, gain, first, count, before=None):
+    _, per_half, rows, chans = xhat.shape
+    seqs = 2 * per_half
     pieces = len(qs)
     quad = 4 * rows
     nar2 = 2 * wl_t.shape[0]
     blocks = (qs[0].shape[0] - nar2 * chans // 128) // quad
-    every = count == seqs // (8 * blocks)
+    per_half //= 8 * blocks
+    every = count == 2 * per_half
     given = () if before is None else (before,)
 
     def piece(n, me_ref):
@@ -613,12 +626,16 @@
                 g = dot(both, wc[half])
                 for j in range(4):
                     s = half * 4 + j
-                    xh = x_ref[8 * b + s].astype(F32)
+                    xh = x_ref[0, 8 * b + s].astype(F32)
                     gc = g[j * rows : (j + 1) * rows]
                     m = jnp.mean(gc * xh, axis=-1, keepdims=True)
                     out[8 * b + s] = (gc - xh * m).astype(BF)
 
     blk = pl.BlockSpec((8 * blocks, rows, chans), lambda n, me_ref: (piece(n, me_ref), 0, 0))
+    source = pl.BlockSpec(
+        (1, 8 * blocks, rows, chans),
+        lambda n, me_ref: (piece(n, me_ref) // per_half, piece(n, me_ref) % per_half, 0, 0),
+    )
     return pl.pallas_call(
         kernel,
         name="finish",
@@ -626,7 +643,7 @@
             num_scalar_prefetch=1,
             grid=(count,),
             in_specs=[
-                blk,
+                source,
                 whole(wl_t.shape),
                 whole(wr_t.shape),
                 whole((1, chans)),
@@ -639,15 +656,15 @@
                 pltpu.VMEM((blocks * quad, 128), BF),
             ],
         ),
-        out_shape=shape(alignment.shape),
+        out_shape=sent((seqs, rows, chans)),
         input_output_aliases={5 + pieces: 0} if given else {},
-        compiler_params=params(),
+        compiler_params=params(VMEM // 2),
         cost_estimate=pl.CostEstimate(
             flops=int(COST.get("finish_a" if before is None else "finish_b", 0) * 1e9),
             bytes_accessed=1024,
             transcendentals=0,
         ),
-    )(me, alignment, wl_t, wr_t, gain[None, :], *qs, *given)
+    )(me, *near(xhat), *far(wl_t, wr_t, gain[None, :]), *qs, *given)
 
 
 def join_send(me, parts, qs, nar2):
@@ -675,12 +692,13 @@
         (1,),
         [whole((m, lanes))] * n
         + [pl.BlockSpec((extra, 128), lambda *_: (h // extra, 0))] * len(qs),
-        [(whole((total, lanes)), shape((total, lanes)))],
+        [(whole((total, lanes)), sent((total, lanes)))],
         [pltpu.VMEM((n * m, lanes), F32)],
         (me,),
         (*parts, *qs),
         1e6,
         1e6,
+        VMEM // 2,
     )[0]
 
 
@@ -717,9 +735,10 @@
         ],
         [],
         (me,),
-        parts,
+        (*far(parts[0]), *parts[1:]),
         1e6,
         1e6,
+        VMEM // 2,
     )
 
 
@@ -836,8 +855,6 @@
     cov_far = [spread_small(cov_t, m, ratio) for m in range(ratio)]
     normed, xhat, stat, right = project(cov_t, alignment, layer_norm_gain, layer_norm_bias, wr_t)
     right, cov_far = lax.optimization_barrier((right, cov_far))
-    normed = normed.reshape(seqs, rows, chans)
-    xhat = xhat.reshape(seqs, rows, chans)
 
     right_pieces, firsts = [], []
     for m in range(ratio):

time: 99.4 us -> 97.1 us (0.977)
  Pallas kernels: 47.5 us -> 43 us
  waiting for transfers between devices: 12.7 us -> 15.4 us
  other arithmetic: 1.38 us -> 0.01 us
    pallas_call x8, Pallas kernels: 40.5 us -> 37.3 us  [call(): pl.pallas_call(kernel, name=name, grid_spec=pltpu.PrefetchScalarGridSpec(...]
    ppermute x15, waiting for transfers between devices: 6.29 us -> 7.77 us  [shift(): return lax.ppermute(value, axis, [(k, (k + t) % n) for k in range(n)])]
    add x1, other arithmetic: 1.38 us -> 0.01 us  [body(): part = sum(shifts(pieces[0], pieces[1:], 'col'))]
    pallas_call x2, Pallas kernels: 6.99 us -> 5.71 us  [finish(): pl.pallas_call(kernel, name='finish', grid_spec=pltpu.PrefetchScalarGridS...]
    ppermute x3, waiting for transfers between devices: 6.37 us -> 7.59 us  [swap(): return lax.ppermute(value, axis, [(k, k ^ t) for k in range(n)])]
  transfers between devices with their start and end apart: 25 -> 25, of which waited for: 4 -> 5; matrix products, arithmetic and copies ran while one was open for 1% -> 0% of each run, Pallas kernels for 44% -> 42%
where the time goes in v4:
time: 97.1 us; the launch traced here: 96.5 us
  Pallas kernels  43 us (44%)
  starting transfers between devices  35.7 us (37%)
  waiting for transfers between devices  15.4 us (16%)
  local copies, waits for them, and re-layouts  1.65 us (2%)
    pallas_call x8, Pallas kernels, call(): pl.pallas_call(kernel, name=name, grid_spec=pltpu.PrefetchScalarGridSpec(...  37.3 us
    ppermute x15, starting transfers between devices, shift(): return lax.ppermute(value, axis, [(k, (k + t) % n) for k in range(n)])  18.1 us
    ppermute x1, starting transfers between devices, spread(): lax.ppermute(value, BOTH, second)  9.41 us
    ppermute x15, waiting for transfers between devices, shift(): return lax.ppermute(value, axis, [(k, (k + t) % n) for k in range(n)])  7.77 us
    ppermute x3, waiting for transfers between devices, swap(): return lax.ppermute(value, axis, [(k, k ^ t) for k in range(n)])  7.59 us
    pallas_call x2, Pallas kernels, finish(): pl.pallas_call(kernel, name='finish', grid_spec=pltpu.PrefetchScalarGridS...  5.71 us
    ppermute x4, starting transfers between devices, to_owners(): parts.append(lax.ppermute(piece, BOTH, pairs))  5.3 us
  transfers between devices with their start and end apart: 25, of which 5 were waited for; matrix products, arithmetic and copies ran while one was open for 0% of the time, Pallas kernels for 42%

profile of v4, /device:TPU:0, one launch (start us, length us, event | category | flops | bytes accessed | tf_op | source)
XLA Modules:
  0.0 96.5 jit_solution(5874027139367846608)
XLA Ops:
  1.3 6.8 %project.1 = (bf16[2,48,64,256]{3,2,1,0:T(8,128)(2,1)}, bf16[2,48,64,256]{3,2,1,0:T(8,128)(2,1)S(1)}, f32[2,6,64,128]{3,2,1,0:T(8,128)}, bf16[96,2048]{1,0:T(8,128)(2,1)}) custom-call(s32[64,96]{1,0:T(8,128)} %bitcast.14, bf16[2,48,64,256]{3,2,1,0:T(8,128)(2,1)} %bitcast.19, f32[1,256]{1,0:T(1,128)} %bitcast.29, f32[1,256]{1,0:T(1,128)} %bitcast.28, ...), custom_call_target="tpu_custom_call" | custom-call | flops 1000000000 | bytes 1024 | tf_op jit(solution)/shard_map/project/pallas_call | solution.py:53
  8.1 1.6 %copy-done.1 = bf16[2,48,64,256]{3,2,1,0:T(8,128)(2,1)} copy-done((bf16[2,48,64,256]{3,2,1,0:T(8,128)(2,1)}, bf16[2,48,64,256]{3,2,1,0:T(8,128)(2,1)S(1)}, u32[]{:S(2)}) %copy-start.1) | copy-done | bytes 3145752
  9.8 9.4 %collective-permute-start.2 = (bf16[96,2048]{1,0:T(8,128)(2,1)}, bf16[96,2048]{1,0:T(8,128)(2,1)S(1)}, u32[]{:S(2)}, u32[]{:S(2)}) collective-permute-start(bf16[96,2048]{1,0:T(8,128)(2,1)} %get-tuple-element.56.rest_0_), channel_id=1, source_target_pairs={{0,12},{5,9},{10,6},{15,3},{16,28},{21,25},{26,22},{31,19}} | collective-permute-start | bytes 1179656 | tf_op jit(solution)/shard_map/ppermute | solution.py:791
  19.2 1.3 %collective-permute-start.1 = (bf16[96,2048]{1,0:T(8,128)(2,1)}, bf16[96,2048]{1,0:T(8,128)(2,1)S(1)}, u32[]{:S(2)}, u32[]{:S(2)}) collective-permute-start(bf16[96,2048]{1,0:T(8,128)(2,1)} %get-tuple-element.56.rest_0_), channel_id=1, source_target_pairs={{0,8},{5,13},{10,2},{15,7},{1,4},{4,1},{11,14},{14,11},{16,24},{21... | collective-permute-start | bytes 1179656 | tf_op jit(solution)/shard_map/ppermute | solution.py:791
  20.5 8.4 %grad_outer_right.1 = (bf16[64,64,128]{2,1,0:T(8,128)(2,1)S(1)}, bf16[2048,2048]{1,0:T(8,128)(2,1)S(1)}, bf16[512,256]{1,0:T(8,128)(2,1)S(1)}, bf16[2048,96]{1,0...) custom-call(s32[1]{0:T(128)} %bitcast.2.own_ref, ...), custom_call_target="tpu_custom_call" | custom-call | flops 4000000000 | bytes 1024 | tf_op jit(solution)/shard_map/grad_outer_right/pallas_call | solution.py:53
  28.9 1.5 %collective-permute-start.6 = (bf16[24,2048]{1,0:T(8,128)(2,1)}, bf16[24,2048]{1,0:T(8,128)(2,1)S(1)}, u32[]{:S(2)}, u32[]{:S(2)}) collective-permute-start(bf16[24,2048]{1,0:T(8,128)(2,1)} %get-tuple-element.74), channel_id=1, source_target_pairs={{0,0},{1,4},{2,8},{3,12},{4,1},{5,5},{6,9},{7,13},{8,2},{9,6},{10,... | collective-permute-start | bytes 294920 | tf_op jit(solution)/shard_map/ppermute | solution.py:824
  30.5 4.2 %grad_left_side.1 = (bf16[96,2048]{1,0:T(8,128)(2,1)S(1)}, bf16[24,2048]{1,0:T(8,128)(2,1)}, bf16[24,2048]{1,0:T(8,128)(2,1)}, bf16[24,2048]{1,0:T(8,128)(2,1)}, bf16[24,2048]{1,0:T(8,128)(2,1)}) custom-call(s32[1]{0:T(128)} %bitcast.sel_ref, s32[1]{0:T(128)} %bitcast.1.me_ref, bf16[2048,2048]{1,0:T(8,128)(2,1)S(1)} %get-tuple-element.55.g_ref, ...), custom_call_target="tpu_custom_call" | custom-call | flops 4000000000 | bytes 1024 | tf_op jit(solution)/shard_map/grad_left_side/pallas_call | solution.py:53
  34.7 3.0 %collective-permute-start.4 = (bf16[24,2048]{1,0:T(8,128)(2,1)}, bf16[24,2048]{1,0:T(8,128)(2,1)S(1)}, u32[]{:S(2)}, u32[]{:S(2)}) collective-permute-start(bf16[24,2048]{1,0:T(8,128)(2,1)} %get-tuple-element.59), channel_id=1, source_target_pairs={{0,2},{1,3},{2,0},{3,1},{4,6},{5,7},{6,4},{7,5},{8,10},{9,11},{10,... | collective-permute-start | bytes 294920 | tf_op jit(solution)/shard_map/ppermute | solution.py:750
  38.6 2.0 %collective-permute-start.8 = (bf16[24,2048]{1,0:T(8,128)(2,1)S(1)}, bf16[24,2048]{1,0:T(8,128)(2,1)S(1)}, u32[]{:S(2)}, u32[]{:S(2)}) collective-permute-start(bf16[24,2048]{1,0:T(8,128)(2,1)S(1)} %copy-done.4), channel_id=1, source_target_pairs={{0,2},{1,6},{2,10},{3,14},{4,3},{5,7},{6,11},{7,15},{8,0},{9,4},{1... | collective-permute-start | bytes 294920 | tf_op jit(solution)/shard_map/ppermute | solution.py:824
  40.5 1.8 %collective-permute-start.9 = (bf16[24,2048]{1,0:T(8,128)(2,1)S(1)}, bf16[24,2048]{1,0:T(8,128)(2,1)S(1)}, u32[]{:S(2)}, u32[]{:S(2)}) collective-permute-start(bf16[24,2048]{1,0:T(8,128)(2,1)S(1)} %copy-done.3), channel_id=1, source_target_pairs={{0,3},{1,7},{2,11},{3,15},{4,0},{5,4},{6,8},{7,12},{8,1},{9,5},{10... | collective-permute-start | bytes 294920 | tf_op jit(solution)/shard_map/ppermute | solution.py:824
  42.3 10.8 %forward.1 = (bf16[64,64,128]{2,1,0:T(8,128)(2,1)}, f32[128,256]{1,0:T(8,128)}, bf16[128,256]{1,0:T(8,128)(2,1)}, bf16[128,256]{1,0:T(8,128)(2,1)}, bf16[128,256]{1,0:T(8,128)(2,1)}) custom-call(s32[1]{0:T(128)} %bitcast.3.me_ref, s32[64,96]{1,0:T(8,128)} %bitcast.16, bf16[2048,96]{1,0:T(8,128)(2,1)S(1)} %get-tuple-element.61.lt_ref, ...), custom_call_target="tpu_custom_call" | custom-call | bytes 1024 | tf_op jit(solution)/shard_map/forward/pallas_call | solution.py:53
  53.2 3.6 %collective-permute-start.12 = (bf16[128,256]{1,0:T(8,128)(2,1)}, bf16[128,256]{1,0:T(8,128)(2,1)S(1)}, u32[]{:S(2)}, u32[]{:S(2)}) collective-permute-start(bf16[128,256]{1,0:T(8,128)(2,1)} %get-tuple-element.80), channel_id=1, source_target_pairs={{0,8},{4,12},{8,0},{12,4},{1,9},{5,13},{9,1},{13,5},{2,10},{6,14},... | collective-permute-start | bytes 196616 | tf_op jit(solution)/shard_map/ppermute | solution.py:750
  56.9 3.3 %tokens.1.rest_0_.rest_4_ = bf16[896,128]{1,0:T(8,128)(2,1)S(1)} custom-call(s32[1]{0:T(128)} %bitcast.1.me_ref, s32[64,96]{1,0:T(8,128)} %bitcast.17, f32[2,6,64,128]{3,2,1,0:T(8,128)} %get-tuple-element.69.stat_ref, bf16[2,48,64,256]{3,2,1,0:T(8,128)(2,1)} %get-tuple-element.54.n_ref, bf16[24,2048]{1,0:T(8,128)(2,1)} %get-tuple-element.70.rest_0_, ...), custom_call_target="tpu_custom_call" | custom-call | bytes 1024 | tf_op jit(solution)/shard_map/tokens/pallas_call | solution.py:53
  61.1 1.1 %cut.1 = (f32[32,256]{1,0:T(8,128)S(1)}, f32[32,256]{1,0:T(8,128)S(1)}, f32[32,256]{1,0:T(8,128)S(1)}, f32[32,256]{1,0:T(8,128)S(1)}) custom-call(s32[1]{0:T(128)} %bitcast.1.me_ref, f32[128,256]{1,0:T(8,128)} %get-tuple-element.78.rest_0_, bf16[128,256]{1,0:T(8,128)(2,1)S(1)} %collective-permute-done.11.rest_1_, ...), custom_call_target="tpu_custom_call" | custom-call | flops 20000000000 | bytes 1024 | tf_op jit(solution)/shard_map/cut/pallas_call | solution.py:53
  62.3 2.2 %collective-permute-start.15 = (f32[32,256]{1,0:T(8,128)S(1)}, f32[32,256]{1,0:T(8,128)S(1)}, u32[]{:S(2)}, u32[]{:S(2)}) collective-permute-start(f32[32,256]{1,0:T(8,128)S(1)} %get-tuple-element.84), channel_id=1, source_target_pairs={{0,2},{1,3},{2,0},{3,1},{4,6},{5,7},{6,4},{7,5},{8,10},{9,11},{10,... | collective-permute-start | bytes 98312 | tf_op jit(solution)/shard_map/ppermute | solution.py:750
  64.5 2.8 %collective-permute-start.16 = (f32[32,256]{1,0:T(8,128)S(1)}, f32[32,256]{1,0:T(8,128)S(1)}, u32[]{:S(2)}, u32[]{:S(2)}) collective-permute-start(f32[32,256]{1,0:T(8,128)S(1)} %get-tuple-element.85), channel_id=1, source_target_pairs={{0,3},{1,0},{2,1},{3,2},{4,7},{5,4},{6,5},{7,6},{8,11},{9,8},{10,9... | collective-permute-start | bytes 98312 | tf_op jit(solution)/shard_map/ppermute | solution.py:750
  67.3 6.5 %collective-permute-done.20.rest_6_.rest_2_ = bf16[896,128]{1,0:T(8,128)(2,1)S(1)} collective-permute-done((bf16[896,128]{1,0:T(8,128)(2,1)S(1)}, bf16[896,128]{1,0:T(8,128)(2,1)S(1)}, u32[]{:S(2)}, u32[]{:S(2)}) %collective-permute-start.20) | collective-permute-done | bytes 229408 | tf_op jit(solution)/shard_map/ppermute | solution.py:759
  74.5 2.3 %collective-permute-start.19 = (f32[32,256]{1,0:T(8,128)S(1)}, f32[32,256]{1,0:T(8,128)S(1)}, u32[]{:S(2)}, u32[]{:S(2)}) collective-permute-start(f32[32,256]{1,0:T(8,128)S(1)} %add_add_fusion.rest_0_), channel_id=1, source_target_pairs={{0,3},{1,0},{2,1},{3,2},{4,7},{5,4},{6,5},{7,6},{8,11},{9,8},{10,9... | collective-permute-start | bytes 98312 | tf_op jit(solution)/shard_map/ppermute | solution.py:750
  79.4 2.8 %finish.2.rest_4_ = bf16[96,64,256]{2,1,0:T(8,128)(2,1)} custom-call(s32[1]{0:T(128)} %bitcast.1.me_ref, bf16[2,48,64,256]{3,2,1,0:T(8,128)(2,1)S(1)} %copy-done.2, bf16[32,256]{1,0:T(8,128)(2,1)} %bitcast.23, bf16[32,256]{1,0:T(8,128)(2,1)} %bitcast.26, f32[1,256]{1,0:T(1,128)} %bitcast.30, bf16[896,128]{1,0:T(8,128)(2,1)S(1)} %tokens.1.rest_0_.rest_4_, ...), custom_call_target="tpu_custom_call" | custom-call | flops 2000000000 | bytes 1024 | tf_op jit(solution)/shard_map/finish/pallas_call | solution.py:639
  82.3 4.0 %collective-permute-done.19.rest_3_ = f32[32,256]{1,0:T(8,128)S(1)} collective-permute-done((f32[32,256]{1,0:T(8,128)S(1)}, f32[32,256]{1,0:T(8,128)S(1)}, u32[]{:S(2)}, u32[]{:S(2)}) %collective-permute-start.19) | collective-permute-done | bytes 32800 | tf_op jit(solution)/shard_map/ppermute | solution.py:750
  87.0 1.6 %collective-permute-start.23 = (bf16[192,256]{1,0:T(8,128)(2,1)}, bf16[192,256]{1,0:T(8,128)(2,1)S(1)}, u32[]{:S(2)}, u32[]{:S(2)}) collective-permute-start(bf16[192,256]{1,0:T(8,128)(2,1)} %join_send.1.rest_0_), channel_id=1, source_target_pairs={{0,8},{4,12},{8,0},{12,4},{1,9},{5,13},{9,1},{13,5},{2,10},{6,14},... | collective-permute-start | bytes 294920 | tf_op jit(solution)/shard_map/ppermute | solution.py:750
  88.6 2.9 %finish.3 = bf16[96,64,256]{2,1,0:T(8,128)(2,1)} custom-call(s32[1]{0:T(128)} %bitcast.1.me_ref, bf16[2,48,64,256]{3,2,1,0:T(8,128)(2,1)S(1)} %copy-done.2, bf16[32,256]{1,0:T(8,128)(2,1)} %bitcast.24, bf16[32,256]{1,0:T(8,128)(2,1)} %bitcast.27, f32[1,256]{1,0:T(1,128)} %bitcast.31, ...), custom_call_target="tpu_custom_call", output_to_operand_aliasing={{}: (9, {})} | custom-call | flops 6000000000 | bytes 1024 | tf_op jit(solution)/shard_map/finish/pallas_call | solution.py:639
  91.5 3.0 %collective-permute-done.23.rest_2_ = bf16[192,256]{1,0:T(8,128)(2,1)S(1)} collective-permute-done((bf16[192,256]{1,0:T(8,128)(2,1)}, bf16[192,256]{1,0:T(8,128)(2,1)S(1)}, u32[]{:S(2)}, u32[]{:S(2)}) %collective-permute-start.23) | collective-permute-done | bytes 98336 | tf_op jit(solution)/shard_map/ppermute | solution.py:750
  94.5 2.0 %join_out.1 = (f32[1024,128]{1,0:T(8,128)}, f32[32,256]{1,0:T(8,128)}, f32[32,256]{1,0:T(8,128)}) custom-call(s32[1]{0:T(128)} %bitcast.3.me_ref, bf16[192,256]{1,0:T(8,128)(2,1)} %join_send.1.rest_0_, bf16[192,256]{1,0:T(8,128)(2,1)S(1)} %collective-permute-done.22.rest_1_, bf16[192,256]{1,0:T(8,128)(2,1)S(1)} %collective-permute-done.23.rest_2_, ...), custom_call_target="tpu_custom_call" | custom-call | bytes 1024 | tf_op jit(solution)/shard_map/join_out/pallas_call | solution.py:53
  (47 shorter events, 6.6 us)
Async XLA Ops:
  0.6 9.1 %collective-permute-start = (s32[64,96]{1,0:T(8,128)}, s32[64,96]{1,0:T(8,128)S(1)}, u32[]{:S(2)}, u32[]{:S(2)}) collective-permute-start(s32[64,96]{1,0:T(8,128)} %bitcast.13), channel_id=1, source_target_pairs={{1,4},{2,8},{3,12},{6,9},{7,13},{4,1},{11,14},{8,2},{9,6},{12,3},{... | collective-permute-start | bytes 73736 | tf_op jit(solution)/shard_map/ppermute | solution.py:779
  9.8 20.7 %collective-permute-start.2 = (bf16[96,2048]{1,0:T(8,128)(2,1)}, bf16[96,2048]{1,0:T(8,128)(2,1)S(1)}, u32[]{:S(2)}, u32[]{:S(2)}) collective-permute-start(bf16[96,2048]{1,0:T(8,128)(2,1)} %get-tuple-element.56.rest_0_), channel_id=1, source_target_pairs={{0,12},{5,9},{10,6},{15,3},{16,28},{21,25},{26,22},{31,19}} | collective-permute-start | bytes 1179656 | tf_op jit(solution)/shard_map/ppermute | solution.py:791
  19.2 11.3 %collective-permute-start.1 = (bf16[96,2048]{1,0:T(8,128)(2,1)}, bf16[96,2048]{1,0:T(8,128)(2,1)S(1)}, u32[]{:S(2)}, u32[]{:S(2)}) collective-permute-start(bf16[96,2048]{1,0:T(8,128)(2,1)} %get-tuple-element.56.rest_0_), channel_id=1, source_target_pairs={{0,8},{5,13},{10,2},{15,7},{1,4},{4,1},{11,14},{14,11},{16,24},{21... | collective-permute-start | bytes 1179656 | tf_op jit(solution)/shard_map/ppermute | solution.py:791
  28.9 9.6 %collective-permute-start.6 = (bf16[24,2048]{1,0:T(8,128)(2,1)}, bf16[24,2048]{1,0:T(8,128)(2,1)S(1)}, u32[]{:S(2)}, u32[]{:S(2)}) collective-permute-start(bf16[24,2048]{1,0:T(8,128)(2,1)} %get-tuple-element.74), channel_id=1, source_target_pairs={{0,0},{1,4},{2,8},{3,12},{4,1},{5,5},{6,9},{7,13},{8,2},{9,6},{10,... | collective-permute-start | bytes 294920 | tf_op jit(solution)/shard_map/ppermute | solution.py:824
  30.5 10.1 %collective-permute-start.7 = (bf16[24,2048]{1,0:T(8,128)(2,1)}, bf16[24,2048]{1,0:T(8,128)(2,1)S(1)}, u32[]{:S(2)}, u32[]{:S(2)}) collective-permute-start(bf16[24,2048]{1,0:T(8,128)(2,1)} %get-tuple-element.75), channel_id=1, source_target_pairs={{0,1},{1,5},{2,9},{3,13},{4,2},{5,6},{6,10},{7,14},{8,3},{9,7},{10... | collective-permute-start | bytes 294920 | tf_op jit(solution)/shard_map/ppermute | solution.py:824
  34.7 18.5 %collective-permute-start.3 = (bf16[24,2048]{1,0:T(8,128)(2,1)}, bf16[24,2048]{1,0:T(8,128)(2,1)S(1)}, u32[]{:S(2)}, u32[]{:S(2)}) collective-permute-start(bf16[24,2048]{1,0:T(8,128)(2,1)} %get-tuple-element.58), channel_id=1, source_target_pairs={{0,1},{1,2},{2,3},{3,0},{4,5},{5,6},{6,7},{7,4},{8,9},{9,10},{10,1... | collective-permute-start | bytes 294920 | tf_op jit(solution)/shard_map/ppermute | solution.py:750
  34.7 18.6 %collective-permute-start.4 = (bf16[24,2048]{1,0:T(8,128)(2,1)}, bf16[24,2048]{1,0:T(8,128)(2,1)S(1)}, u32[]{:S(2)}, u32[]{:S(2)}) collective-permute-start(bf16[24,2048]{1,0:T(8,128)(2,1)} %get-tuple-element.59), channel_id=1, source_target_pairs={{0,2},{1,3},{2,0},{3,1},{4,6},{5,7},{6,4},{7,5},{8,10},{9,11},{10,... | collective-permute-start | bytes 294920 | tf_op jit(solution)/shard_map/ppermute | solution.py:750
  37.7 19.2 %collective-permute-start.5 = (bf16[24,2048]{1,0:T(8,128)(2,1)}, bf16[24,2048]{1,0:T(8,128)(2,1)S(1)}, u32[]{:S(2)}, u32[]{:S(2)}) collective-permute-start(bf16[24,2048]{1,0:T(8,128)(2,1)} %get-tuple-element.60), channel_id=1, source_target_pairs={{0,3},{1,0},{2,1},{3,2},{4,7},{5,4},{6,5},{7,6},{8,11},{9,8},{10,9... | collective-permute-start | bytes 294920 | tf_op jit(solution)/shard_map/ppermute | solution.py:750
  38.6 18.3 %collective-permute-start.8 = (bf16[24,2048]{1,0:T(8,128)(2,1)S(1)}, bf16[24,2048]{1,0:T(8,128)(2,1)S(1)}, u32[]{:S(2)}, u32[]{:S(2)}) collective-permute-start(bf16[24,2048]{1,0:T(8,128)(2,1)S(1)} %copy-done.4), channel_id=1, source_target_pairs={{0,2},{1,6},{2,10},{3,14},{4,3},{5,7},{6,11},{7,15},{8,0},{9,4},{1... | collective-permute-start | bytes 294920 | tf_op jit(solution)/shard_map/ppermute | solution.py:824
  40.5 16.3 %collective-permute-start.9 = (bf16[24,2048]{1,0:T(8,128)(2,1)S(1)}, bf16[24,2048]{1,0:T(8,128)(2,1)S(1)}, u32[]{:S(2)}, u32[]{:S(2)}) collective-permute-start(bf16[24,2048]{1,0:T(8,128)(2,1)S(1)} %copy-done.3), channel_id=1, source_target_pairs={{0,3},{1,7},{2,11},{3,15},{4,0},{5,4},{6,8},{7,12},{8,1},{9,5},{10... | collective-permute-start | bytes 294920 | tf_op jit(solution)/shard_map/ppermute | solution.py:824
  53.2 7.9 %collective-permute-start.11 = (bf16[128,256]{1,0:T(8,128)(2,1)}, bf16[128,256]{1,0:T(8,128)(2,1)S(1)}, u32[]{:S(2)}, u32[]{:S(2)}) collective-permute-start(bf16[128,256]{1,0:T(8,128)(2,1)} %get-tuple-element.79), channel_id=1, source_target_pairs={{0,4},{4,8},{8,12},{12,0},{1,5},{5,9},{9,13},{13,1},{2,6},{6,10},{... | collective-permute-start | bytes 196616 | tf_op jit(solution)/shard_map/ppermute | solution.py:750
  53.2 7.9 %collective-permute-start.12 = (bf16[128,256]{1,0:T(8,128)(2,1)}, bf16[128,256]{1,0:T(8,128)(2,1)S(1)}, u32[]{:S(2)}, u32[]{:S(2)}) collective-permute-start(bf16[128,256]{1,0:T(8,128)(2,1)} %get-tuple-element.80), channel_id=1, source_target_pairs={{0,8},{4,12},{8,0},{12,4},{1,9},{5,13},{9,1},{13,5},{2,10},{6,14},... | collective-permute-start | bytes 196616 | tf_op jit(solution)/shard_map/ppermute | solution.py:750
  60.2 13.6 %collective-permute-start.20 = (bf16[896,128]{1,0:T(8,128)(2,1)S(1)}, bf16[896,128]{1,0:T(8,128)(2,1)S(1)}, u32[]{:S(2)}, u32[]{:S(2)}) collective-permute-start(bf16[896,128]{1,0:T(8,128)(2,1)S(1)} %tokens.1.rest_0_.rest_4_), channel_id=1, source_target_pairs={{0,2},{1,3},{2,0},{3,1},{4,6},{5,7},{6,4},{7,5},{8,10},{9,11},{10,... | collective-permute-start | bytes 688136 | tf_op jit(solution)/shard_map/ppermute | solution.py:759
  62.2 11.6 %collective-permute-start.14 = (f32[32,256]{1,0:T(8,128)S(1)}, f32[32,256]{1,0:T(8,128)S(1)}, u32[]{:S(2)}, u32[]{:S(2)}) collective-permute-start(f32[32,256]{1,0:T(8,128)S(1)} %get-tuple-element.83), channel_id=1, source_target_pairs={{0,1},{1,2},{2,3},{3,0},{4,5},{5,6},{6,7},{7,4},{8,9},{9,10},{10,1... | collective-permute-start | bytes 98312 | tf_op jit(solution)/shard_map/ppermute | solution.py:750
  62.3 12.2 %collective-permute-start.15 = (f32[32,256]{1,0:T(8,128)S(1)}, f32[32,256]{1,0:T(8,128)S(1)}, u32[]{:S(2)}, u32[]{:S(2)}) collective-permute-start(f32[32,256]{1,0:T(8,128)S(1)} %get-tuple-element.84), channel_id=1, source_target_pairs={{0,2},{1,3},{2,0},{3,1},{4,6},{5,7},{6,4},{7,5},{8,10},{9,11},{10,... | collective-permute-start | bytes 98312 | tf_op jit(solution)/shard_map/ppermute | solution.py:750
  64.5 10.0 %collective-permute-start.16 = (f32[32,256]{1,0:T(8,128)S(1)}, f32[32,256]{1,0:T(8,128)S(1)}, u32[]{:S(2)}, u32[]{:S(2)}) collective-permute-start(f32[32,256]{1,0:T(8,128)S(1)} %get-tuple-element.85), channel_id=1, source_target_pairs={{0,3},{1,0},{2,1},{3,2},{4,7},{5,4},{6,5},{7,6},{8,11},{9,8},{10,9... | collective-permute-start | bytes 98312 | tf_op jit(solution)/shard_map/ppermute | solution.py:750
  67.3 12.1 %collective-permute-start.10 = (bf16[896,128]{1,0:T(8,128)(2,1)S(1)}, bf16[896,128]{1,0:T(8,128)(2,1)S(1)}, u32[]{:S(2)}, u32[]{:S(2)}) collective-permute-start(bf16[896,128]{1,0:T(8,128)(2,1)S(1)} %tokens.1.rest_0_.rest_4_), channel_id=1, source_target_pairs={{0,1},{1,0},{2,3},{3,2},{4,5},{5,4},{6,7},{7,6},{8,9},{9,8},{10,11... | collective-permute-start | bytes 688136 | tf_op jit(solution)/shard_map/ppermute | solution.py:759
  73.8 12.5 %collective-permute-start.21 = (bf16[896,128]{1,0:T(8,128)(2,1)S(1)}, bf16[896,128]{1,0:T(8,128)(2,1)S(1)}, u32[]{:S(2)}, u32[]{:S(2)}) collective-permute-start(bf16[896,128]{1,0:T(8,128)(2,1)S(1)} %collective-permute-done.20.rest_6_.rest_2_), channel_id=1, source_target_pairs={{0,1},{1,0},{2,3},{3,2},{4,5},{5,4},{6,7},{7,6},{8,9},{9,8},{10,11... | collective-permute-start | bytes 688136 | tf_op jit(solution)/shard_map/ppermute | solution.py:759
  74.5 11.8 %collective-permute-start.19 = (f32[32,256]{1,0:T(8,128)S(1)}, f32[32,256]{1,0:T(8,128)S(1)}, u32[]{:S(2)}, u32[]{:S(2)}) collective-permute-start(f32[32,256]{1,0:T(8,128)S(1)} %add_add_fusion.rest_0_), channel_id=1, source_target_pairs={{0,3},{1,0},{2,1},{3,2},{4,7},{5,4},{6,5},{7,6},{8,11},{9,8},{10,9... | collective-permute-start | bytes 98312 | tf_op jit(solution)/shard_map/ppermute | solution.py:750
  76.8 9.5 %collective-permute-start.18 = (f32[32,256]{1,0:T(8,128)S(1)}, f32[32,256]{1,0:T(8,128)S(1)}, u32[]{:S(2)}, u32[]{:S(2)}) collective-permute-start(f32[32,256]{1,0:T(8,128)S(1)} %add_add_fusion.rest_0_), channel_id=1, source_target_pairs={{0,2},{1,3},{2,0},{3,1},{4,6},{5,7},{6,4},{7,5},{8,10},{9,11},{10,... | collective-permute-start | bytes 98312 | tf_op jit(solution)/shard_map/ppermute | solution.py:750
  77.4 8.9 %collective-permute-start.17 = (f32[32,256]{1,0:T(8,128)S(1)}, f32[32,256]{1,0:T(8,128)S(1)}, u32[]{:S(2)}, u32[]{:S(2)}) collective-permute-start(f32[32,256]{1,0:T(8,128)S(1)} %add_add_fusion.rest_0_), channel_id=1, source_target_pairs={{0,1},{1,2},{2,3},{3,0},{4,5},{5,6},{6,7},{7,4},{8,9},{9,10},{10,1... | collective-permute-start | bytes 98312 | tf_op jit(solution)/shard_map/ppermute | solution.py:750
  87.0 4.5 %collective-permute-start.24 = (bf16[192,256]{1,0:T(8,128)(2,1)}, bf16[192,256]{1,0:T(8,128)(2,1)S(1)}, u32[]{:S(2)}, u32[]{:S(2)}) collective-permute-start(bf16[192,256]{1,0:T(8,128)(2,1)} %join_send.1.rest_0_), channel_id=1, source_target_pairs={{0,12},{4,0},{8,4},{12,8},{1,13},{5,1},{9,5},{13,9},{2,14},{6,2},{... | collective-permute-start | bytes 294920 | tf_op jit(solution)/shard_map/ppermute | solution.py:750
  87.0 7.5 %collective-permute-start.23 = (bf16[192,256]{1,0:T(8,128)(2,1)}, bf16[192,256]{1,0:T(8,128)(2,1)S(1)}, u32[]{:S(2)}, u32[]{:S(2)}) collective-permute-start(bf16[192,256]{1,0:T(8,128)(2,1)} %join_send.1.rest_0_), channel_id=1, source_target_pairs={{0,8},{4,12},{8,0},{12,4},{1,9},{5,13},{9,1},{13,5},{2,10},{6,14},... | collective-permute-start | bytes 294920 | tf_op jit(solution)/shard_map/ppermute | solution.py:750
  88.6 5.9 %collective-permute-start.22 = (bf16[192,256]{1,0:T(8,128)(2,1)}, bf16[192,256]{1,0:T(8,128)(2,1)S(1)}, u32[]{:S(2)}, u32[]{:S(2)}) collective-permute-start(bf16[192,256]{1,0:T(8,128)(2,1)} %join_send.1.rest_0_), channel_id=1, source_target_pairs={{0,4},{4,8},{8,12},{12,0},{1,5},{5,9},{9,13},{13,1},{2,6},{6,10},{... | collective-permute-start | bytes 294920 | tf_op jit(solution)/shard_map/ppermute | solution.py:750
  (6 other events, 52.3 us)

commit v5 on v4

--- a/solution.py
+++ b/solution.py
@@ -12,7 +12,7 @@
 TN = (((0,), (0,)), ((), ()))
 VMEM = 64 * 1024 * 1024
 COST = {'grad_outer_right': 4, 'grad_left_side': 4, 'cut': 20, 'finish_a': 2, 'finish_b': 6, 'join_send': 2, 'project': 1}
-IBLK = 8
+IBLK = 32
 
 
 def params(vmem=VMEM):
@@ -147,7 +147,7 @@
         ],
         [
             (tile, sent((2, half, rows, chans))),
-            (tile, kept((2, half, rows, chans))),
+            (tile, sent((2, half, rows, chans))),
             (
                 pl.BlockSpec((2, blk // 8, rows, 128), lambda n: (0, n, 0, 0)),
                 sent((2, half // 8, rows, 128), F32),
@@ -664,7 +664,7 @@
             bytes_accessed=1024,
             transcendentals=0,
         ),
-    )(me, *near(xhat), *far(wl_t, wr_t, gain[None, :]), *qs, *given)
+    )(me, *far(xhat, wl_t, wr_t, gain[None, :]), *qs, *given)
 
 
 def join_send(me, parts, qs, nar2):

time: 97.1 us -> 94.1 us (0.969)
  local copies, waits for them, and re-layouts: 1.65 us -> 0.01 us
    unnamed x10 -> x6, local copies, waits for them, and re-layouts: 1.65 us -> 0.01 us
    pallas_call x8, Pallas kernels: 37.3 us -> 35.9 us  [call(): pl.pallas_call(kernel, name=name, grid_spec=pltpu.PrefetchScalarGridSpec(...]
  transfers between devices with their start and end apart: 25 -> 25, of which waited for: 5 -> 5; matrix products, arithmetic and copies ran while one was open for 0% -> 0% of each run, Pallas kernels for 42% -> 43%
where the time goes in v5:
time: 94.1 us; the launch traced here: 93.6 us
  Pallas kernels  42.5 us (45%)
  starting transfers between devices  35.6 us (38%)
  waiting for transfers between devices  14.6 us (16%)
    pallas_call x8, Pallas kernels, call(): pl.pallas_call(kernel, name=name, grid_spec=pltpu.PrefetchScalarGridSpec(...  35.9 us
    ppermute x15, starting transfers between devices, shift(): return lax.ppermute(value, axis, [(k, (k + t) % n) for k in range(n)])  18.1 us
    ppermute x1, starting transfers between devices, spread(): lax.ppermute(value, BOTH, second)  9.42 us
    ppermute x3, waiting for transfers between devices, swap(): return lax.ppermute(value, axis, [(k, k ^ t) for k in range(n)])  7.73 us
    ppermute x15, waiting for transfers between devices, shift(): return lax.ppermute(value, axis, [(k, (k + t) % n) for k in range(n)])  6.88 us
    pallas_call x2, Pallas kernels, finish(): pl.pallas_call(kernel, name='finish', grid_spec=pltpu.PrefetchScalarGridS...  6.55 us
    ppermute x4, starting transfers between devices, to_owners(): parts.append(lax.ppermute(piece, BOTH, pairs))  5.3 us
  transfers between devices with their start and end apart: 25, of which 5 were waited for; matrix products, arithmetic and copies ran while one was open for 0% of the time, Pallas kernels for 43%

profile of v5, /device:TPU:0, one launch (start us, length us, event | category | flops | bytes accessed | tf_op | source)
XLA Modules:
  0.0 93.6 jit_solution(10083783536458853594)
XLA Ops:
  1.3 7.5 %project.1 = (bf16[2,48,64,256]{3,2,1,0:T(8,128)(2,1)}, bf16[2,48,64,256]{3,2,1,0:T(8,128)(2,1)}, f32[2,6,64,128]{3,2,1,0:T(8,128)}, bf16[96,2048]{1,0:T(8,128)(2,1)}) custom-call(s32[64,96]{1,0:T(8,128)} %bitcast.14, bf16[2,48,64,256]{3,2,1,0:T(8,128)(2,1)} %bitcast.19, f32[1,256]{1,0:T(1,128)} %bitcast.29, f32[1,256]{1,0:T(1,128)} %bitcast.28, ...), custom_call_target="tpu_custom_call" | custom-call | flops 1000000000 | bytes 1024 | tf_op jit(solution)/shard_map/project/pallas_call | solution.py:53
  8.8 9.4 %collective-permute-start.2 = (bf16[96,2048]{1,0:T(8,128)(2,1)}, bf16[96,2048]{1,0:T(8,128)(2,1)S(1)}, u32[]{:S(2)}, u32[]{:S(2)}) collective-permute-start(bf16[96,2048]{1,0:T(8,128)(2,1)} %get-tuple-element.56.rest_0_), channel_id=1, source_target_pairs={{0,12},{5,9},{10,6},{15,3},{16,28},{21,25},{26,22},{31,19}} | collective-permute-start | bytes 1179656 | tf_op jit(solution)/shard_map/ppermute | solution.py:791
  18.2 1.3 %collective-permute-start.1 = (bf16[96,2048]{1,0:T(8,128)(2,1)}, bf16[96,2048]{1,0:T(8,128)(2,1)S(1)}, u32[]{:S(2)}, u32[]{:S(2)}) collective-permute-start(bf16[96,2048]{1,0:T(8,128)(2,1)} %get-tuple-element.56.rest_0_), channel_id=1, source_target_pairs={{0,8},{5,13},{10,2},{15,7},{1,4},{4,1},{11,14},{14,11},{16,24},{21... | collective-permute-start | bytes 1179656 | tf_op jit(solution)/shard_map/ppermute | solution.py:791
  19.6 8.4 %grad_outer_right.1 = (bf16[64,64,128]{2,1,0:T(8,128)(2,1)S(1)}, bf16[2048,2048]{1,0:T(8,128)(2,1)S(1)}, bf16[512,256]{1,0:T(8,128)(2,1)S(1)}, bf16[2048,96]{1,0...) custom-call(s32[1]{0:T(128)} %bitcast.2.own_ref, ...), custom_call_target="tpu_custom_call" | custom-call | flops 4000000000 | bytes 1024 | tf_op jit(solution)/shard_map/grad_outer_right/pallas_call | solution.py:53
  28.0 1.5 %collective-permute-start.6 = (bf16[24,2048]{1,0:T(8,128)(2,1)}, bf16[24,2048]{1,0:T(8,128)(2,1)S(1)}, u32[]{:S(2)}, u32[]{:S(2)}) collective-permute-start(bf16[24,2048]{1,0:T(8,128)(2,1)} %get-tuple-element.74), channel_id=1, source_target_pairs={{0,0},{1,4},{2,8},{3,12},{4,1},{5,5},{6,9},{7,13},{8,2},{9,6},{10,... | collective-permute-start | bytes 294920 | tf_op jit(solution)/shard_map/ppermute | solution.py:824
  29.5 4.1 %grad_left_side.1 = (bf16[96,2048]{1,0:T(8,128)(2,1)S(1)}, bf16[24,2048]{1,0:T(8,128)(2,1)}, bf16[24,2048]{1,0:T(8,128)(2,1)}, bf16[24,2048]{1,0:T(8,128)(2,1)}, bf16[24,2048]{1,0:T(8,128)(2,1)}) custom-call(s32[1]{0:T(128)} %bitcast.sel_ref, s32[1]{0:T(128)} %bitcast.1.me_ref, bf16[2048,2048]{1,0:T(8,128)(2,1)S(1)} %get-tuple-element.55.g_ref, ...), custom_call_target="tpu_custom_call" | custom-call | flops 4000000000 | bytes 1024 | tf_op jit(solution)/shard_map/grad_left_side/pallas_call | solution.py:53
  33.7 3.0 %collective-permute-start.4 = (bf16[24,2048]{1,0:T(8,128)(2,1)}, bf16[24,2048]{1,0:T(8,128)(2,1)S(1)}, u32[]{:S(2)}, u32[]{:S(2)}) collective-permute-start(bf16[24,2048]{1,0:T(8,128)(2,1)} %get-tuple-element.59), channel_id=1, source_target_pairs={{0,2},{1,3},{2,0},{3,1},{4,6},{5,7},{6,4},{7,5},{8,10},{9,11},{10,... | collective-permute-start | bytes 294920 | tf_op jit(solution)/shard_map/ppermute | solution.py:750
  37.6 2.0 %collective-permute-start.8 = (bf16[24,2048]{1,0:T(8,128)(2,1)S(1)}, bf16[24,2048]{1,0:T(8,128)(2,1)S(1)}, u32[]{:S(2)}, u32[]{:S(2)}) collective-permute-start(bf16[24,2048]{1,0:T(8,128)(2,1)S(1)} %copy-done.2), channel_id=1, source_target_pairs={{0,2},{1,6},{2,10},{3,14},{4,3},{5,7},{6,11},{7,15},{8,0},{9,4},{1... | collective-permute-start | bytes 294920 | tf_op jit(solution)/shard_map/ppermute | solution.py:824
  39.6 1.8 %collective-permute-start.9 = (bf16[24,2048]{1,0:T(8,128)(2,1)S(1)}, bf16[24,2048]{1,0:T(8,128)(2,1)S(1)}, u32[]{:S(2)}, u32[]{:S(2)}) collective-permute-start(bf16[24,2048]{1,0:T(8,128)(2,1)S(1)} %copy-done.1), channel_id=1, source_target_pairs={{0,3},{1,7},{2,11},{3,15},{4,0},{5,4},{6,8},{7,12},{8,1},{9,5},{10... | collective-permute-start | bytes 294920 | tf_op jit(solution)/shard_map/ppermute | solution.py:824
  41.4 9.0 %forward.1 = (bf16[64,64,128]{2,1,0:T(8,128)(2,1)}, f32[128,256]{1,0:T(8,128)}, bf16[128,256]{1,0:T(8,128)(2,1)}, bf16[128,256]{1,0:T(8,128)(2,1)}, bf16[128,256]{1,0:T(8,128)(2,1)}) custom-call(s32[1]{0:T(128)} %bitcast.3.me_ref, s32[64,96]{1,0:T(8,128)} %bitcast.16, bf16[2048,96]{1,0:T(8,128)(2,1)S(1)} %get-tuple-element.61.lt_ref, ...), custom_call_target="tpu_custom_call" | custom-call | bytes 1024 | tf_op jit(solution)/shard_map/forward/pallas_call | solution.py:53
  50.4 3.6 %collective-permute-start.12 = (bf16[128,256]{1,0:T(8,128)(2,1)}, bf16[128,256]{1,0:T(8,128)(2,1)S(1)}, u32[]{:S(2)}, u32[]{:S(2)}) collective-permute-start(bf16[128,256]{1,0:T(8,128)(2,1)} %get-tuple-element.80), channel_id=1, source_target_pairs={{0,8},{4,12},{8,0},{12,4},{1,9},{5,13},{9,1},{13,5},{2,10},{6,14},... | collective-permute-start | bytes 196616 | tf_op jit(solution)/shard_map/ppermute | solution.py:750
  54.1 3.3 %tokens.1.rest_0_.rest_4_ = bf16[896,128]{1,0:T(8,128)(2,1)S(1)} custom-call(s32[1]{0:T(128)} %bitcast.1.me_ref, s32[64,96]{1,0:T(8,128)} %bitcast.17, f32[2,6,64,128]{3,2,1,0:T(8,128)} %get-tuple-element.69.stat_ref, bf16[2,48,64,256]{3,2,1,0:T(8,128)(2,1)} %get-tuple-element.54.n_ref, bf16[24,2048]{1,0:T(8,128)(2,1)} %get-tuple-element.70.rest_0_, ...), custom_call_target="tpu_custom_call" | custom-call | bytes 1024 | tf_op jit(solution)/shard_map/tokens/pallas_call | solution.py:53
  59.3 2.2 %collective-permute-start.15 = (f32[32,256]{1,0:T(8,128)S(1)}, f32[32,256]{1,0:T(8,128)S(1)}, u32[]{:S(2)}, u32[]{:S(2)}) collective-permute-start(f32[32,256]{1,0:T(8,128)S(1)} %get-tuple-element.84), channel_id=1, source_target_pairs={{0,2},{1,3},{2,0},{3,1},{4,6},{5,7},{6,4},{7,5},{8,10},{9,11},{10,... | collective-permute-start | bytes 98312 | tf_op jit(solution)/shard_map/ppermute | solution.py:750
  61.5 2.8 %collective-permute-start.16 = (f32[32,256]{1,0:T(8,128)S(1)}, f32[32,256]{1,0:T(8,128)S(1)}, u32[]{:S(2)}, u32[]{:S(2)}) collective-permute-start(f32[32,256]{1,0:T(8,128)S(1)} %get-tuple-element.85), channel_id=1, source_target_pairs={{0,3},{1,0},{2,1},{3,2},{4,7},{5,4},{6,5},{7,6},{8,11},{9,8},{10,9... | collective-permute-start | bytes 98312 | tf_op jit(solution)/shard_map/ppermute | solution.py:750
  64.4 6.7 %collective-permute-done.20.rest_6_.rest_2_ = bf16[896,128]{1,0:T(8,128)(2,1)S(1)} collective-permute-done((bf16[896,128]{1,0:T(8,128)(2,1)S(1)}, bf16[896,128]{1,0:T(8,128)(2,1)S(1)}, u32[]{:S(2)}, u32[]{:S(2)}) %collective-permute-start.20) | collective-permute-done | bytes 229408 | tf_op jit(solution)/shard_map/ppermute | solution.py:759
  71.7 2.3 %collective-permute-start.19 = (f32[32,256]{1,0:T(8,128)S(1)}, f32[32,256]{1,0:T(8,128)S(1)}, u32[]{:S(2)}, u32[]{:S(2)}) collective-permute-start(f32[32,256]{1,0:T(8,128)S(1)} %add_add_fusion.rest_0_), channel_id=1, source_target_pairs={{0,3},{1,0},{2,1},{3,2},{4,7},{5,4},{6,5},{7,6},{8,11},{9,8},{10,9... | collective-permute-start | bytes 98312 | tf_op jit(solution)/shard_map/ppermute | solution.py:750
  74.6 1.0 %collective-permute-start.17 = (f32[32,256]{1,0:T(8,128)S(1)}, f32[32,256]{1,0:T(8,128)S(1)}, u32[]{:S(2)}, u32[]{:S(2)}) collective-permute-start(f32[32,256]{1,0:T(8,128)S(1)} %add_add_fusion.rest_0_), channel_id=1, source_target_pairs={{0,1},{1,2},{2,3},{3,0},{4,5},{5,6},{6,7},{7,4},{8,9},{9,10},{10,1... | collective-permute-start | bytes 98312 | tf_op jit(solution)/shard_map/ppermute | solution.py:750
  75.6 1.0 %collective-permute-done.10.rest_1_.rest_5_ = bf16[896,128]{1,0:T(8,128)(2,1)S(1)} collective-permute-done((bf16[896,128]{1,0:T(8,128)(2,1)S(1)}, bf16[896,128]{1,0:T(8,128)(2,1)S(1)}, u32[]{:S(2)}, u32[]{:S(2)}) %collective-permute-start.10) | collective-permute-done | bytes 229408 | tf_op jit(solution)/shard_map/ppermute | solution.py:759
  76.6 3.3 %finish.2.rest_4_ = bf16[96,64,256]{2,1,0:T(8,128)(2,1)} custom-call(s32[1]{0:T(128)} %bitcast.1.me_ref, bf16[2,48,64,256]{3,2,1,0:T(8,128)(2,1)} %get-tuple-element.68.x_ref, bf16[32,256]{1,0:T(8,128)(2,1)} %bitcast.23, bf16[32,256]{1,0:T(8,128)(2,1)} %bitcast.26, f32[1,256]{1,0:T(1,128)} %bitcast.30, bf16[896,128]{1,0:T(8,128)(2,1)S(1)} %tokens.1.rest_0_.rest_4_, ...), custom_call_target="tpu_custom_call" | custom-call | flops 2000000000 | bytes 1024 | tf_op jit(solution)/shard_map/finish/pallas_call | solution.py:639
  79.9 3.5 %collective-permute-done.19.rest_3_ = f32[32,256]{1,0:T(8,128)S(1)} collective-permute-done((f32[32,256]{1,0:T(8,128)S(1)}, f32[32,256]{1,0:T(8,128)S(1)}, u32[]{:S(2)}, u32[]{:S(2)}) %collective-permute-start.19) | collective-permute-done | bytes 32800 | tf_op jit(solution)/shard_map/ppermute | solution.py:750
  84.1 1.5 %collective-permute-start.23 = (bf16[192,256]{1,0:T(8,128)(2,1)}, bf16[192,256]{1,0:T(8,128)(2,1)S(1)}, u32[]{:S(2)}, u32[]{:S(2)}) collective-permute-start(bf16[192,256]{1,0:T(8,128)(2,1)} %join_send.1.rest_0_), channel_id=1, source_target_pairs={{0,8},{4,12},{8,0},{12,4},{1,9},{5,13},{9,1},{13,5},{2,10},{6,14},... | collective-permute-start | bytes 294920 | tf_op jit(solution)/shard_map/ppermute | solution.py:750
  85.6 3.3 %finish.3 = bf16[96,64,256]{2,1,0:T(8,128)(2,1)} custom-call(s32[1]{0:T(128)} %bitcast.1.me_ref, bf16[2,48,64,256]{3,2,1,0:T(8,128)(2,1)} %get-tuple-element.68.x_ref, bf16[32,256]{1,0:T(8,128)(2,1)} %bitcast.24, bf16[32,256]{1,0:T(8,128)(2,1)} %bitcast.27, f32[1,256]{1,0:T(1,128)} %bitcast.31, ...), custom_call_target="tpu_custom_call", output_to_operand_aliasing={{}: (9, {})} | custom-call | flops 6000000000 | bytes 1024 | tf_op jit(solution)/shard_map/finish/pallas_call | solution.py:639
  88.9 2.6 %collective-permute-done.23.rest_2_ = bf16[192,256]{1,0:T(8,128)(2,1)S(1)} collective-permute-done((bf16[192,256]{1,0:T(8,128)(2,1)}, bf16[192,256]{1,0:T(8,128)(2,1)S(1)}, u32[]{:S(2)}, u32[]{:S(2)}) %collective-permute-start.23) | collective-permute-done | bytes 98336 | tf_op jit(solution)/shard_map/ppermute | solution.py:750
  91.6 2.0 %join_out.1 = (f32[1024,128]{1,0:T(8,128)}, f32[32,256]{1,0:T(8,128)}, f32[32,256]{1,0:T(8,128)}) custom-call(s32[1]{0:T(128)} %bitcast.3.me_ref, bf16[192,256]{1,0:T(8,128)(2,1)} %join_send.1.rest_0_, bf16[192,256]{1,0:T(8,128)(2,1)S(1)} %collective-permute-done.22.rest_1_, bf16[192,256]{1,0:T(8,128)(2,1)S(1)} %collective-permute-done.23.rest_2_, ...), custom_call_target="tpu_custom_call" | custom-call | bytes 1024 | tf_op jit(solution)/shard_map/join_out/pallas_call | solution.py:53
  (43 shorter events, 5.5 us)
Async XLA Ops:
  0.6 8.2 %collective-permute-start = (s32[64,96]{1,0:T(8,128)}, s32[64,96]{1,0:T(8,128)S(1)}, u32[]{:S(2)}, u32[]{:S(2)}) collective-permute-start(s32[64,96]{1,0:T(8,128)} %bitcast.13), channel_id=1, source_target_pairs={{1,4},{2,8},{3,12},{6,9},{7,13},{4,1},{11,14},{8,2},{9,6},{12,3},{... | collective-permute-start | bytes 73736 | tf_op jit(solution)/shard_map/ppermute | solution.py:779
  8.8 20.7 %collective-permute-start.2 = (bf16[96,2048]{1,0:T(8,128)(2,1)}, bf16[96,2048]{1,0:T(8,128)(2,1)S(1)}, u32[]{:S(2)}, u32[]{:S(2)}) collective-permute-start(bf16[96,2048]{1,0:T(8,128)(2,1)} %get-tuple-element.56.rest_0_), channel_id=1, source_target_pairs={{0,12},{5,9},{10,6},{15,3},{16,28},{21,25},{26,22},{31,19}} | collective-permute-start | bytes 1179656 | tf_op jit(solution)/shard_map/ppermute | solution.py:791
  18.2 11.3 %collective-permute-start.1 = (bf16[96,2048]{1,0:T(8,128)(2,1)}, bf16[96,2048]{1,0:T(8,128)(2,1)S(1)}, u32[]{:S(2)}, u32[]{:S(2)}) collective-permute-start(bf16[96,2048]{1,0:T(8,128)(2,1)} %get-tuple-element.56.rest_0_), channel_id=1, source_target_pairs={{0,8},{5,13},{10,2},{15,7},{1,4},{4,1},{11,14},{14,11},{16,24},{21... | collective-permute-start | bytes 1179656 | tf_op jit(solution)/shard_map/ppermute | solution.py:791
  28.0 9.6 %collective-permute-start.6 = (bf16[24,2048]{1,0:T(8,128)(2,1)}, bf16[24,2048]{1,0:T(8,128)(2,1)S(1)}, u32[]{:S(2)}, u32[]{:S(2)}) collective-permute-start(bf16[24,2048]{1,0:T(8,128)(2,1)} %get-tuple-element.74), channel_id=1, source_target_pairs={{0,0},{1,4},{2,8},{3,12},{4,1},{5,5},{6,9},{7,13},{8,2},{9,6},{10,... | collective-permute-start | bytes 294920 | tf_op jit(solution)/shard_map/ppermute | solution.py:824
  29.5 10.1 %collective-permute-start.7 = (bf16[24,2048]{1,0:T(8,128)(2,1)}, bf16[24,2048]{1,0:T(8,128)(2,1)S(1)}, u32[]{:S(2)}, u32[]{:S(2)}) collective-permute-start(bf16[24,2048]{1,0:T(8,128)(2,1)} %get-tuple-element.75), channel_id=1, source_target_pairs={{0,1},{1,5},{2,9},{3,13},{4,2},{5,6},{6,10},{7,14},{8,3},{9,7},{10... | collective-permute-start | bytes 294920 | tf_op jit(solution)/shard_map/ppermute | solution.py:824
  33.7 16.6 %collective-permute-start.3 = (bf16[24,2048]{1,0:T(8,128)(2,1)}, bf16[24,2048]{1,0:T(8,128)(2,1)S(1)}, u32[]{:S(2)}, u32[]{:S(2)}) collective-permute-start(bf16[24,2048]{1,0:T(8,128)(2,1)} %get-tuple-element.58), channel_id=1, source_target_pairs={{0,1},{1,2},{2,3},{3,0},{4,5},{5,6},{6,7},{7,4},{8,9},{9,10},{10,1... | collective-permute-start | bytes 294920 | tf_op jit(solution)/shard_map/ppermute | solution.py:750
  33.7 16.7 %collective-permute-start.4 = (bf16[24,2048]{1,0:T(8,128)(2,1)}, bf16[24,2048]{1,0:T(8,128)(2,1)S(1)}, u32[]{:S(2)}, u32[]{:S(2)}) collective-permute-start(bf16[24,2048]{1,0:T(8,128)(2,1)} %get-tuple-element.59), channel_id=1, source_target_pairs={{0,2},{1,3},{2,0},{3,1},{4,6},{5,7},{6,4},{7,5},{8,10},{9,11},{10,... | collective-permute-start | bytes 294920 | tf_op jit(solution)/shard_map/ppermute | solution.py:750
  36.7 17.3 %collective-permute-start.5 = (bf16[24,2048]{1,0:T(8,128)(2,1)}, bf16[24,2048]{1,0:T(8,128)(2,1)S(1)}, u32[]{:S(2)}, u32[]{:S(2)}) collective-permute-start(bf16[24,2048]{1,0:T(8,128)(2,1)} %get-tuple-element.60), channel_id=1, source_target_pairs={{0,3},{1,0},{2,1},{3,2},{4,7},{5,4},{6,5},{7,6},{8,11},{9,8},{10,9... | collective-permute-start | bytes 294920 | tf_op jit(solution)/shard_map/ppermute | solution.py:750
  37.6 16.5 %collective-permute-start.8 = (bf16[24,2048]{1,0:T(8,128)(2,1)S(1)}, bf16[24,2048]{1,0:T(8,128)(2,1)S(1)}, u32[]{:S(2)}, u32[]{:S(2)}) collective-permute-start(bf16[24,2048]{1,0:T(8,128)(2,1)S(1)} %copy-done.2), channel_id=1, source_target_pairs={{0,2},{1,6},{2,10},{3,14},{4,3},{5,7},{6,11},{7,15},{8,0},{9,4},{1... | collective-permute-start | bytes 294920 | tf_op jit(solution)/shard_map/ppermute | solution.py:824
  39.6 14.5 %collective-permute-start.9 = (bf16[24,2048]{1,0:T(8,128)(2,1)S(1)}, bf16[24,2048]{1,0:T(8,128)(2,1)S(1)}, u32[]{:S(2)}, u32[]{:S(2)}) collective-permute-start(bf16[24,2048]{1,0:T(8,128)(2,1)S(1)} %copy-done.1), channel_id=1, source_target_pairs={{0,3},{1,7},{2,11},{3,15},{4,0},{5,4},{6,8},{7,12},{8,1},{9,5},{10... | collective-permute-start | bytes 294920 | tf_op jit(solution)/shard_map/ppermute | solution.py:824
  50.3 7.9 %collective-permute-start.11 = (bf16[128,256]{1,0:T(8,128)(2,1)}, bf16[128,256]{1,0:T(8,128)(2,1)S(1)}, u32[]{:S(2)}, u32[]{:S(2)}) collective-permute-start(bf16[128,256]{1,0:T(8,128)(2,1)} %get-tuple-element.79), channel_id=1, source_target_pairs={{0,4},{4,8},{8,12},{12,0},{1,5},{5,9},{9,13},{13,1},{2,6},{6,10},{... | collective-permute-start | bytes 196616 | tf_op jit(solution)/shard_map/ppermute | solution.py:750
  50.4 7.9 %collective-permute-start.12 = (bf16[128,256]{1,0:T(8,128)(2,1)}, bf16[128,256]{1,0:T(8,128)(2,1)S(1)}, u32[]{:S(2)}, u32[]{:S(2)}) collective-permute-start(bf16[128,256]{1,0:T(8,128)(2,1)} %get-tuple-element.80), channel_id=1, source_target_pairs={{0,8},{4,12},{8,0},{12,4},{1,9},{5,13},{9,1},{13,5},{2,10},{6,14},... | collective-permute-start | bytes 196616 | tf_op jit(solution)/shard_map/ppermute | solution.py:750
  57.4 13.6 %collective-permute-start.20 = (bf16[896,128]{1,0:T(8,128)(2,1)S(1)}, bf16[896,128]{1,0:T(8,128)(2,1)S(1)}, u32[]{:S(2)}, u32[]{:S(2)}) collective-permute-start(bf16[896,128]{1,0:T(8,128)(2,1)S(1)} %tokens.1.rest_0_.rest_4_), channel_id=1, source_target_pairs={{0,2},{1,3},{2,0},{3,1},{4,6},{5,7},{6,4},{7,5},{8,10},{9,11},{10,... | collective-permute-start | bytes 688136 | tf_op jit(solution)/shard_map/ppermute | solution.py:759
  59.2 11.8 %collective-permute-start.14 = (f32[32,256]{1,0:T(8,128)S(1)}, f32[32,256]{1,0:T(8,128)S(1)}, u32[]{:S(2)}, u32[]{:S(2)}) collective-permute-start(f32[32,256]{1,0:T(8,128)S(1)} %get-tuple-element.83), channel_id=1, source_target_pairs={{0,1},{1,2},{2,3},{3,0},{4,5},{5,6},{6,7},{7,4},{8,9},{9,10},{10,1... | collective-permute-start | bytes 98312 | tf_op jit(solution)/shard_map/ppermute | solution.py:750
  59.3 12.4 %collective-permute-start.15 = (f32[32,256]{1,0:T(8,128)S(1)}, f32[32,256]{1,0:T(8,128)S(1)}, u32[]{:S(2)}, u32[]{:S(2)}) collective-permute-start(f32[32,256]{1,0:T(8,128)S(1)} %get-tuple-element.84), channel_id=1, source_target_pairs={{0,2},{1,3},{2,0},{3,1},{4,6},{5,7},{6,4},{7,5},{8,10},{9,11},{10,... | collective-permute-start | bytes 98312 | tf_op jit(solution)/shard_map/ppermute | solution.py:750
  61.5 10.2 %collective-permute-start.16 = (f32[32,256]{1,0:T(8,128)S(1)}, f32[32,256]{1,0:T(8,128)S(1)}, u32[]{:S(2)}, u32[]{:S(2)}) collective-permute-start(f32[32,256]{1,0:T(8,128)S(1)} %get-tuple-element.85), channel_id=1, source_target_pairs={{0,3},{1,0},{2,1},{3,2},{4,7},{5,4},{6,5},{7,6},{8,11},{9,8},{10,9... | collective-permute-start | bytes 98312 | tf_op jit(solution)/shard_map/ppermute | solution.py:750
  64.4 12.3 %collective-permute-start.10 = (bf16[896,128]{1,0:T(8,128)(2,1)S(1)}, bf16[896,128]{1,0:T(8,128)(2,1)S(1)}, u32[]{:S(2)}, u32[]{:S(2)}) collective-permute-start(bf16[896,128]{1,0:T(8,128)(2,1)S(1)} %tokens.1.rest_0_.rest_4_), channel_id=1, source_target_pairs={{0,1},{1,0},{2,3},{3,2},{4,5},{5,4},{6,7},{7,6},{8,9},{9,8},{10,11... | collective-permute-start | bytes 688136 | tf_op jit(solution)/shard_map/ppermute | solution.py:759
  71.0 12.4 %collective-permute-start.21 = (bf16[896,128]{1,0:T(8,128)(2,1)S(1)}, bf16[896,128]{1,0:T(8,128)(2,1)S(1)}, u32[]{:S(2)}, u32[]{:S(2)}) collective-permute-start(bf16[896,128]{1,0:T(8,128)(2,1)S(1)} %collective-permute-done.20.rest_6_.rest_2_), channel_id=1, source_target_pairs={{0,1},{1,0},{2,3},{3,2},{4,5},{5,4},{6,7},{7,6},{8,9},{9,8},{10,11... | collective-permute-start | bytes 688136 | tf_op jit(solution)/shard_map/ppermute | solution.py:759
  71.7 11.7 %collective-permute-start.19 = (f32[32,256]{1,0:T(8,128)S(1)}, f32[32,256]{1,0:T(8,128)S(1)}, u32[]{:S(2)}, u32[]{:S(2)}) collective-permute-start(f32[32,256]{1,0:T(8,128)S(1)} %add_add_fusion.rest_0_), channel_id=1, source_target_pairs={{0,3},{1,0},{2,1},{3,2},{4,7},{5,4},{6,5},{7,6},{8,11},{9,8},{10,9... | collective-permute-start | bytes 98312 | tf_op jit(solution)/shard_map/ppermute | solution.py:750
  74.0 9.4 %collective-permute-start.18 = (f32[32,256]{1,0:T(8,128)S(1)}, f32[32,256]{1,0:T(8,128)S(1)}, u32[]{:S(2)}, u32[]{:S(2)}) collective-permute-start(f32[32,256]{1,0:T(8,128)S(1)} %add_add_fusion.rest_0_), channel_id=1, source_target_pairs={{0,2},{1,3},{2,0},{3,1},{4,6},{5,7},{6,4},{7,5},{8,10},{9,11},{10,... | collective-permute-start | bytes 98312 | tf_op jit(solution)/shard_map/ppermute | solution.py:750
  74.6 8.8 %collective-permute-start.17 = (f32[32,256]{1,0:T(8,128)S(1)}, f32[32,256]{1,0:T(8,128)S(1)}, u32[]{:S(2)}, u32[]{:S(2)}) collective-permute-start(f32[32,256]{1,0:T(8,128)S(1)} %add_add_fusion.rest_0_), channel_id=1, source_target_pairs={{0,1},{1,2},{2,3},{3,0},{4,5},{5,6},{6,7},{7,4},{8,9},{9,10},{10,1... | collective-permute-start | bytes 98312 | tf_op jit(solution)/shard_map/ppermute | solution.py:750
  84.1 4.8 %collective-permute-start.24 = (bf16[192,256]{1,0:T(8,128)(2,1)}, bf16[192,256]{1,0:T(8,128)(2,1)S(1)}, u32[]{:S(2)}, u32[]{:S(2)}) collective-permute-start(bf16[192,256]{1,0:T(8,128)(2,1)} %join_send.1.rest_0_), channel_id=1, source_target_pairs={{0,12},{4,0},{8,4},{12,8},{1,13},{5,1},{9,5},{13,9},{2,14},{6,2},{... | collective-permute-start | bytes 294920 | tf_op jit(solution)/shard_map/ppermute | solution.py:750
  84.1 7.4 %collective-permute-start.23 = (bf16[192,256]{1,0:T(8,128)(2,1)}, bf16[192,256]{1,0:T(8,128)(2,1)S(1)}, u32[]{:S(2)}, u32[]{:S(2)}) collective-permute-start(bf16[192,256]{1,0:T(8,128)(2,1)} %join_send.1.rest_0_), channel_id=1, source_target_pairs={{0,8},{4,12},{8,0},{12,4},{1,9},{5,13},{9,1},{13,5},{2,10},{6,14},... | collective-permute-start | bytes 294920 | tf_op jit(solution)/shard_map/ppermute | solution.py:750
  85.6 6.0 %collective-permute-start.22 = (bf16[192,256]{1,0:T(8,128)(2,1)}, bf16[192,256]{1,0:T(8,128)(2,1)S(1)}, u32[]{:S(2)}, u32[]{:S(2)}) collective-permute-start(bf16[192,256]{1,0:T(8,128)(2,1)} %join_send.1.rest_0_), channel_id=1, source_target_pairs={{0,4},{4,8},{8,12},{12,0},{1,5},{5,9},{9,13},{13,1},{2,6},{6,10},{... | collective-permute-start | bytes 294920 | tf_op jit(solution)/shard_map/ppermute | solution.py:750
  (4 other events, 32.3 us)
